TPU v7x, 32 devices: a whole 2x2x4 slice. The times are simulated.
32 devices in a mesh: seq: 8 (over z, y), row: 4 (over x, core).
Axes of the slice: x: 2, y: 2, z: 4, core: 2. Of those that a mesh axis runs over, the one named last changes fastest.
Arguments:
- block_input: bfloat16 [4, 1024, 2048], P('row', 'seq'), may hold values from -6 to 6
- memory: bfloat16 [4, 1024, 2048], P('row', 'seq'), may hold values from -6 to 6
- key_cache: bfloat16 [4, 1024, 2048], P('row', 'seq'), may hold values from -12 to 12
- value_cache: bfloat16 [4, 1024, 2048], P('row', 'seq'), may hold values from -6 to 6
- doc_lengths: int32 [4, 8], replicated, may hold values from 1 to 1024, as said below
- gmu_gate: bfloat16 [2048, 2048], P('seq', 'row'), may hold values from -0.125 to 0.125
- gmu_out: bfloat16 [2048, 2048], P('row', 'seq'), may hold values from -0.125 to 0.125
- ffn1_gate: bfloat16 [2048, 8192], P('seq', 'row'), may hold values from -0.125 to 0.125
- ffn1_up: bfloat16 [2048, 8192], P('seq', 'row'), may hold values from -0.125 to 0.125
- ffn1_down: bfloat16 [8192, 2048], P('row', 'seq'), may hold values from -0.0625 to 0.0625
- query_weight: bfloat16 [2048, 2048], P('seq', 'row'), may hold values from -0.125 to 0.125
- attn_out: bfloat16 [2048, 2048], P('row', 'seq'), may hold values from -0.5 to 0.5
- ffn2_gate: bfloat16 [2048, 8192], P('seq', 'row'), may hold values from -0.125 to 0.125
- ffn2_up: bfloat16 [2048, 8192], P('seq', 'row'), may hold values from -0.125 to 0.125
- ffn2_down: bfloat16 [8192, 2048], P('row', 'seq'), may hold values from -0.0625 to 0.0625
- gain_a: float32 [2048], replicated, may hold values from 0.5 to 1.5
- gain_b: float32 [2048], replicated, may hold values from 0.5 to 1.5
- gain_c: float32 [2048], replicated, may hold values from 0.5 to 1.5
- gain_d: float32 [2048], replicated, may hold values from 0.5 to 1.5
- cotangent: bfloat16 [4, 1024, 2048], P('row', 'seq'), may hold values from -6 to 6
Outputs:
- mixed: float32 [4, 1024, 2048], P('row', 'seq')
- input_grad: float32 [4, 1024, 2048], P('row', 'seq')
- memory_grad: float32 [4, 1024, 2048], P('row', 'seq')
- key_grad: float32 [4, 1024, 2048], P('row', 'seq')
- value_grad: float32 [4, 1024, 2048], P('row', 'seq')
- gmu_gate_grad: float32 [2048, 2048], P('seq', 'row')
- gmu_out_grad: float32 [2048, 2048], P('row', 'seq')
- ffn1_gate_grad: float32 [2048, 8192], P('seq', 'row')
- ffn1_up_grad: float32 [2048, 8192], P('seq', 'row')
- ffn1_down_grad: float32 [8192, 2048], P('row', 'seq')
- query_weight_grad: float32 [2048, 2048], P('seq', 'row')
- attn_out_grad: float32 [2048, 2048], P('row', 'seq')
- ffn2_gate_grad: float32 [2048, 8192], P('seq', 'row')
- ffn2_up_grad: float32 [2048, 8192], P('seq', 'row')
- ffn2_down_grad: float32 [8192, 2048], P('row', 'seq')
- gain_a_grad: float32 [2048], replicated
- gain_b_grad: float32 [2048], replicated
- gain_c_grad: float32 [2048], replicated
- gain_d_grad: float32 [2048], replicated
Inputs may be any that keep to these rules, and one draw needn't show every extreme that they name: `doc_lengths`: each row's 8 lengths sum to 1024.
All inputs are finite; a program needn't handle non-finite values.
Results may differ from a plain program's by a relative error of at most 0.04.
Values may be sent and summed in bfloat16 or wider, within the bound.
A program may use at most 256 MiB of HBM per device.

v0:
```python
import jax
import jax.numpy as jnp
from jax import lax
from jax.sharding import PartitionSpec as P

HEAD_DIM = 128


EPSILON = 1e-05
MASKED = -1e30


def passed_along(value, axis, steps):
    count = lax.axis_size(axis)
    first, last = (max(0, -steps), min(count, count - steps))
    return lax.ppermute(value, axis, [(source, source + steps) for source in range(first, last)])


def shifted(value, axis, steps):
    count = lax.axis_size(axis)
    pairs = [(source, (source + steps) % count) for source in range(count)]
    return lax.ppermute(value, axis, pairs)


def silu_slope(values):
    sigmoid = jax.nn.sigmoid(values)
    return sigmoid * (1.0 + values * (1.0 - sigmoid))


def rms_forward(values, gain_vec):
    inverse = lax.rsqrt(jnp.mean(values * values, axis=-1, keepdims=True) + EPSILON)
    return (values * inverse * gain_vec, inverse)


def rms_backward(values, inverse, gain_vec, grad_normed):
    scaled = grad_normed * gain_vec
    gain_grad = jnp.sum(grad_normed * values * inverse, axis=0)
    inner_sum = jnp.mean(scaled * values, axis=-1, keepdims=True)
    return (inverse * scaled - values * inverse * inverse * inverse * inner_sum, gain_grad)


def doc_numbers(doc_lengths, positions):
    doc_ends = jnp.cumsum(doc_lengths, axis=1, dtype=jnp.int32)
    return jnp.sum((positions[None, :, None] >= doc_ends[:, None, :]).astype(jnp.int32), axis=-1)


def dot_plain(left, right):
    return jnp.dot(left, right, preferred_element_type=jnp.float32)


def dot_left_t(left, right):
    return lax.dot_general(
        left, right, (((0,), (0,)), ((), ())), preferred_element_type=jnp.float32
    )


def dot_right_t(left, right):
    return lax.dot_general(
        left, right, (((1,), (1,)), ((), ())), preferred_element_type=jnp.float32
    )


def ffn_forward(rows_in, gate_weight, up_weight, down_weight):
    gate_val = dot_plain(rows_in, gate_weight)
    up_val = dot_plain(rows_in, up_weight)
    hidden = (jax.nn.silu(gate_val) * up_val).astype(jnp.bfloat16)
    return (dot_plain(hidden, down_weight), gate_val, up_val, hidden)


def ffn_backward(cot_rows, rows_in, gate_val, up_val, hidden, gate_weight, up_weight, down_weight):
    dhid = dot_right_t(cot_rows, down_weight)
    down_grad = dot_left_t(hidden, cot_rows)
    dgate = (dhid * up_val * silu_slope(gate_val)).astype(jnp.bfloat16)
    dup = (dhid * jax.nn.silu(gate_val)).astype(jnp.bfloat16)
    gate_grad = dot_left_t(rows_in, dgate)
    up_grad = dot_left_t(rows_in, dup)
    drows = dot_right_t(dgate, gate_weight) + dot_right_t(dup, up_weight)
    return (drows, gate_grad, up_grad, down_grad)


def body(
    block_input,
    memory,
    key_cache,
    value_cache,
    doc_lengths,
    gmu_gate,
    gmu_out,
    ffn1_gate,
    ffn1_up,
    ffn1_down,
    query_weight,
    attn_out,
    ffn2_gate,
    ffn2_up,
    ffn2_down,
    gain_a,
    gain_b,
    gain_c,
    gain_d,
    cotangent,
):
    seq_count = lax.axis_size("seq")
    row_count = lax.axis_size("row")
    seq_index = lax.axis_index("seq")
    tok_len = block_input.shape[1]
    width = block_input.shape[2]
    head_count = query_weight.shape[1] // HEAD_DIM
    score_scale = HEAD_DIM ** (-0.5)
    local_pos = jnp.arange(tok_len, dtype=jnp.int32)

    def gather_weights():
        inner_w = (
            lax.all_gather(gmu_gate, "seq", axis=0, tiled=True),
            lax.all_gather(query_weight, "seq", axis=0, tiled=True),
            lax.all_gather(ffn1_gate, "seq", axis=0, tiled=True),
            lax.all_gather(ffn1_up, "seq", axis=0, tiled=True),
            lax.all_gather(ffn2_gate, "seq", axis=0, tiled=True),
            lax.all_gather(ffn2_up, "seq", axis=0, tiled=True),
        )
        outer_w = (
            lax.all_gather(gmu_out, "seq", axis=1, tiled=True),
            lax.all_gather(attn_out, "seq", axis=1, tiled=True),
            lax.all_gather(ffn1_down, "seq", axis=1, tiled=True),
            lax.all_gather(ffn2_down, "seq", axis=1, tiled=True),
        )
        return (inner_w, outer_w)

    def spread(normed):
        return lax.all_gather(normed[None], "row", axis=0, tiled=True).reshape(
            row_count * tok_len, width
        )

    def collect(partial_value):
        return lax.psum_scatter(
            partial_value.reshape(row_count, tok_len, width).astype(jnp.bfloat16),
            "row",
            scatter_dimension=0,
            tiled=True,
        ).astype(jnp.float32)[0]

    def spread_grad(grad_res):
        return lax.all_gather(
            grad_res.astype(jnp.bfloat16)[None], "row", axis=0, tiled=True
        ).reshape(row_count * tok_len, width)

    def collect_grad(partial_value):
        return lax.psum_scatter(
            partial_value.reshape(row_count, tok_len, width).astype(jnp.bfloat16),
            "row",
            scatter_dimension=0,
            tiled=True,
        ).astype(jnp.float32)[0]

    def allowed_between(query_source, key_source):
        q_positions = query_source * tok_len + local_pos
        key_pos = key_source * tok_len + local_pos
        q_docs = doc_numbers(doc_lengths, q_positions)
        key_docs = doc_numbers(doc_lengths, key_pos)
        causal = key_pos[None, :] <= q_positions[:, None]
        same_doc = q_docs[:, :, None] == key_docs[:, None, :]
        return (causal[None] & same_doc)[:, :, None, :]

    def allowed_pairs(source):
        return allowed_between(seq_index, source)

    inner_w, outer_w = gather_weights()
    gate_full, query_full, gate_one_w, up_one_w, gate_two_w, up_two_w = inner_w
    gout_full, aout_full, down_one_w, down_two_w = outer_w
    pieces = (
        lax.all_to_all(memory, "row", split_axis=2, concat_axis=0, tiled=True),
        lax.all_to_all(key_cache, "row", split_axis=2, concat_axis=0, tiled=True),
        lax.all_to_all(value_cache, "row", split_axis=2, concat_axis=0, tiled=True),
    )
    mem_cols = pieces[0].reshape(row_count * tok_len, -1).astype(jnp.float32)
    kv_here = jnp.stack(
        [
            pieces[1].reshape(row_count, tok_len, head_count, HEAD_DIM),
            pieces[2].reshape(row_count, tok_len, head_count, HEAD_DIM),
        ]
    )
    x_zero = block_input[0].astype(jnp.float32)
    normed_a, inv_a = rms_forward(x_zero, gain_a)
    rows_a = spread(normed_a.astype(jnp.bfloat16))
    gmu_pre = dot_plain(rows_a, gate_full)
    gmu_act = (mem_cols * jax.nn.silu(gmu_pre)).astype(jnp.bfloat16)
    x_one = x_zero + collect(dot_plain(gmu_act, gout_full))
    normed_b, inv_b = rms_forward(x_one, gain_b)
    rows_b = spread(normed_b.astype(jnp.bfloat16))
    part_one, gate_one, up_one, hidden_one = ffn_forward(rows_b, gate_one_w, up_one_w, down_one_w)
    x_two = x_one + collect(part_one)
    normed_c, inv_c = rms_forward(x_two, gain_c)
    rows_c = spread(normed_c.astype(jnp.bfloat16))
    queries = (
        dot_plain(rows_c, query_full)
        .astype(jnp.bfloat16)
        .reshape(row_count, tok_len, head_count, HEAD_DIM)
    )

    def absorb(softmax_state, kv_block, source):
        run_max, totals, accum = softmax_state
        scores = jnp.einsum(
            "rihd,rjhd->rihj", queries, kv_block[0], preferred_element_type=jnp.float32
        )
        allowed = allowed_pairs(source)
        scores = jnp.where(allowed, scores * score_scale, MASKED)
        new_max = jnp.maximum(run_max, jnp.max(scores, axis=-1, keepdims=True))
        weights = jnp.where(allowed, jnp.exp(scores - new_max), 0.0)
        shrink = jnp.exp(run_max - new_max)
        totals = totals * shrink + jnp.sum(weights, axis=-1, keepdims=True)
        accum = accum * shrink + jnp.einsum(
            "rihj,rjhd->rihd",
            weights.astype(jnp.bfloat16),
            kv_block[1],
            preferred_element_type=jnp.float32,
        )
        return (new_max, totals, accum)

    stat_shape = (row_count, tok_len, head_count, 1)
    start_state = (
        jnp.full(stat_shape, MASKED, jnp.float32),
        jnp.zeros(stat_shape, jnp.float32),
        jnp.zeros((row_count, tok_len, head_count, HEAD_DIM), jnp.float32),
    )
    first_state = absorb(start_state, kv_here, seq_index)

    def cycle_forward(section_num, carry):
        softmax_state, kv_block = carry
        kv_block = passed_along(kv_block, "seq", 1)
        source = (seq_index - section_num) % seq_count
        return (absorb(softmax_state, kv_block, source), kv_block)

    final_state, _ = lax.fori_loop(1, seq_count, cycle_forward, (first_state, kv_here))
    run_max, totals, accum = final_state
    outputs = accum / totals
    log_sums = run_max + jnp.log(totals)
    attended = outputs.astype(jnp.bfloat16).reshape(row_count * tok_len, head_count * HEAD_DIM)
    x_three = x_two + collect(dot_plain(attended, aout_full))
    normed_d, inv_d = rms_forward(x_three, gain_d)
    rows_d = spread(normed_d.astype(jnp.bfloat16))
    part_two, gate_two, up_two, hidden_two = ffn_forward(rows_d, gate_two_w, up_two_w, down_two_w)
    mixed = x_three + collect(part_two)
    inner_w, outer_w = gather_weights()
    gate_full, query_full, gate_one_w, up_one_w, gate_two_w, up_two_w = inner_w
    gout_full, aout_full, down_one_w, down_two_w = outer_w
    grad_y = cotangent[0].astype(jnp.float32)
    drows_d, gate_two_grad, up_two_grad, down_two_grad = ffn_backward(
        spread_grad(grad_y), rows_d, gate_two, up_two, hidden_two, gate_two_w, up_two_w, down_two_w
    )
    dx_d, gain_d_grad = rms_backward(x_three, inv_d, gain_d, collect_grad(drows_d))
    grad_three = grad_y + dx_d
    cot_three = spread_grad(grad_three)
    dattended = dot_right_t(cot_three, aout_full)
    aout_grad = dot_left_t(attended, cot_three)
    dout = dattended.astype(jnp.bfloat16).reshape(row_count, tok_len, head_count, HEAD_DIM)
    row_delta = jnp.sum(dout.astype(jnp.float32) * outputs, axis=-1, keepdims=True)
    head_shape = (row_count, tok_len, head_count, HEAD_DIM)

    def cycle_backward(section_num, carry):
        query_acc, kv_block, grad_block = carry
        source = (seq_index - section_num) % seq_count
        scores = jnp.einsum(
            "rihd,rjhd->rihj", queries, kv_block[0], preferred_element_type=jnp.float32
        )
        allowed = allowed_pairs(source)
        probs = jnp.where(allowed, jnp.exp(scores * score_scale - log_sums), 0.0)
        dprob = jnp.einsum("rihd,rjhd->rihj", dout, kv_block[1], preferred_element_type=jnp.float32)
        dscores = (probs * (dprob - row_delta)).astype(jnp.bfloat16)
        query_acc = (
            query_acc
            + jnp.einsum(
                "rihj,rjhd->rihd", dscores, kv_block[0], preferred_element_type=jnp.float32
            )
            * score_scale
        )
        key_part = (
            jnp.einsum("rihj,rihd->rjhd", dscores, queries, preferred_element_type=jnp.float32)
            * score_scale
        )
        value_part = jnp.einsum(
            "rihj,rihd->rjhd", probs.astype(jnp.bfloat16), dout, preferred_element_type=jnp.float32
        )
        grad_block = grad_block + jnp.stack([key_part, value_part])
        kv_block = passed_along(kv_block, "seq", 1)
        grad_block = shifted(grad_block.astype(jnp.bfloat16), "seq", 1).astype(grad_block.dtype)
        return (query_acc, kv_block, grad_block)

    query_acc, _, grad_block = lax.fori_loop(
        0,
        seq_count,
        cycle_backward,
        (jnp.zeros(head_shape, jnp.float32), kv_here, jnp.zeros((2,) + head_shape, jnp.float32)),
    )
    dqueries = query_acc.astype(jnp.bfloat16).reshape(row_count * tok_len, head_count * HEAD_DIM)
    query_grad = dot_left_t(rows_c, dqueries)
    dx_c, gain_c_grad = rms_backward(
        x_two, inv_c, gain_c, collect_grad(dot_right_t(dqueries, query_full))
    )
    grad_two = grad_three + dx_c
    drows_b, gate_one_grad, up_one_grad, down_one_grad = ffn_backward(
        spread_grad(grad_two),
        rows_b,
        gate_one,
        up_one,
        hidden_one,
        gate_one_w,
        up_one_w,
        down_one_w,
    )
    dx_b, gain_b_grad = rms_backward(x_one, inv_b, gain_b, collect_grad(drows_b))
    grad_one = grad_two + dx_b
    cot_one = spread_grad(grad_one)
    dact = dot_right_t(cot_one, gout_full)
    gout_grad = dot_left_t(gmu_act, cot_one)
    mem_grad_cols = dact * jax.nn.silu(gmu_pre)
    dpre = (dact * mem_cols * silu_slope(gmu_pre)).astype(jnp.bfloat16)
    gate_a_grad = dot_left_t(rows_a, dpre)
    dx_a, gain_a_grad = rms_backward(
        x_zero, inv_a, gain_a, collect_grad(dot_right_t(dpre, gate_full))
    )
    input_grad = grad_one + dx_a
    home = (
        lax.all_to_all(
            mem_grad_cols.reshape(row_count, tok_len, -1).astype(jnp.bfloat16),
            "row",
            split_axis=0,
            concat_axis=2,
            tiled=True,
        ).astype(jnp.float32),
        lax.all_to_all(
            grad_block[0].reshape(row_count, tok_len, -1).astype(jnp.bfloat16),
            "row",
            split_axis=0,
            concat_axis=2,
            tiled=True,
        ).astype(jnp.float32),
        lax.all_to_all(
            grad_block[1].reshape(row_count, tok_len, -1).astype(jnp.bfloat16),
            "row",
            split_axis=0,
            concat_axis=2,
            tiled=True,
        ).astype(jnp.float32),
    )
    grads_rows = (
        lax.psum_scatter(
            gate_a_grad.astype(jnp.bfloat16), "seq", scatter_dimension=0, tiled=True
        ).astype(jnp.float32),
        lax.psum_scatter(
            query_grad.astype(jnp.bfloat16), "seq", scatter_dimension=0, tiled=True
        ).astype(jnp.float32),
        lax.psum_scatter(
            gate_one_grad.astype(jnp.bfloat16), "seq", scatter_dimension=0, tiled=True
        ).astype(jnp.float32),
        lax.psum_scatter(
            up_one_grad.astype(jnp.bfloat16), "seq", scatter_dimension=0, tiled=True
        ).astype(jnp.float32),
        lax.psum_scatter(
            gate_two_grad.astype(jnp.bfloat16), "seq", scatter_dimension=0, tiled=True
        ).astype(jnp.float32),
        lax.psum_scatter(
            up_two_grad.astype(jnp.bfloat16), "seq", scatter_dimension=0, tiled=True
        ).astype(jnp.float32),
    )
    grads_cols = (
        lax.psum_scatter(
            gout_grad.astype(jnp.bfloat16), "seq", scatter_dimension=1, tiled=True
        ).astype(jnp.float32),
        lax.psum_scatter(
            aout_grad.astype(jnp.bfloat16), "seq", scatter_dimension=1, tiled=True
        ).astype(jnp.float32),
        lax.psum_scatter(
            down_one_grad.astype(jnp.bfloat16), "seq", scatter_dimension=1, tiled=True
        ).astype(jnp.float32),
        lax.psum_scatter(
            down_two_grad.astype(jnp.bfloat16), "seq", scatter_dimension=1, tiled=True
        ).astype(jnp.float32),
    )
    gain_grads = lax.psum((gain_a_grad, gain_b_grad, gain_c_grad, gain_d_grad), ("seq", "row"))
    return (
        mixed[None],
        input_grad[None],
        home[0],
        home[1],
        home[2],
        grads_rows[0],
        grads_cols[0],
        grads_rows[2],
        grads_rows[3],
        grads_cols[2],
        grads_rows[1],
        grads_cols[1],
        grads_rows[4],
        grads_rows[5],
        grads_cols[3],
        gain_grads[0],
        gain_grads[1],
        gain_grads[2],
        gain_grads[3],
    )


def solution(mesh):
    in_specs = (
        P("row", "seq", None),
        P("row", "seq", None),
        P("row", "seq", None),
        P("row", "seq", None),
        P(),
        P("seq", "row"),
        P("row", "seq"),
        P("seq", "row"),
        P("seq", "row"),
        P("row", "seq"),
        P("seq", "row"),
        P("row", "seq"),
        P("seq", "row"),
        P("seq", "row"),
        P("row", "seq"),
        P(),
        P(),
        P(),
        P(),
        P("row", "seq", None),
    )
    out_specs = (
        P("row", "seq", None),
        P("row", "seq", None),
        P("row", "seq", None),
        P("row", "seq", None),
        P("row", "seq", None),
        P("seq", "row"),
        P("row", "seq"),
        P("seq", "row"),
        P("seq", "row"),
        P("row", "seq"),
        P("seq", "row"),
        P("row", "seq"),
        P("seq", "row"),
        P("seq", "row"),
        P("row", "seq"),
        P(),
        P(),
        P(),
        P(),
    )
    return jax.shard_map(body, mesh=mesh, in_specs=in_specs, out_specs=out_specs, check_vma=False)
```

profile of v0, /device:TPU:1, one launch (start us, length us, event | category | flops | bytes accessed | tf_op | source)
XLA Modules:
  0.0 3324.4 jit_solution(2045333885818265055)
XLA Ops:
  41.6 46.4 %all-gather.21.cloned.1.call-done = bf16[2048,512]{1,0:T(8,128)(2,1)} async-done(((bf16[256,512]{1,0:T(8,128)(2,1)}), bf16[2048,512]{1,0:T(8,128)(2,1)}) %all-gather.21.cloned.1.call-update) | async-done | bytes 2097168 | tf_op jit(solution)/shard_map/all_gather | solution.py:114
  92.5 47.6 %all-gather.23.cloned.1.call-done = bf16[512,2048]{1,0:T(8,128)(2,1)} async-done(((bf16[512,256]{1,0:T(8,128)(2,1)}), bf16[512,2048]{1,0:T(8,128)(2,1)}) %all-gather.23.cloned.1.call-update) | async-done | bytes 2097168 | tf_op jit(solution)/shard_map/all_gather | solution.py:122
  144.4 30.3 reduce-scatter.19.cloned.1.call-done
  180.4 20.8 all-gather.25.cloned.1.call-done
  201.2 126.4 %all-gather.27.cloned.1.call-done = bf16[2048,2048]{1,0:T(8,128)(2,1)} async-done(((bf16[256,2048]{1,0:T(8,128)(2,1)}), bf16[2048,2048]{1,0:T(8,128)(2,1)}) %all-gather.27.cloned.1.call-update) | async-done | bytes 8388624 | tf_op jit(solution)/shard_map/all_gather | solution.py:116
  338.3 114.8 %all-gather.29.cloned.1.call-done = bf16[2048,2048]{1,0:T(8,128)(2,1)} async-done(((bf16[256,2048]{1,0:T(8,128)(2,1)}), bf16[2048,2048]{1,0:T(8,128)(2,1)}) %all-gather.29.cloned.1.call-update) | async-done | bytes 8388624 | tf_op jit(solution)/shard_map/all_gather | solution.py:117
  463.9 115.0 %all-gather.31.cloned.1.call-done = bf16[2048,2048]{1,0:T(8,128)(2,1)} async-done(((bf16[2048,256]{1,0:T(8,128)(2,1)}), bf16[2048,2048]{1,0:T(8,128)(2,1)}) %all-gather.31.cloned.1.call-update) | async-done | bytes 8388624 | tf_op jit(solution)/shard_map/all_gather | solution.py:124
  589.6 29.3 reduce-scatter.21.cloned.1.call-done
  677.8 16.2 all-gather.33.cloned.1.call-done
  700.0 214.0 %while.44 = (s32[]{:T(128)}, f32[4,128,4,1]{1,2,0,3:T(4,128)S(1)}, f32[4,128,4,1]{1,2,0,3:T(4,128)S(1)}, f32[4,128,4,128]{3,1,2,0:T(8,128)S(1)}, bf16[2,4,128,4,...) while((s32[]{:T(128)}, f32[4,128,4,1]{1,2,0,3:T(4,128)S(1)}, ...), condition=%wide.region_14.15_spmd.clone.clone, body=%wide.region_9.14_spmd.clone.clone.sunk | while | flops 137278736 | bytes 13544890 | solution.py:233
  703.6 25.3 collective-permute-done
  744.6 19.8 collective-permute-done
  780.1 20.9 collective-permute-done
  809.8 19.9 collective-permute-done
  838.6 19.0 collective-permute-done
  866.5 18.1 collective-permute-done
  893.4 17.1 collective-permute-done
  920.3 42.9 %reduce-scatter.23.cloned.1.call-done = bf16[1,128,2048]{2,1,0:T(8,128)(2,1)} async-done(((bf16[4,128,2048]{2,1,0:T(8,128)(2,1)}), bf16[1,128,2048]{2,1,0:T(8,128)(2,1)}) %reduce-scatter.23.cloned.1.call-update) | async-done | bytes 524304 | tf_op jit(solution)/shard_map/reduce_scatter | solution.py:135
  968.7 121.3 %all-gather.41.cloned.1.call-done = bf16[2048,2048]{1,0:T(8,128)(2,1)} async-done(((bf16[256,2048]{1,0:T(8,128)(2,1)}), bf16[2048,2048]{1,0:T(8,128)(2,1)}) %all-gather.41.cloned.1.call-update) | async-done | bytes 8388624 | tf_op jit(solution)/shard_map/all_gather | solution.py:118
  1090.0 23.7 all-gather.39.cloned.1.call-done
  1124.2 115.8 %all-gather.43.cloned.1.call-done = bf16[2048,2048]{1,0:T(8,128)(2,1)} async-done(((bf16[256,2048]{1,0:T(8,128)(2,1)}), bf16[2048,2048]{1,0:T(8,128)(2,1)}) %all-gather.43.cloned.1.call-update) | async-done | bytes 8388624 | tf_op jit(solution)/shard_map/all_gather | solution.py:119
  1263.1 126.7 %all-gather.45.cloned.1.call-done = bf16[2048,2048]{1,0:T(8,128)(2,1)} async-done(((bf16[2048,256]{1,0:T(8,128)(2,1)}), bf16[2048,2048]{1,0:T(8,128)(2,1)}) %all-gather.45.cloned.1.call-update) | async-done | bytes 8388624 | tf_op jit(solution)/shard_map/all_gather | solution.py:125
  1420.2 30.1 reduce-scatter.27.cloned.1.call-done
  1454.0 23.1 all-gather.49.cloned.1.call-done
  1484.9 400.9 %while.45 = (s32[]{:T(128)}, f32[4,128,4,128]{3,1,2,0:T(8,128)}, bf16[2,4,128,4,128]{4,2,3,1,0:T(8,128)(2,1)}, f32[2,4,128,4,128]{4,2,3,1,0:T(8,128)}, s32[]{:T(...) while((s32[]{:T(128)}, f32[4,128,4,128]{3,1,2,0:T(8,128)}, ...), condition=%wide.region_24.25_spmd.clone.clone, body=%wide.region_21.24_spmd.clone.clone.sunk | while | flops 341220608 | bytes 42135100 | solution.py:288
  1497.2 20.9 collective-permute-done.2
  1520.9 15.9 collective-permute-done.1
  1552.3 18.0 collective-permute-done.2
  1573.1 15.8 collective-permute-done.1
  1605.2 16.1 collective-permute-done.2
  1624.1 15.8 collective-permute-done.1
  1657.2 15.5 collective-permute-done.2
  1675.5 15.3 collective-permute-done.1
  1902.8 30.6 reduce-scatter.29.cloned.1.call-done
  1934.8 32.7 reduce-scatter.25.cloned.1.call-done
  1971.4 23.1 all-gather.51.cloned.1.call-done
  2024.4 31.1 reduce-scatter.31.cloned.1.call-done
  2184.5 38.2 %reduce-scatter.45.cloned.1.call-done = bf16[256,512]{1,0:T(8,128)(2,1)} async-done(((bf16[2048,512]{1,0:T(8,128)(2,1)}), bf16[256,512]{1,0:T(8,128)(2,1)}) %reduce-scatter.45.cloned.1.call-update) | async-done | bytes 262160 | tf_op jit(solution)/shard_map/reduce_scatter | solution.py:349
  2224.5 152.2 %reduce-scatter.49.cloned.1.call-done = bf16[256,2048]{1,0:T(8,128)(2,1)} async-done(((bf16[2048,2048]{1,0:T(8,128)(2,1)}), bf16[256,2048]{1,0:T(8,128)(2,1)}) %reduce-scatter.49.cloned.1.call-update) | async-done | bytes 1048592 | tf_op jit(solution)/shard_map/reduce_scatter | solution.py:358
  2379.5 148.9 %reduce-scatter.51.cloned.1.call-done = bf16[256,2048]{1,0:T(8,128)(2,1)} async-done(((bf16[2048,2048]{1,0:T(8,128)(2,1)}), bf16[256,2048]{1,0:T(8,128)(2,1)}) %reduce-scatter.51.cloned.1.call-update) | async-done | bytes 1048592 | tf_op jit(solution)/shard_map/reduce_scatter | solution.py:361
  2531.2 149.6 %reduce-scatter.53.cloned.1.call-done = bf16[2048,256]{1,0:T(8,128)(2,1)} async-done(((bf16[2048,2048]{1,0:T(8,128)(2,1)}), bf16[2048,256]{1,0:T(8,128)(2,1)}) %reduce-scatter.53.cloned.1.call-update) | async-done | bytes 1048592 | tf_op jit(solution)/shard_map/reduce_scatter | solution.py:375
  2684.8 65.5 %reduce-scatter.37.cloned.1.call-done = bf16[512,256]{1,0:T(8,128)(2,1)} async-done(((bf16[512,2048]{1,0:T(8,128)(2,1)}), bf16[512,256]{1,0:T(8,128)(2,1)}) %reduce-scatter.37.cloned.1.call-update) | async-done | bytes 262160 | tf_op jit(solution)/shard_map/reduce_scatter | solution.py:366
  2752.0 69.2 %reduce-scatter.35.cloned.1.call-done = bf16[256,512]{1,0:T(8,128)(2,1)} async-done(((bf16[2048,512]{1,0:T(8,128)(2,1)}), bf16[256,512]{1,0:T(8,128)(2,1)}) %reduce-scatter.35.cloned.1.call-update) | async-done | bytes 262160 | tf_op jit(solution)/shard_map/reduce_scatter | solution.py:346
  2823.0 33.4 %reduce-scatter.33.cloned.1.call-done = bf16[1,128,2048]{2,1,0:T(8,128)(2,1)} async-done(((bf16[4,128,2048]{2,1,0:T(8,128)(2,1)}), bf16[1,128,2048]{2,1,0:T(8,128)(2,1)}) %reduce-scatter.33.cloned.1.call-update) | async-done | bytes 524304 | tf_op jit(solution)/shard_map/reduce_scatter | solution.py:148
  2857.8 43.1 %all-reduce = (f32[2048]{0:T(1024)}, f32[2048]{0:T(1024)}, f32[2048]{0:T(1024)}, f32[2048]{0:T(1024)}) all-reduce(f32[2048]{0:T(1024)S(1)} %get-tuple-element.831, f32[2048]{0:T(1024)S(1)} %get-tuple-element.829, f32[2048]{0:T(1024)S(1)} %get-tuple-element.827, f32[2048]{0:T(1024)S(1)} %copy-done.34), channel_id=1, replica_groups=mesh['seq'=8,'row'=4] {'seq','row'}, use_global_device_ids=true, to_apply=%region_42.43 | all-reduce | flops 8192 | bytes 65536 | tf_op jit(solution)/shard_map/psum | solution.py:379
  2903.8 107.1 %reduce-scatter.43.cloned.1.call-done = bf16[2048,256]{1,0:T(8,128)(2,1)} async-done(((bf16[2048,2048]{1,0:T(8,128)(2,1)}), bf16[2048,256]{1,0:T(8,128)(2,1)}) %reduce-scatter.43.cloned.1.call-update) | async-done | bytes 1048592 | tf_op jit(solution)/shard_map/reduce_scatter | solution.py:372
  3013.6 149.0 %reduce-scatter.39.cloned.1.call-done = bf16[256,2048]{1,0:T(8,128)(2,1)} async-done(((bf16[2048,2048]{1,0:T(8,128)(2,1)}), bf16[256,2048]{1,0:T(8,128)(2,1)}) %reduce-scatter.39.cloned.1.call-update) | async-done | bytes 1048592 | tf_op jit(solution)/shard_map/reduce_scatter | solution.py:352
  3165.4 149.2 %reduce-scatter.41.cloned.1.call-done = bf16[256,2048]{1,0:T(8,128)(2,1)} async-done(((bf16[2048,2048]{1,0:T(8,128)(2,1)}), bf16[256,2048]{1,0:T(8,128)(2,1)}) %reduce-scatter.41.cloned.1.call-update) | async-done | bytes 1048592 | tf_op jit(solution)/shard_map/reduce_scatter | solution.py:355
  (558 shorter events, 781.2 us)
Async XLA Ops:
  7.2 34.4 %all-gather.19.cloned.1.call-start = ((), (), s32[]{:S(2)}) async-start(), calls=%async_computation.24 | async-start | bytes 2621440 | tf_op jit(solution)/shard_map/all_gather | solution.py:130
  10.6 77.4 %all-gather.21.cloned.1.call-start = ((), (), s32[]{:S(2)}) async-start(), calls=%async_computation.25 | async-start | bytes 2359296 | tf_op jit(solution)/shard_map/all_gather | solution.py:114
  11.3 128.8 %all-gather.23.cloned.1.call-start = ((), (), s32[]{:S(2)}) async-start(), calls=%async_computation.26 | async-start | bytes 2359296 | tf_op jit(solution)/shard_map/all_gather | solution.py:122
  12.1 162.6 %reduce-scatter.19.cloned.1.call-start = ((), (), s32[]{:S(2)}) async-start(), calls=%async_computation.27 | async-start | bytes 2621440 | tf_op jit(solution)/shard_map/reduce_scatter | solution.py:135
  144.4 56.9 %all-gather.25.cloned.1.call-start = ((), (), s32[]{:S(2)}) async-start(), calls=%async_computation.28 | async-start | bytes 2621440 | tf_op jit(solution)/shard_map/all_gather | solution.py:130
  178.1 149.5 %all-gather.27.cloned.1.call-start = ((), (), s32[]{:S(2)}) async-start(), calls=%async_computation.29 | async-start | bytes 9437184 | tf_op jit(solution)/shard_map/all_gather | solution.py:116
  178.7 274.4 %all-gather.29.cloned.1.call-start = ((), (), s32[]{:S(2)}) async-start(), calls=%async_computation.30 | async-start | bytes 9437184 | tf_op jit(solution)/shard_map/all_gather | solution.py:117
  179.4 399.5 %all-gather.31.cloned.1.call-start = ((), (), s32[]{:S(2)}) async-start(), calls=%async_computation.31 | async-start | bytes 9437184 | tf_op jit(solution)/shard_map/all_gather | solution.py:124
  180.2 438.8 %reduce-scatter.21.cloned.1.call-start = ((), (), s32[]{:S(2)}) async-start(), calls=%async_computation.32 | async-start | bytes 2621440 | tf_op jit(solution)/shard_map/reduce_scatter | solution.py:135
  588.7 89.1 %all-gather.35.cloned.1.call-start = ((), (), s32[]{:S(2)}) async-start(), calls=%async_computation.34 | async-start | bytes 2359296 | tf_op jit(solution)/shard_map/all_gather | solution.py:115
  589.3 104.6 %all-gather.33.cloned.1.call-start = ((), (), s32[]{:S(2)}) async-start(), calls=%async_computation.33 | async-start | bytes 2621440 | tf_op jit(solution)/shard_map/all_gather | solution.py:130
  639.8 274.8 %all-gather.37.cloned.1.call-start = ((), (), s32[]{:S(2)}) async-start(), calls=%async_computation.35 | async-start | bytes 2359296 | tf_op jit(solution)/shard_map/all_gather | solution.py:123
  659.3 303.9 %reduce-scatter.23.cloned.1.call-start = ((), (), s32[]{:S(2)}) async-start(), calls=%async_computation.36 | async-start | bytes 2621440 | tf_op jit(solution)/shard_map/reduce_scatter | solution.py:135
  700.0 28.8 collective-permute-start
  732.4 32.0 collective-permute-start
  767.9 33.1 collective-permute-start
  919.6 170.3 %all-gather.41.cloned.1.call-start = ((), (), s32[]{:S(2)}) async-start(), calls=%async_computation.38 | async-start | bytes 9437184 | tf_op jit(solution)/shard_map/all_gather | solution.py:118
  920.2 193.4 %all-gather.39.cloned.1.call-start = ((), (), s32[]{:S(2)}) async-start(), calls=%async_computation.37 | async-start | bytes 2621440 | tf_op jit(solution)/shard_map/all_gather | solution.py:130
  966.7 273.3 %all-gather.43.cloned.1.call-start = ((), (), s32[]{:S(2)}) async-start(), calls=%async_computation.39 | async-start | bytes 9437184 | tf_op jit(solution)/shard_map/all_gather | solution.py:119
  967.3 295.8 %all-gather.47.cloned.1.call-start = ((), (), s32[]{:S(2)}) async-start(), calls=%async_computation.42 | async-start | bytes 2621440 | tf_op jit(solution)/shard_map/all_gather | solution.py:143
  967.9 421.9 %all-gather.45.cloned.1.call-start = ((), (), s32[]{:S(2)}) async-start(), calls=%async_computation.40 | async-start | bytes 9437184 | tf_op jit(solution)/shard_map/all_gather | solution.py:125
  968.5 481.8 %reduce-scatter.27.cloned.1.call-start = ((), (), s32[]{:S(2)}) async-start(), calls=%async_computation.43 | async-start | bytes 2621440 | tf_op jit(solution)/shard_map/reduce_scatter | solution.py:148
  1420.1 56.9 %all-gather.49.cloned.1.call-start = ((), (), s32[]{:S(2)}) async-start(), calls=%async_computation.44 | async-start | bytes 2621440 | tf_op jit(solution)/shard_map/all_gather | solution.py:143
  1453.9 479.5 %reduce-scatter.29.cloned.1.call-start = ((), (), s32[]{:S(2)}) async-start(), calls=%async_computation.45 | async-start | bytes 2621440 | tf_op jit(solution)/shard_map/reduce_scatter | solution.py:148
  1491.8 45.0 %collective-permute-start.1 = (bf16[2,4,128,4,128]{4,2,3,1,0:T(8,128)(2,1)S(1)}, bf16[2,4,128,4,128]{4,2,3,1,0:T(8,128)(2,1)}, u32[]{:S(2)}, u32[]{:S(2)}) collective-permute-start(bf16[2,4,128,4,128]{4,2,3,1,0:T(8,128)(2,1)S(1)} %copy.197), channel_id=1, source_target_pairs={{0,4},{4,8},{8,12},{12,16},{16,20},{20,24},{24,28},{1,5},{5,9},{9,... | collective-permute-start | bytes 3145736 | tf_op jit(solution)/shard_map/while/body/eval_jaxpr/ppermute | solution.py:16
  1544.8 44.0 %collective-permute-start.1 = (bf16[2,4,128,4,128]{4,2,3,1,0:T(8,128)(2,1)S(1)}, bf16[2,4,128,4,128]{4,2,3,1,0:T(8,128)(2,1)}, u32[]{:S(2)}, u32[]{:S(2)}) collective-permute-start(bf16[2,4,128,4,128]{4,2,3,1,0:T(8,128)(2,1)S(1)} %copy.197), channel_id=1, source_target_pairs={{0,4},{4,8},{8,12},{12,16},{16,20},{20,24},{24,28},{1,5},{5,9},{9,... | collective-permute-start | bytes 3145736 | tf_op jit(solution)/shard_map/while/body/eval_jaxpr/ppermute | solution.py:16
  1596.8 43.1 %collective-permute-start.1 = (bf16[2,4,128,4,128]{4,2,3,1,0:T(8,128)(2,1)S(1)}, bf16[2,4,128,4,128]{4,2,3,1,0:T(8,128)(2,1)}, u32[]{:S(2)}, u32[]{:S(2)}) collective-permute-start(bf16[2,4,128,4,128]{4,2,3,1,0:T(8,128)(2,1)S(1)} %copy.197), channel_id=1, source_target_pairs={{0,4},{4,8},{8,12},{12,16},{16,20},{20,24},{24,28},{1,5},{5,9},{9,... | collective-permute-start | bytes 3145736 | tf_op jit(solution)/shard_map/while/body/eval_jaxpr/ppermute | solution.py:16
  1648.6 42.2 %collective-permute-start.1 = (bf16[2,4,128,4,128]{4,2,3,1,0:T(8,128)(2,1)S(1)}, bf16[2,4,128,4,128]{4,2,3,1,0:T(8,128)(2,1)}, u32[]{:S(2)}, u32[]{:S(2)}) collective-permute-start(bf16[2,4,128,4,128]{4,2,3,1,0:T(8,128)(2,1)S(1)} %copy.197), channel_id=1, source_target_pairs={{0,4},{4,8},{8,12},{12,16},{16,20},{20,24},{24,28},{1,5},{5,9},{9,... | collective-permute-start | bytes 3145736 | tf_op jit(solution)/shard_map/while/body/eval_jaxpr/ppermute | solution.py:16
  1699.6 41.3 %collective-permute-start.1 = (bf16[2,4,128,4,128]{4,2,3,1,0:T(8,128)(2,1)S(1)}, bf16[2,4,128,4,128]{4,2,3,1,0:T(8,128)(2,1)}, u32[]{:S(2)}, u32[]{:S(2)}) collective-permute-start(bf16[2,4,128,4,128]{4,2,3,1,0:T(8,128)(2,1)S(1)} %copy.197), channel_id=1, source_target_pairs={{0,4},{4,8},{8,12},{12,16},{16,20},{20,24},{24,28},{1,5},{5,9},{9,... | collective-permute-start | bytes 3145736 | tf_op jit(solution)/shard_map/while/body/eval_jaxpr/ppermute | solution.py:16
  1749.8 40.3 %collective-permute-start.1 = (bf16[2,4,128,4,128]{4,2,3,1,0:T(8,128)(2,1)S(1)}, bf16[2,4,128,4,128]{4,2,3,1,0:T(8,128)(2,1)}, u32[]{:S(2)}, u32[]{:S(2)}) collective-permute-start(bf16[2,4,128,4,128]{4,2,3,1,0:T(8,128)(2,1)S(1)} %copy.197), channel_id=1, source_target_pairs={{0,4},{4,8},{8,12},{12,16},{16,20},{20,24},{24,28},{1,5},{5,9},{9,... | collective-permute-start | bytes 3145736 | tf_op jit(solution)/shard_map/while/body/eval_jaxpr/ppermute | solution.py:16
  1799.0 39.4 %collective-permute-start.1 = (bf16[2,4,128,4,128]{4,2,3,1,0:T(8,128)(2,1)S(1)}, bf16[2,4,128,4,128]{4,2,3,1,0:T(8,128)(2,1)}, u32[]{:S(2)}, u32[]{:S(2)}) collective-permute-start(bf16[2,4,128,4,128]{4,2,3,1,0:T(8,128)(2,1)S(1)} %copy.197), channel_id=1, source_target_pairs={{0,4},{4,8},{8,12},{12,16},{16,20},{20,24},{24,28},{1,5},{5,9},{9,... | collective-permute-start | bytes 3145736 | tf_op jit(solution)/shard_map/while/body/eval_jaxpr/ppermute | solution.py:16
  1847.3 38.5 %collective-permute-start.1 = (bf16[2,4,128,4,128]{4,2,3,1,0:T(8,128)(2,1)S(1)}, bf16[2,4,128,4,128]{4,2,3,1,0:T(8,128)(2,1)}, u32[]{:S(2)}, u32[]{:S(2)}) collective-permute-start(bf16[2,4,128,4,128]{4,2,3,1,0:T(8,128)(2,1)S(1)} %copy.197), channel_id=1, source_target_pairs={{0,4},{4,8},{8,12},{12,16},{16,20},{20,24},{24,28},{1,5},{5,9},{9,... | collective-permute-start | bytes 3145736 | tf_op jit(solution)/shard_map/while/body/eval_jaxpr/ppermute | solution.py:16
  1891.7 75.8 %reduce-scatter.25.cloned.1.call-start = ((), (), s32[]{:S(2)}) async-start(), calls=%async_computation.41 | async-start | bytes 2621440 | tf_op jit(solution)/shard_map/reduce_scatter | solution.py:135
  1902.8 91.7 %all-gather.51.cloned.1.call-start = ((), (), s32[]{:S(2)}) async-start(), calls=%async_computation.46 | async-start | bytes 2621440 | tf_op jit(solution)/shard_map/all_gather | solution.py:143
  1971.3 84.2 %reduce-scatter.31.cloned.1.call-start = ((), (), s32[]{:S(2)}) async-start(), calls=%async_computation.47 | async-start | bytes 2621440 | tf_op jit(solution)/shard_map/reduce_scatter | solution.py:148
  2024.3 74.1 %all-gather.53.cloned.1.call-start = ((), (), s32[]{:S(2)}) async-start(), calls=%async_computation.48 | async-start | bytes 2621440 | tf_op jit(solution)/shard_map/all_gather | solution.py:143
  2059.3 123.4 %reduce-scatter.47.cloned.1.call-start = ((), (), s32[]{:S(2)}) async-start(), calls=%async_computation.56 | async-start | bytes 2359296 | tf_op jit(solution)/shard_map/reduce_scatter | solution.py:369
  2063.9 158.8 %reduce-scatter.45.cloned.1.call-start = ((), (), s32[]{:S(2)}) async-start(), calls=%async_computation.55 | async-start | bytes 2359296 | tf_op jit(solution)/shard_map/reduce_scatter | solution.py:349
  2069.7 307.0 %reduce-scatter.49.cloned.1.call-start = ((), (), s32[]{:S(2)}) async-start(), calls=%async_computation.57 | async-start | bytes 9437184 | tf_op jit(solution)/shard_map/reduce_scatter | solution.py:358
  2079.6 448.8 %reduce-scatter.51.cloned.1.call-start = ((), (), s32[]{:S(2)}) async-start(), calls=%async_computation.58 | async-start | bytes 9437184 | tf_op jit(solution)/shard_map/reduce_scatter | solution.py:361
  2088.2 592.6 %reduce-scatter.53.cloned.1.call-start = ((), (), s32[]{:S(2)}) async-start(), calls=%async_computation.59 | async-start | bytes 9437184 | tf_op jit(solution)/shard_map/reduce_scatter | solution.py:375
  2098.3 651.9 %reduce-scatter.37.cloned.1.call-start = ((), (), s32[]{:S(2)}) async-start(), calls=%async_computation.51 | async-start | bytes 2359296 | tf_op jit(solution)/shard_map/reduce_scatter | solution.py:366
  2103.6 717.6 %reduce-scatter.35.cloned.1.call-start = ((), (), s32[]{:S(2)}) async-start(), calls=%async_computation.50 | async-start | bytes 2359296 | tf_op jit(solution)/shard_map/reduce_scatter | solution.py:346
  2113.4 743.0 %reduce-scatter.33.cloned.1.call-start = ((), (), s32[]{:S(2)}) async-start(), calls=%async_computation.49 | async-start | bytes 2621440 | tf_op jit(solution)/shard_map/reduce_scatter | solution.py:148
  2118.7 892.3 %reduce-scatter.43.cloned.1.call-start = ((), (), s32[]{:S(2)}) async-start(), calls=%async_computation.54 | async-start | bytes 9437184 | tf_op jit(solution)/shard_map/reduce_scatter | solution.py:372
  2128.7 1033.9 %reduce-scatter.39.cloned.1.call-start = ((), (), s32[]{:S(2)}) async-start(), calls=%async_computation.52 | async-start | bytes 9437184 | tf_op jit(solution)/shard_map/reduce_scatter | solution.py:352
  2138.9 1175.7 %reduce-scatter.41.cloned.1.call-start = ((), (), s32[]{:S(2)}) async-start(), calls=%async_computation.53 | async-start | bytes 9437184 | tf_op jit(solution)/shard_map/reduce_scatter | solution.py:355
  2174.5 509.0 %all-to-all-start.3 = ((bf16[4,128,512]{2,1,0:T(8,128)(2,1)}), bf16[4,128,512]{2,1,0:T(8,128)(2,1)S(1)}, u32[]{:S(2)}, u32[]{:S(2)}) async-start(bf16[4,128,512]{2,1,0:T(8,128)(2,1)} %bitcast.44), calls=%async_computation.11 | async-start | bytes 1048576 | tf_op jit(solution)/shard_map/all_to_all | solution.py:323
  (82 other events, 2536.2 us)
Sparse Core Ops, SparseCore 0:
  10.7 27.3 all-gather.18
  40.2 47.7 all-gather.20
  90.1 50.0 all-gather.22
  144.5 30.1 reduce-scatter.18
  178.2 22.9 all-gather.24
  203.4 124.1 all-gather.26
  329.9 123.1 all-gather.28
  455.3 123.5 all-gather.30
  588.9 30.0 reduce-scatter.20
  620.9 48.1 all-gather.34
  671.3 22.6 all-gather.32
  695.9 61.2 all-gather.36
  919.7 43.3 reduce-scatter.22
  965.4 124.5 all-gather.40
  1092.0 21.5 all-gather.38
  1115.8 124.1 all-gather.42
  1241.5 21.5 all-gather.46
  1265.2 124.5 all-gather.44
  1420.2 30.0 reduce-scatter.26
  1454.0 22.9 all-gather.48
  1891.9 41.5 reduce-scatter.28
  1936.1 31.3 reduce-scatter.24
  1971.5 22.9 all-gather.50
  2024.4 31.0 reduce-scatter.30
  2059.5 22.9 all-gather.52
  2086.3 66.6 reduce-scatter.46
  2156.8 65.8 reduce-scatter.44
  2226.8 149.9 reduce-scatter.48
  2380.3 148.0 reduce-scatter.50
  2532.4 148.4 reduce-scatter.52
  2684.9 65.2 reduce-scatter.36
  2754.3 66.8 reduce-scatter.34
  2824.1 32.2 reduce-scatter.32
  2860.5 150.3 reduce-scatter.42
  3014.6 148.0 reduce-scatter.38
  3166.5 148.0 reduce-scatter.40
where the time goes:
time: 3340 us; the launch traced here: 3320 us
  waiting for transfers between devices  2620 us (78%)
  matrix products  279 us (8%)
  other arithmetic  134 us (4%)
  starting transfers between devices  129 us (4%)
  blocking collectives  80.3 us (2%)
  local copies, waits for them, and re-layouts  62.4 us (2%)
    ppermute x15, waiting for transfers between devices, passed_along(): lax.ppermute(value, axis, [(source, source + steps) for source in range(f...  264 us
    reduce_scatter x1, waiting for transfers between devices, body(): lax.psum_scatter(gate_two_grad.astype(jnp.bfloat16), 'seq', scatter_dimen...  152 us
    reduce_scatter x1, waiting for transfers between devices, body(): lax.psum_scatter(down_two_grad.astype(jnp.bfloat16), 'seq', scatter_dimen...  150 us
    reduce_scatter x1, waiting for transfers between devices, body(): lax.psum_scatter(up_one_grad.astype(jnp.bfloat16), 'seq', scatter_dimensi...  149 us
    reduce_scatter x1, waiting for transfers between devices, body(): lax.psum_scatter(gate_one_grad.astype(jnp.bfloat16), 'seq', scatter_dimen...  149 us
    reduce_scatter x1, waiting for transfers between devices, body(): lax.psum_scatter(up_two_grad.astype(jnp.bfloat16), 'seq', scatter_dimensi...  149 us
    reduce_scatter x4, waiting for transfers between devices, collect(): lax.psum_scatter(partial_value.reshape(row_count, tok_len, width).astype(...  135 us
    all_gather x1, waiting for transfers between devices, gather_weights(): lax.all_gather(ffn2_down, 'seq', axis=1, tiled=True)  127 us
  transfers between devices with their start and end apart: 62, of which 55 were waited for; matrix products, arithmetic and copies ran while one was open for 9% of the time, Pallas kernels for 0%

commit v1 on v0

v1 whole, which is shorter than its diff:
```python
import jax
import jax.numpy as jnp
from jax import lax
from jax.experimental import pallas as pl
from jax.experimental.pallas import tpu as pltpu
from jax.sharding import PartitionSpec as P

HEAD_DIM = 128


EPSILON = 1e-05
MASKED = -1e30
BF = jnp.bfloat16
F32 = jnp.float32


def passed_along(value, axis, steps):
    count = lax.axis_size(axis)
    first, last = (max(0, -steps), min(count, count - steps))
    return lax.ppermute(value, axis, [(source, source + steps) for source in range(first, last)])


def shifted(value, axis, steps):
    count = lax.axis_size(axis)
    pairs = [(source, (source + steps) % count) for source in range(count)]
    return lax.ppermute(value, axis, pairs)


def swapped(value, axis, mask):
    count = lax.axis_size(axis)
    return lax.ppermute(value, axis, [(source, source ^ mask) for source in range(count)])


def silu_slope(values):
    sigmoid = jax.nn.sigmoid(values)
    return sigmoid * (1.0 + values * (1.0 - sigmoid))


def rms_forward(values, gain_vec):
    inverse = lax.rsqrt(jnp.mean(values * values, axis=-1, keepdims=True) + EPSILON)
    return (values * inverse * gain_vec, inverse)


def rms_backward(values, inverse, gain_vec, grad_normed):
    scaled = grad_normed * gain_vec
    gain_grad = jnp.sum(grad_normed * values * inverse, axis=0)
    inner_sum = jnp.mean(scaled * values, axis=-1, keepdims=True)
    return (inverse * scaled - values * inverse * inverse * inverse * inner_sum, gain_grad)


def doc_numbers(doc_lengths, positions):
    doc_ends = jnp.cumsum(doc_lengths, axis=1, dtype=jnp.int32)
    return jnp.sum((positions[None, :, None] >= doc_ends[:, None, :]).astype(jnp.int32), axis=-1)


def dot_plain(left, right):
    return jnp.dot(left, right, preferred_element_type=F32)


def dot_left_t(left, right):
    return lax.dot_general(left, right, (((0,), (0,)), ((), ())), preferred_element_type=F32)


def dot_right_t(left, right):
    return lax.dot_general(left, right, (((1,), (1,)), ((), ())), preferred_element_type=F32)


def tile_mask(docs_col, docs_row, start, tile):
    keys = start + tile
    q_pos = lax.broadcasted_iota(jnp.int32, (tile, keys), 0) + start
    k_pos = lax.broadcasted_iota(jnp.int32, (tile, keys), 1)
    return (k_pos <= q_pos) & (docs_col[pl.ds(start, tile), :] == docs_row[:, pl.ds(0, keys)])


def attention_forward_kernel(tile, q_ref, k_ref, v_ref, docs_col, docs_row, out_ref, stat_ref):
    length = q_ref.shape[0]
    scale = HEAD_DIM ** (-0.5)
    for start in range(0, length, tile):
        keys = start + tile
        allowed = tile_mask(docs_col, docs_row, start, tile)
        scores = dot_right_t(q_ref[pl.ds(start, tile), :], k_ref[pl.ds(0, keys), :]) * scale
        scores = jnp.where(allowed, scores, MASKED)
        top = jnp.max(scores, axis=1, keepdims=True)
        expo = jnp.exp(scores - top)
        total = jnp.sum(expo, axis=1, keepdims=True)
        probs = (expo * (1.0 / total)).astype(BF)
        out_ref[pl.ds(start, tile), :] = dot_plain(probs, v_ref[pl.ds(0, keys), :]).astype(BF)
        stat_ref[pl.ds(start, tile), :] = jnp.broadcast_to(top + jnp.log(total), (tile, HEAD_DIM))


def attention_forward(q, k, v, docs):
    length, lanes = q.shape
    heads = lanes // HEAD_DIM
    tile = min(256, length)
    block = pl.BlockSpec((length, HEAD_DIM), lambda h: (0, h))
    return pl.pallas_call(
        lambda *refs: attention_forward_kernel(tile, *refs),
        grid=(heads,),
        in_specs=[
            block,
            block,
            block,
            pl.BlockSpec((length, 1), lambda h: (0, 0)),
            pl.BlockSpec((1, length), lambda h: (0, 0)),
        ],
        out_specs=[block, block],
        out_shape=[
            jax.ShapeDtypeStruct((length, lanes), BF),
            jax.ShapeDtypeStruct((length, lanes), F32),
        ],
        compiler_params=pltpu.CompilerParams(vmem_limit_bytes=40 * 2**20),
    )(q, k, v, docs[:, None], docs[None, :])


def attention_backward_kernel(
    tile, q_ref, k_ref, v_ref, dout_ref, stat_ref, docs_col, docs_row, dq_ref, dk_ref, dv_ref, dk_acc, dv_acc
):
    length = q_ref.shape[0]
    scale = HEAD_DIM ** (-0.5)
    for start in reversed(range(0, length, tile)):
        keys = start + tile
        allowed = tile_mask(docs_col, docs_row, start, tile)
        q = q_ref[pl.ds(start, tile), :]
        dout = dout_ref[pl.ds(start, tile), :]
        k = k_ref[pl.ds(0, keys), :]
        scores = dot_right_t(q, k) * scale
        probs = jnp.where(allowed, jnp.exp(scores - stat_ref[pl.ds(start, tile), 0:1]), 0.0)
        dprob = dot_right_t(dout, v_ref[pl.ds(0, keys), :])
        delta = jnp.sum(probs * dprob, axis=1, keepdims=True)
        dscores = (probs * (dprob - delta)).astype(BF)
        dq_ref[pl.ds(start, tile), :] = (dot_plain(dscores, k) * scale).astype(BF)
        dk = dot_left_t(dscores, q)
        dv = dot_left_t(probs.astype(BF), dout)
        if keys == length:
            dk_acc[...] = dk
            dv_acc[...] = dv
        else:
            dk_acc[pl.ds(0, keys), :] += dk
            dv_acc[pl.ds(0, keys), :] += dv
    dk_ref[...] = (dk_acc[...] * scale).astype(BF)
    dv_ref[...] = dv_acc[...].astype(BF)


def attention_backward(q, k, v, dout, stat, docs):
    length, lanes = q.shape
    heads = lanes // HEAD_DIM
    tile = min(256, length)
    block = pl.BlockSpec((length, HEAD_DIM), lambda h: (0, h))
    shape = jax.ShapeDtypeStruct((length, lanes), BF)
    return pl.pallas_call(
        lambda *refs: attention_backward_kernel(tile, *refs),
        grid=(heads,),
        in_specs=[
            block,
            block,
            block,
            block,
            block,
            pl.BlockSpec((length, 1), lambda h: (0, 0)),
            pl.BlockSpec((1, length), lambda h: (0, 0)),
        ],
        out_specs=[block, block, block],
        out_shape=[shape, shape, shape],
        scratch_shapes=[pltpu.VMEM((length, HEAD_DIM), F32), pltpu.VMEM((length, HEAD_DIM), F32)],
        compiler_params=pltpu.CompilerParams(vmem_limit_bytes=40 * 2**20),
    )(q, k, v, dout, stat, docs[:, None], docs[None, :])


def ring_attention(queries, kv_here, doc_lengths, tok_len, head_count):
    seq_count = lax.axis_size("seq")
    seq_index = lax.axis_index("seq")
    row_count = queries.shape[0]
    score_scale = HEAD_DIM ** (-0.5)
    local_pos = jnp.arange(tok_len, dtype=jnp.int32)

    def allowed_pairs(source):
        q_positions = seq_index * tok_len + local_pos
        key_pos = source * tok_len + local_pos
        q_docs = doc_numbers(doc_lengths, q_positions)
        key_docs = doc_numbers(doc_lengths, key_pos)
        causal = key_pos[None, :] <= q_positions[:, None]
        same_doc = q_docs[:, :, None] == key_docs[:, None, :]
        return (causal[None] & same_doc)[:, :, None, :]

    def absorb(softmax_state, kv_block, source):
        run_max, totals, accum = softmax_state
        scores = jnp.einsum("rihd,rjhd->rihj", queries, kv_block[0], preferred_element_type=F32)
        allowed = allowed_pairs(source)
        scores = jnp.where(allowed, scores * score_scale, MASKED)
        new_max = jnp.maximum(run_max, jnp.max(scores, axis=-1, keepdims=True))
        weights = jnp.where(allowed, jnp.exp(scores - new_max), 0.0)
        shrink = jnp.exp(run_max - new_max)
        totals = totals * shrink + jnp.sum(weights, axis=-1, keepdims=True)
        accum = accum * shrink + jnp.einsum(
            "rihj,rjhd->rihd", weights.astype(BF), kv_block[1], preferred_element_type=F32
        )
        return (new_max, totals, accum)

    stat_shape = (row_count, tok_len, head_count, 1)
    start_state = (
        jnp.full(stat_shape, MASKED, F32),
        jnp.zeros(stat_shape, F32),
        jnp.zeros((row_count, tok_len, head_count, HEAD_DIM), F32),
    )
    first_state = absorb(start_state, kv_here, seq_index)

    def cycle_forward(section_num, carry):
        softmax_state, kv_block = carry
        kv_block = passed_along(kv_block, "seq", 1)
        source = (seq_index - section_num) % seq_count
        return (absorb(softmax_state, kv_block, source), kv_block)

    final_state, _ = lax.fori_loop(1, seq_count, cycle_forward, (first_state, kv_here))
    run_max, totals, accum = final_state
    outputs = accum / totals
    log_sums = run_max + jnp.log(totals)

    def backward(dout):
        row_delta = jnp.sum(dout.astype(F32) * outputs, axis=-1, keepdims=True)
        head_shape = (row_count, tok_len, head_count, HEAD_DIM)

        def cycle_backward(section_num, carry):
            query_acc, kv_block, grad_block = carry
            source = (seq_index - section_num) % seq_count
            scores = jnp.einsum("rihd,rjhd->rihj", queries, kv_block[0], preferred_element_type=F32)
            allowed = allowed_pairs(source)
            probs = jnp.where(allowed, jnp.exp(scores * score_scale - log_sums), 0.0)
            dprob = jnp.einsum("rihd,rjhd->rihj", dout, kv_block[1], preferred_element_type=F32)
            dscores = (probs * (dprob - row_delta)).astype(BF)
            query_acc = (
                query_acc
                + jnp.einsum("rihj,rjhd->rihd", dscores, kv_block[0], preferred_element_type=F32)
                * score_scale
            )
            key_part = (
                jnp.einsum("rihj,rihd->rjhd", dscores, queries, preferred_element_type=F32)
                * score_scale
            )
            value_part = jnp.einsum(
                "rihj,rihd->rjhd", probs.astype(BF), dout, preferred_element_type=F32
            )
            grad_block = grad_block + jnp.stack([key_part, value_part])
            kv_block = passed_along(kv_block, "seq", 1)
            grad_block = shifted(grad_block.astype(BF), "seq", 1).astype(grad_block.dtype)
            return (query_acc, kv_block, grad_block)

        query_acc, _, grad_block = lax.fori_loop(
            0,
            seq_count,
            cycle_backward,
            (jnp.zeros(head_shape, F32), kv_here, jnp.zeros((2,) + head_shape, F32)),
        )
        return query_acc.astype(BF), grad_block.astype(BF)

    return outputs.astype(BF), backward


def body(
    block_input,
    memory,
    key_cache,
    value_cache,
    doc_lengths,
    gmu_gate,
    gmu_out,
    ffn1_gate,
    ffn1_up,
    ffn1_down,
    query_weight,
    attn_out,
    ffn2_gate,
    ffn2_up,
    ffn2_down,
    gain_a,
    gain_b,
    gain_c,
    gain_d,
    cotangent,
):
    seq_count = lax.axis_size("seq")
    row_count = lax.axis_size("row")
    seq_index = lax.axis_index("seq")
    tok_len = block_input.shape[1]
    width = block_input.shape[2]
    head_count = query_weight.shape[1] // HEAD_DIM
    depth = ffn1_gate.shape[0]
    half = ffn1_gate.shape[1] // 2
    z_count = seq_count // 2
    z_index, y_index = seq_index // 2, seq_index % 2
    parity = z_index % 2

    def spread(normed):
        return lax.all_gather(normed[None], "row", axis=0, tiled=True).reshape(
            row_count * tok_len, width
        )

    def collect(partial_value):
        return lax.psum_scatter(
            partial_value.reshape(row_count, tok_len, width).astype(BF),
            "row",
            scatter_dimension=0,
            tiled=True,
        ).astype(F32)[0]

    def spread_wide(normed):
        both = jnp.stack([normed, swapped(normed, "seq", 2)])
        return lax.all_gather(both[None], "row", axis=0, tiled=True).reshape(
            2 * row_count * tok_len, width
        )

    def collect_wide(partial_value):
        parts = partial_value.reshape(row_count, 2, tok_len, width).astype(BF)
        summed = lax.psum_scatter(parts, "row", scatter_dimension=0, tiled=True)[0]
        other = swapped(summed[1], "seq", 2)
        return summed[0].astype(F32) + other.astype(F32)

    def gather_ffn(gate, up, down):
        shard = jnp.stack([gate, up, down.T])
        whole = jnp.zeros((z_count, 2, 3, depth, half), BF)
        for step in range(z_count):
            want = (parity + step) % 2
            piece = lax.dynamic_slice_in_dim(shard, want * half, half, axis=2)
            if step:
                piece = swapped(piece, "seq", 2 * step)
            over = swapped(piece, "seq", 1)
            source = z_index ^ step
            whole = lax.dynamic_update_slice(whole, piece[None, None], (source, y_index, 0, 0, 0))
            whole = lax.dynamic_update_slice(whole, over[None, None], (source, 1 - y_index, 0, 0, 0))
        whole = whole.transpose(2, 0, 1, 3, 4).reshape(3, seq_count * depth, half)
        return whole[0], whole[1], whole[2]

    def scatter_ffn(gate_grad, up_grad, down_grad_t):
        whole = jnp.stack([gate_grad.astype(BF), up_grad.astype(BF), down_grad_t.astype(BF)])
        whole = whole.reshape(3, z_count, 2, depth, half)
        sums = [None, None]
        for step in range(z_count):
            target = z_index ^ step
            there = lax.dynamic_slice(
                whole, (0, target, 1 - y_index, 0, 0), (3, 1, 1, depth, half)
            )[:, 0, 0]
            here = lax.dynamic_slice(whole, (0, target, y_index, 0, 0), (3, 1, 1, depth, half))[:, 0, 0]
            total = here.astype(F32) + swapped(there, "seq", 1).astype(F32)
            if step:
                total = swapped(total.astype(BF), "seq", 2 * step).astype(F32)
            kind = step % 2
            sums[kind] = total if sums[kind] is None else sums[kind] + total
        pair = jnp.stack(sums)
        lower = lax.dynamic_index_in_dim(pair, parity, 0, keepdims=False)
        upper = lax.dynamic_index_in_dim(pair, 1 - parity, 0, keepdims=False)
        full = jnp.concatenate([lower, upper], axis=2)
        return full[0], full[1], full[2].T

    gmu_gate_full = lax.all_gather(gmu_gate, "seq", axis=0, tiled=True)
    gmu_out_full = lax.all_gather(gmu_out, "seq", axis=1, tiled=True)
    gate_one_w, up_one_w, down_one_t = gather_ffn(ffn1_gate, ffn1_up, ffn1_down)
    query_full = lax.all_gather(query_weight, "seq", axis=0, tiled=True)
    aout_full = lax.all_gather(attn_out, "seq", axis=1, tiled=True)
    gate_two_w, up_two_w, down_two_t = gather_ffn(ffn2_gate, ffn2_up, ffn2_down)

    def ffn_forward(rows_in, gate_weight, up_weight, down_weight_t):
        gate_val = dot_plain(rows_in, gate_weight)
        up_val = dot_plain(rows_in, up_weight)
        hidden = (jax.nn.silu(gate_val) * up_val).astype(BF)
        return (dot_right_t(hidden, down_weight_t), gate_val, up_val, hidden)

    def ffn_backward(cot_rows, rows_in, gate_val, up_val, hidden, gate_weight, up_weight, down_weight_t):
        dhid = dot_plain(cot_rows, down_weight_t)
        dgate = (dhid * up_val * silu_slope(gate_val)).astype(BF)
        dup = (dhid * jax.nn.silu(gate_val)).astype(BF)
        drows = dot_right_t(dgate, gate_weight) + dot_right_t(dup, up_weight)
        down_grad_t = dot_left_t(cot_rows, hidden)
        gate_grad = dot_left_t(rows_in, dgate)
        up_grad = dot_left_t(rows_in, dup)
        return (drows, gate_grad, up_grad, down_grad_t)

    mem_cols = lax.all_to_all(memory, "row", split_axis=2, concat_axis=0, tiled=True)
    mem_cols = mem_cols.reshape(row_count * tok_len, -1).astype(F32)
    kv_here = lax.all_to_all(
        jnp.concatenate([key_cache, value_cache], axis=0)[:, None], "row", split_axis=3, concat_axis=1, tiled=True
    )

    by_heads = seq_count % row_count == 0 and head_count % (seq_count // row_count) == 0
    share = max(1, seq_count // row_count)

    def to_heads(value):
        count = value.shape[0]
        value = value.reshape(count, row_count, tok_len, share, -1).transpose(1, 3, 0, 2, 4)
        value = value.reshape(seq_count, count, tok_len, -1)
        value = lax.all_to_all(value, "seq", split_axis=0, concat_axis=0, tiled=True)
        return value.transpose(1, 0, 2, 3).reshape(count, seq_count * tok_len, -1)

    def from_heads(value):
        count = value.shape[0]
        value = value.reshape(count, seq_count, tok_len, -1).transpose(1, 0, 2, 3)
        value = lax.all_to_all(value, "seq", split_axis=0, concat_axis=0, tiled=True)
        value = value.reshape(row_count, share, count, tok_len, -1).transpose(2, 0, 3, 1, 4)
        return value.reshape(count, row_count, tok_len, head_count * HEAD_DIM)

    x_zero = block_input[0].astype(F32)
    normed_a, inv_a = rms_forward(x_zero, gain_a)
    rows_a = spread(normed_a.astype(BF))
    gmu_pre = dot_plain(rows_a, gmu_gate_full)
    gmu_act = (mem_cols * jax.nn.silu(gmu_pre)).astype(BF)
    x_one = x_zero + collect(dot_plain(gmu_act, gmu_out_full))
    normed_b, inv_b = rms_forward(x_one, gain_b)
    rows_b = spread_wide(normed_b.astype(BF))
    part_one, gate_one, up_one, hidden_one = ffn_forward(rows_b, gate_one_w, up_one_w, down_one_t)
    x_two = x_one + collect_wide(part_one)
    normed_c, inv_c = rms_forward(x_two, gain_c)
    rows_c = spread(normed_c.astype(BF))
    queries = dot_plain(rows_c, query_full).astype(BF)
    if by_heads:
        positions = jnp.arange(seq_count * tok_len, dtype=jnp.int32)
        docs = lax.dynamic_index_in_dim(
            doc_numbers(doc_lengths, positions), seq_index // share, 0, keepdims=False
        )
        kv_heads = to_heads(kv_here)
        q_heads = to_heads(queries.reshape(1, row_count, tok_len, -1))[0]
        out_heads, stats = attention_forward(q_heads, kv_heads[0], kv_heads[1], docs)
        attended = from_heads(out_heads[None])

        def attention_grad(dout):
            dout_heads = to_heads(dout.reshape(1, row_count, tok_len, -1))[0]
            dq, dk, dv = attention_backward(
                q_heads, kv_heads[0], kv_heads[1], dout_heads, stats, docs
            )
            return from_heads(dq[None]), from_heads(jnp.stack([dk, dv]))

    else:
        head_shape = (row_count, tok_len, head_count, HEAD_DIM)
        attended, ring_grad = ring_attention(
            queries.reshape(head_shape), kv_here.reshape((2,) + head_shape), doc_lengths, tok_len, head_count
        )

        def attention_grad(dout):
            return ring_grad(dout.reshape(head_shape))

    attended = attended.reshape(row_count * tok_len, head_count * HEAD_DIM)
    x_three = x_two + collect(dot_plain(attended, aout_full))
    normed_d, inv_d = rms_forward(x_three, gain_d)
    rows_d = spread_wide(normed_d.astype(BF))
    part_two, gate_two, up_two, hidden_two = ffn_forward(rows_d, gate_two_w, up_two_w, down_two_t)
    mixed = x_three + collect_wide(part_two)

    grad_y = cotangent[0].astype(F32)
    drows_d, gate_two_grad, up_two_grad, down_two_grad = ffn_backward(
        spread_wide(cotangent[0]), rows_d, gate_two, up_two, hidden_two, gate_two_w, up_two_w, down_two_t
    )
    dx_d, gain_d_grad = rms_backward(x_three, inv_d, gain_d, collect_wide(drows_d))
    grad_three = grad_y + dx_d
    cot_three = spread(grad_three.astype(BF))
    dattended = dot_right_t(cot_three, aout_full)
    aout_grad = dot_left_t(attended, cot_three)
    dqueries, kv_grad = attention_grad(dattended.astype(BF))
    dqueries = dqueries.reshape(row_count * tok_len, head_count * HEAD_DIM)
    query_grad = dot_left_t(rows_c, dqueries)
    dx_c, gain_c_grad = rms_backward(x_two, inv_c, gain_c, collect(dot_right_t(dqueries, query_full)))
    grad_two = grad_three + dx_c
    drows_b, gate_one_grad, up_one_grad, down_one_grad = ffn_backward(
        spread_wide(grad_two.astype(BF)), rows_b, gate_one, up_one, hidden_one, gate_one_w, up_one_w, down_one_t
    )
    dx_b, gain_b_grad = rms_backward(x_one, inv_b, gain_b, collect_wide(drows_b))
    grad_one = grad_two + dx_b
    cot_one = spread(grad_one.astype(BF))
    dact = dot_right_t(cot_one, gmu_out_full)
    gout_grad = dot_left_t(gmu_act, cot_one)
    mem_grad_cols = dact * jax.nn.silu(gmu_pre)
    dpre = (dact * mem_cols * silu_slope(gmu_pre)).astype(BF)
    gate_a_grad = dot_left_t(rows_a, dpre)
    dx_a, gain_a_grad = rms_backward(x_zero, inv_a, gain_a, collect(dot_right_t(dpre, gmu_gate_full)))
    input_grad = grad_one + dx_a

    mem_grad = lax.all_to_all(
        mem_grad_cols.reshape(row_count, tok_len, -1).astype(BF), "row", split_axis=0, concat_axis=2, tiled=True
    ).astype(F32)
    kv_home = lax.all_to_all(
        kv_grad.reshape(2, row_count, tok_len, -1), "row", split_axis=1, concat_axis=3, tiled=True
    ).astype(F32)

    def scatter(grad, dim):
        return lax.psum_scatter(grad.astype(BF), "seq", scatter_dimension=dim, tiled=True).astype(F32)

    gate_two_out, up_two_out, down_two_out = scatter_ffn(gate_two_grad, up_two_grad, down_two_grad)
    aout_out = scatter(aout_grad, 1)
    query_out = scatter(query_grad, 0)
    gate_one_out, up_one_out, down_one_out = scatter_ffn(gate_one_grad, up_one_grad, down_one_grad)
    gout_out = scatter(gout_grad, 1)
    gate_a_out = scatter(gate_a_grad, 0)
    gain_grads = lax.psum((gain_a_grad, gain_b_grad, gain_c_grad, gain_d_grad), ("seq", "row"))
    return (
        mixed[None],
        input_grad[None],
        mem_grad,
        kv_home[0],
        kv_home[1],
        gate_a_out,
        gout_out,
        gate_one_out,
        up_one_out,
        down_one_out,
        query_out,
        aout_out,
        gate_two_out,
        up_two_out,
        down_two_out,
        gain_grads[0],
        gain_grads[1],
        gain_grads[2],
        gain_grads[3],
    )


def solution(mesh):
    tokens = P("row", "seq", None)
    inner, outer = P("seq", "row"), P("row", "seq")
    in_specs = (
        (tokens,) * 4
        + (P(), inner, outer, inner, inner, outer, inner, outer, inner, inner, outer)
        + (P(),) * 4
        + (tokens,)
    )
    out_specs = (
        (tokens,) * 5
        + (inner, outer, inner, inner, outer, inner, outer, inner, inner, outer)
        + (P(),) * 4
    )
    return jax.shard_map(body, mesh=mesh, in_specs=in_specs, out_specs=out_specs, check_vma=False)
```

time: 3340 us -> 1850 us (0.55)
  waiting for transfers between devices: 2620 us -> 1190 us
  matrix products: 279 us -> 179 us
  local copies, waits for them, and re-layouts: 62.4 us -> 122 us
  starting transfers between devices: 129 us -> 71.2 us
  blocking collectives: 80.3 us -> 136 us
    reduce_scatter x14 -> x8, waiting for transfers between devices: 1150 us -> 179 us  [the longest x4 179 us: collect_wide(): summed = lax.psum_scatter(parts, 'row', scatter_dimension=0, tiled=True)[0]]
    all_gather x14 -> x8, waiting for transfers between devices: 873 us -> 128 us  [the longest x1 47.6 us: body(): gmu_out_full = lax.all_gather(gmu_out, 'seq', axis=1, tiled=True)]
    ppermute x23 -> x36, waiting for transfers between devices: 387 us -> 665 us  [swapped(): lax.ppermute(value, axis, [(source, source ^ mask) for source in range(co...]
    ppermute x23 -> x36, starting transfers between devices: 113 us -> 40.3 us  [swapped(): lax.ppermute(value, axis, [(source, source ^ mask) for source in range(co...]
    all_to_all x3 -> x5, waiting for transfers between devices: 6.45 us -> 77.7 us  [the longest x1 56.6 us: from_heads(): lax.all_to_all(value, 'seq', split_axis=0, concat_axis=0, tiled=True)]
    dot_general x66 -> x10, matrix products: 136 us -> 72.1 us  [dot_plain(): return jnp.dot(left, right, preferred_element_type=F32)]
    all_to_all x2 -> x4, blocking collectives: 22.7 us -> 85.2 us  [the longest x2 47.4 us: from_heads(): lax.all_to_all(value, 'seq', split_axis=0, concat_axis=0, tiled=True)]
    reduce_scatter x4, waiting for transfers between devices: 135 us -> 92.2 us  [collect(): lax.psum_scatter(partial_value.reshape(row_count, tok_len, width).astype(...]
  transfers between devices with their start and end apart: 62 -> 65, of which waited for: 55 -> 36; matrix products, arithmetic and copies ran while one was open for 9% -> 16% of each run, Pallas kernels for 0% -> 0%
where the time goes in v1:
time: 1850 us; the launch traced here: 1840 us
  waiting for transfers between devices  1190 us (64%)
  matrix products  179 us (10%)
  blocking collectives  136 us (7%)
  local copies, waits for them, and re-layouts  122 us (7%)
  other arithmetic  110 us (6%)
  starting transfers between devices  71.2 us (4%)
    ppermute x36, waiting for transfers between devices, swapped(): lax.ppermute(value, axis, [(source, source ^ mask) for source in range(co...  665 us
    reduce_scatter x4, waiting for transfers between devices, collect_wide(): summed = lax.psum_scatter(parts, 'row', scatter_dimension=0, tiled=True)[0]  179 us
    reduce_scatter x4, waiting for transfers between devices, collect(): lax.psum_scatter(partial_value.reshape(row_count, tok_len, width).astype(...  92.2 us
    dot_general x10, matrix products, dot_plain(): return jnp.dot(left, right, preferred_element_type=F32)  72.1 us
    all_to_all x1, waiting for transfers between devices, from_heads(): lax.all_to_all(value, 'seq', split_axis=0, concat_axis=0, tiled=True)  56.6 us
    dot_general x10, matrix products, dot_left_t(): lax.dot_general(left, right, (((0,), (0,)), ((), ())), preferred_element_...  55.9 us
    dot_general x10, matrix products, dot_right_t(): lax.dot_general(left, right, (((1,), (1,)), ((), ())), preferred_element_...  50.7 us
    all_gather x4, waiting for transfers between devices, spread(): lax.all_gather(normed[None], 'row', axis=0, tiled=True)  47.8 us
  transfers between devices with their start and end apart: 65, of which 36 were waited for; matrix products, arithmetic and copies ran while one was open for 16% of the time, Pallas kernels for 0%

profile of v1, /device:TPU:1, one launch (start us, length us, event | category | flops | bytes accessed | tf_op | source)
XLA Modules:
  0.0 1837.7 jit_solution(3280615286820297994)
XLA Ops:
  15.4 11.5 reduce
  27.1 12.9 all_to_all.72
  42.1 44.8 %all-gather.22.cloned.1.call-done = bf16[2048,512]{1,0:T(8,128)(2,1)} async-done(((bf16[256,512]{1,0:T(8,128)(2,1)}), bf16[2048,512]{1,0:T(8,128)(2,1)}) %all-gather.22.cloned.1.call-update) | async-done | bytes 2097168 | tf_op jit(solution)/shard_map/all_gather | solution.py:353
  91.4 47.6 %all-gather.24.cloned.1.call-done = bf16[512,2048]{1,0:T(8,128)(2,1)} async-done(((bf16[512,256]{1,0:T(8,128)(2,1)}), bf16[512,2048]{1,0:T(8,128)(2,1)}) %all-gather.24.cloned.1.call-update) | async-done | bytes 2097168 | tf_op jit(solution)/shard_map/all_gather | solution.py:354
  143.3 30.3 %reduce-scatter.13.cloned.1.call-done = bf16[1,128,2048]{2,1,0:T(8,128)(2,1)} async-done(((bf16[4,128,2048]{2,1,0:T(8,128)(2,1)}), bf16[1,128,2048]{2,1,0:T(8,128)(2,1)}) %reduce-scatter.13.cloned.1.call-update) | async-done | bytes 524304 | tf_op jit(solution)/shard_map/reduce_scatter | solution.py:298
  178.9 10.3 collective-permute-done
  208.8 54.0 %collective-permute-done.2 = bf16[3,256,1024]{2,1,0:T(8,128)(2,1)} collective-permute-done((bf16[3,256,1024]{2,1,0:T(8,128)(2,1)}, bf16[3,256,1024]{2,1,0:T(8,128)(2,1)}, u32[]{:S(2)}, u32[]{:S(2)}) %collective-permute-start.2) | collective-permute-done | bytes 1572896 | tf_op jit(solution)/shard_map/ppermute | solution.py:31
  264.4 35.3 %collective-permute-done.6 = bf16[3,256,1024]{2,1,0:T(8,128)(2,1)} collective-permute-done((bf16[3,256,1024]{2,1,0:T(8,128)(2,1)S(1)}, bf16[3,256,1024]{2,1,0:T(8,128)(2,1)}, u32[]{:S(2)}, u32[]{:S(2)}) %collective-permute-start.6) | collective-permute-done | bytes 1572896 | tf_op jit(solution)/shard_map/ppermute | solution.py:31
  311.7 12.8 collective-permute-done.5
  329.9 28.3 %collective-permute-done.7 = bf16[3,256,1024]{2,1,0:T(8,128)(2,1)S(1)} collective-permute-done((bf16[3,256,1024]{2,1,0:T(8,128)(2,1)}, bf16[3,256,1024]{2,1,0:T(8,128)(2,1)S(1)}, u32[]{:S(2)}, u32[]{:S(2)}) %collective-permute-start.7) | collective-permute-done | bytes 1572896 | tf_op jit(solution)/shard_map/ppermute | solution.py:31
  391.3 53.4 %reduce-scatter.15.cloned.1.call-done = bf16[1,2,128,2048]{3,2,1,0:T(8,128)(2,1)} async-done(((bf16[4,2,128,2048]{3,2,1,0:T(8,128)(2,1)}), bf16[1,2,128,2048]{3,2,1,0:T(8,128)(2,1)}) %reduce-scatter.15.cloned.1.call-update) | async-done | bytes 1048592 | tf_op jit(solution)/shard_map/reduce_scatter | solution.py:313
  447.0 13.3 collective-permute-done.8
  467.7 19.0 %all_to_all.73 = bf16[2,1,128,2048]{2,0,1,3:T(2,128)(2,1)S(1)} all-to-all(bf16[2,1,128,2048]{2,0,1,3:T(2,128)(2,1)S(1)} %maximum_bitcast_fusion), channel_id=1, replica_groups=mesh['seq'=8,'row'=4] {'row'}, dimensions={3} | all-to-all | bytes 2097152 | tf_op jit(solution)/shard_map/all_to_all | solution.py:378
  497.4 23.8 %all-gather.32.cloned.1.call-done = bf16[512,2048]{1,0:T(8,128)(2,1)} async-done(((bf16[128,2048]{1,0:T(8,128)(2,1)}), bf16[512,2048]{1,0:T(8,128)(2,1)}) %all-gather.32.cloned.1.call-update) | async-done | bytes 2097168 | tf_op jit(solution)/shard_map/all_gather | solution.py:293
  531.6 21.1 %all-to-all-done.1 = bf16[8,1,128,256]{3,2,1,0:T(8,128)(2,1)S(1)} async-done(((bf16[8,1,128,256]{3,2,1,0:T(8,128)(2,1)}), bf16[8,1,128,256]{3,2,1,0:T(8,128)(2,1)S(1)}, u32[]{:S(2)}, u32[]{:S(2)}) %all-to-all-start.1) | async-done | bytes 524320 | tf_op jit(solution)/shard_map/all_to_all | solution.py:389
  557.8 29.5 %all_to_all.74 = bf16[8,1,128,256]{3,2,1,0:T(8,128)(2,1)S(1)} all-to-all(bf16[8,1,128,256]{3,2,1,0:T(8,128)(2,1)S(1)} %bitcast.477), channel_id=1, replica_groups=mesh['seq'=8,'row'=4] {'seq'}, dimensions={0} | all-to-all | bytes 1048576 | tf_op jit(solution)/shard_map/all_to_all | solution.py:395
  595.2 31.4 %reduce-scatter.17.cloned.1.call-done = bf16[1,128,2048]{2,1,0:T(8,128)(2,1)} async-done(((bf16[4,128,2048]{2,1,0:T(8,128)(2,1)}), bf16[1,128,2048]{2,1,0:T(8,128)(2,1)}) %reduce-scatter.17.cloned.1.call-update) | async-done | bytes 524304 | tf_op jit(solution)/shard_map/reduce_scatter | solution.py:298
  629.8 11.5 collective-permute-done.9
  663.3 65.5 %collective-permute-done.18 = bf16[128,2048]{1,0:T(8,128)(2,1)} collective-permute-done((bf16[128,2048]{1,0:T(8,128)(2,1)}, bf16[128,2048]{1,0:T(8,128)(2,1)}, u32[]{:S(2)}, u32[]{:S(2)}) %collective-permute-start.18) | collective-permute-done | bytes 524320 | tf_op jit(solution)/shard_map/ppermute | solution.py:31
  732.8 31.4 %collective-permute-done.15 = bf16[3,256,1024]{2,1,0:T(8,128)(2,1)} collective-permute-done((bf16[3,256,1024]{2,1,0:T(8,128)(2,1)}, bf16[3,256,1024]{2,1,0:T(8,128)(2,1)}, u32[]{:S(2)}, u32[]{:S(2)}) %collective-permute-start.15) | collective-permute-done | bytes 1572896 | tf_op jit(solution)/shard_map/ppermute | solution.py:31
  774.9 23.6 %collective-permute-done.14 = bf16[3,256,1024]{2,1,0:T(8,128)(2,1)S(1)} collective-permute-done((bf16[3,256,1024]{2,1,0:T(8,128)(2,1)}, bf16[3,256,1024]{2,1,0:T(8,128)(2,1)S(1)}, u32[]{:S(2)}, u32[]{:S(2)}) %collective-permute-start.14) | collective-permute-done | bytes 1572896 | tf_op jit(solution)/shard_map/ppermute | solution.py:31
  802.4 29.8 %collective-permute-done.16 = bf16[3,256,1024]{2,1,0:T(8,128)(2,1)S(1)} collective-permute-done((bf16[3,256,1024]{2,1,0:T(8,128)(2,1)}, bf16[3,256,1024]{2,1,0:T(8,128)(2,1)S(1)}, u32[]{:S(2)}, u32[]{:S(2)}) %collective-permute-start.16) | collective-permute-done | bytes 1572896 | tf_op jit(solution)/shard_map/ppermute | solution.py:31
  842.4 10.1 fusion.81
  858.9 13.2 multiply_convert_fusion.2
  883.3 9.5 convolution_convert_fusion.6
  892.9 37.6 %reduce-scatter.21.cloned.1.call-done = bf16[1,2,128,2048]{3,2,1,0:T(8,128)(2,1)} async-done(((bf16[4,2,128,2048]{3,2,1,0:T(8,128)(2,1)}), bf16[1,2,128,2048]{3,2,1,0:T(8,128)(2,1)}) %reduce-scatter.21.cloned.1.call-update) | async-done | bytes 1048592 | tf_op jit(solution)/shard_map/reduce_scatter | solution.py:313
  933.6 43.8 %reduce-scatter.19.cloned.1.call-done = bf16[1,2,128,2048]{3,2,1,0:T(8,128)(2,1)} async-done(((bf16[4,2,128,2048]{3,2,1,0:T(8,128)(2,1)}), bf16[1,2,128,2048]{3,2,1,0:T(8,128)(2,1)}) %reduce-scatter.19.cloned.1.call-update) | async-done | bytes 1048592 | tf_op jit(solution)/shard_map/reduce_scatter | solution.py:313
  982.4 9.1 collective-permute-done.17
  994.8 23.9 %all-gather.38.cloned.1.call-done = bf16[512,2048]{1,0:T(8,128)(2,1)} async-done(((bf16[128,2048]{1,0:T(8,128)(2,1)}), bf16[512,2048]{1,0:T(8,128)(2,1)}) %all-gather.38.cloned.1.call-update) | async-done | bytes 2097168 | tf_op jit(solution)/shard_map/all_gather | solution.py:293
  1026.1 18.8 %all_to_all.75 = bf16[8,1,128,256]{3,2,1,0:T(8,128)(2,1)S(1)} all-to-all(bf16[8,1,128,256]{3,2,1,0:T(8,128)(2,1)S(1)} %bitcast.520), channel_id=1, replica_groups=mesh['seq'=8,'row'=4] {'seq'}, dimensions={0} | all-to-all | bytes 1048576 | tf_op jit(solution)/shard_map/all_to_all | solution.py:389
  1051.5 17.8 all_to_all.76
  1074.8 30.6 %reduce-scatter.23.cloned.1.call-done = bf16[1,128,2048]{2,1,0:T(8,128)(2,1)} async-done(((bf16[4,128,2048]{2,1,0:T(8,128)(2,1)}), bf16[1,128,2048]{2,1,0:T(8,128)(2,1)}) %reduce-scatter.23.cloned.1.call-update) | async-done | bytes 524304 | tf_op jit(solution)/shard_map/reduce_scatter | solution.py:298
  1110.0 11.5 collective-permute-done.20
  1122.7 35.9 %all-gather.40.cloned.1.call-done = bf16[8,128,2048]{2,1,0:T(8,128)(2,1)} async-done(((bf16[2,128,2048]{2,1,0:T(8,128)(2,1)}), bf16[8,128,2048]{2,1,0:T(8,128)(2,1)}) %all-gather.40.cloned.1.call-update) | async-done | bytes 4194320 | tf_op jit(solution)/shard_map/all_gather | solution.py:307
  1158.6 11.8 multiply_convert_fusion
  1181.6 44.0 %reduce-scatter.25.cloned.1.call-done = bf16[1,2,128,2048]{3,2,1,0:T(8,128)(2,1)} async-done(((bf16[4,2,128,2048]{3,2,1,0:T(8,128)(2,1)}), bf16[1,2,128,2048]{3,2,1,0:T(8,128)(2,1)}) %reduce-scatter.25.cloned.1.call-update) | async-done | bytes 1048592 | tf_op jit(solution)/shard_map/reduce_scatter | solution.py:313
  1228.1 11.6 collective-permute-done.21
  1287.3 40.4 %collective-permute-done.30 = bf16[3,256,1024]{2,1,0:T(8,128)(2,1)S(1)} collective-permute-done((bf16[3,256,1024]{2,1,0:T(8,128)(2,1)S(1)}, bf16[3,256,1024]{2,1,0:T(8,128)(2,1)S(1)}, u32[]{:S(2)}, u32[]{:S(2)}) %collective-permute-start.30) | collective-permute-done | bytes 1572896 | tf_op jit(solution)/shard_map/ppermute | solution.py:31
  1327.7 39.4 %collective-permute-done.32 = bf16[3,256,1024]{2,1,0:T(8,128)(2,1)S(1)} collective-permute-done((bf16[3,256,1024]{2,1,0:T(8,128)(2,1)S(1)}, bf16[3,256,1024]{2,1,0:T(8,128)(2,1)S(1)}, u32[]{:S(2)}, u32[]{:S(2)}) %collective-permute-start.32) | collective-permute-done | bytes 1572896 | tf_op jit(solution)/shard_map/ppermute | solution.py:31
  1367.2 42.0 %collective-permute-done.34 = bf16[3,256,1024]{2,1,0:T(8,128)(2,1)S(1)} collective-permute-done((bf16[3,256,1024]{2,1,0:T(8,128)(2,1)S(1)}, bf16[3,256,1024]{2,1,0:T(8,128)(2,1)S(1)}, u32[]{:S(2)}, u32[]{:S(2)}) %collective-permute-start.34) | collective-permute-done | bytes 1572896 | tf_op jit(solution)/shard_map/ppermute | solution.py:31
  1423.7 9.6 convolution_convert_fusion.3
  1462.1 11.3 collective-permute-done.33
  1475.2 35.9 %collective-permute-done.35 = bf16[3,256,1024]{2,1,0:T(8,128)(2,1)} collective-permute-done((bf16[3,256,1024]{2,1,0:T(8,128)(2,1)}, bf16[3,256,1024]{2,1,0:T(8,128)(2,1)}, u32[]{:S(2)}, u32[]{:S(2)}) %collective-permute-start.35) | collective-permute-done | bytes 1572896 | tf_op jit(solution)/shard_map/ppermute | solution.py:31
  1514.9 56.6 %all-to-all-done.8 = bf16[8,2,128,256]{3,2,1,0:T(8,128)(2,1)S(1)} async-done(((bf16[8,2,128,256]{3,2,1,0:T(8,128)(2,1)}), bf16[8,2,128,256]{3,2,1,0:T(8,128)(2,1)S(1)}, u32[]{:S(2)}, u32[]{:S(2)}) %all-to-all-start.8) | async-done | bytes 1048608 | tf_op jit(solution)/shard_map/all_to_all | solution.py:395
  1593.1 20.4 %collective-permute-done.29 = bf16[3,256,1024]{2,1,0:T(8,128)(2,1)} collective-permute-done((bf16[3,256,1024]{2,1,0:T(8,128)(2,1)}, bf16[3,256,1024]{2,1,0:T(8,128)(2,1)}, u32[]{:S(2)}, u32[]{:S(2)}) %collective-permute-start.29) | collective-permute-done | bytes 1572896 | tf_op jit(solution)/shard_map/ppermute | solution.py:31
  1634.2 60.0 %collective-permute-done.26 = bf16[3,256,1024]{2,1,0:T(8,128)(2,1)} collective-permute-done((bf16[3,256,1024]{2,1,0:T(8,128)(2,1)}, bf16[3,256,1024]{2,1,0:T(8,128)(2,1)}, u32[]{:S(2)}, u32[]{:S(2)}) %collective-permute-start.26) | collective-permute-done | bytes 1572896 | tf_op jit(solution)/shard_map/ppermute | solution.py:31
  1698.4 67.0 %collective-permute-done.24 = bf16[3,256,1024]{2,1,0:T(8,128)(2,1)} collective-permute-done((bf16[3,256,1024]{2,1,0:T(8,128)(2,1)}, bf16[3,256,1024]{2,1,0:T(8,128)(2,1)}, u32[]{:S(2)}, u32[]{:S(2)}) %collective-permute-start.24) | collective-permute-done | bytes 1572896 | tf_op jit(solution)/shard_map/ppermute | solution.py:31
  1788.3 37.9 %all-reduce = (f32[2048]{0:T(1024)}, f32[2048]{0:T(1024)}, f32[2048]{0:T(1024)}, f32[2048]{0:T(1024)}) all-reduce(f32[2048]{0:T(1024)S(1)} %get-tuple-element.111, f32[2048]{0:T(1024)S(1)} %get-tuple-element.107, f32[2048]{0:T(1024)S(1)} %copy-done.43, f32[2048]{0:T(1024)S(1)} %copy-done.42), channel_id=1, replica_groups=mesh['seq'=8,'row'=4] {'seq','row'}, use_global_device_ids=true, to_apply=%region_23.24 | all-reduce | flops 8192 | bytes 65536 | tf_op jit(solution)/shard_map/psum | solution.py:489
  (404 shorter events, 430.6 us)
Async XLA Ops:
  11.0 75.8 %all-gather.22.cloned.1.call-start = ((), (), s32[]{:S(2)}) async-start(), calls=%async_computation.23 | async-start | bytes 2359296 | tf_op jit(solution)/shard_map/all_gather | solution.py:353
  11.8 127.2 %all-gather.24.cloned.1.call-start = ((), (), s32[]{:S(2)}) async-start(), calls=%async_computation.24 | async-start | bytes 2359296 | tf_op jit(solution)/shard_map/all_gather | solution.py:354
  12.5 161.1 %reduce-scatter.13.cloned.1.call-start = ((), (), s32[]{:S(2)}) async-start(), calls=%async_computation.25 | async-start | bytes 2621440 | tf_op jit(solution)/shard_map/reduce_scatter | solution.py:298
  143.3 225.0 %all-gather.30.cloned.1.call-start = ((), (), s32[]{:S(2)}) async-start(), calls=%async_computation.39 | async-start | bytes 5242880 | tf_op jit(solution)/shard_map/all_gather | solution.py:307
  190.2 254.4 %reduce-scatter.15.cloned.1.call-start = ((), (), s32[]{:S(2)}) async-start(), calls=%async_computation.26 | async-start | bytes 5242880 | tf_op jit(solution)/shard_map/reduce_scatter | solution.py:313
  195.8 67.1 %collective-permute-start.2 = (bf16[3,256,1024]{2,1,0:T(8,128)(2,1)}, bf16[3,256,1024]{2,1,0:T(8,128)(2,1)}, u32[]{:S(2)}, u32[]{:S(2)}) collective-permute-start(bf16[3,256,1024]{2,1,0:T(8,128)(2,1)} %get-tuple-element.169), channel_id=1, source_target_pairs={{0,8},{4,12},{8,0},{12,4},{16,24},{20,28},{24,16},{28,20},{1,9},{5... | collective-permute-start | bytes 4718600 | tf_op jit(solution)/shard_map/ppermute | solution.py:31
  197.0 67.1 %collective-permute-start.4 = (bf16[3,256,1024]{2,1,0:T(8,128)(2,1)}, bf16[3,256,1024]{2,1,0:T(8,128)(2,1)}, u32[]{:S(2)}, u32[]{:S(2)}) collective-permute-start(bf16[3,256,1024]{2,1,0:T(8,128)(2,1)} %get-tuple-element.168), channel_id=1, source_target_pairs={{0,16},{4,20},{8,24},{12,28},{16,0},{20,4},{24,8},{28,12},{1,17},{... | collective-permute-start | bytes 4718600 | tf_op jit(solution)/shard_map/ppermute | solution.py:31
  199.1 100.6 %collective-permute-start.6 = (bf16[3,256,1024]{2,1,0:T(8,128)(2,1)S(1)}, bf16[3,256,1024]{2,1,0:T(8,128)(2,1)}, u32[]{:S(2)}, u32[]{:S(2)}) collective-permute-start(bf16[3,256,1024]{2,1,0:T(8,128)(2,1)S(1)} %get-tuple-element.167), channel_id=1, source_target_pairs={{0,24},{4,28},{8,16},{12,20},{16,8},{20,12},{24,0},{28,4},{1,25},{... | collective-permute-start | bytes 4718600 | tf_op jit(solution)/shard_map/ppermute | solution.py:31
  207.6 93.3 %collective-permute-start.1 = (bf16[3,256,1024]{2,1,0:T(8,128)(2,1)}, bf16[3,256,1024]{2,1,0:T(8,128)(2,1)}, u32[]{:S(2)}, u32[]{:S(2)}) collective-permute-start(bf16[3,256,1024]{2,1,0:T(8,128)(2,1)} %get-tuple-element.128), channel_id=1, source_target_pairs={{0,4},{4,0},{8,12},{12,8},{16,20},{20,16},{24,28},{28,24},{1,5},{5... | collective-permute-start | bytes 4718600 | tf_op jit(solution)/shard_map/ppermute | solution.py:31
  264.1 60.4 %collective-permute-start.5 = (bf16[3,256,1024]{2,1,0:T(8,128)(2,1)}, bf16[3,256,1024]{2,1,0:T(8,128)(2,1)}, u32[]{:S(2)}, u32[]{:S(2)}) collective-permute-start(bf16[3,256,1024]{2,1,0:T(8,128)(2,1)} %collective-permute-done.4), channel_id=1, source_target_pairs={{0,4},{4,0},{8,12},{12,8},{16,20},{20,16},{24,28},{28,24},{1,5},{5... | collective-permute-start | bytes 4718600 | tf_op jit(solution)/shard_map/ppermute | solution.py:31
  390.1 107.3 %all-gather.26.cloned.1.call-start = ((), (), s32[]{:S(2)}) async-start(), calls=%async_computation.27 | async-start | bytes 2359296 | tf_op jit(solution)/shard_map/all_gather | solution.py:356
  390.9 130.3 %all-gather.32.cloned.1.call-start = ((), (), s32[]{:S(2)}) async-start(), calls=%async_computation.40 | async-start | bytes 2621440 | tf_op jit(solution)/shard_map/all_gather | solution.py:293
  496.6 94.2 %all-gather.28.cloned.1.call-start = ((), (), s32[]{:S(2)}) async-start(), calls=%async_computation.28 | async-start | bytes 2359296 | tf_op jit(solution)/shard_map/all_gather | solution.py:357
  530.9 95.7 %reduce-scatter.17.cloned.1.call-start = ((), (), s32[]{:S(2)}) async-start(), calls=%async_computation.29 | async-start | bytes 2621440 | tf_op jit(solution)/shard_map/reduce_scatter | solution.py:298
  595.2 247.2 %all-gather.34.cloned.1.call-start = ((), (), s32[]{:S(2)}) async-start(), calls=%async_computation.41 | async-start | bytes 5242880 | tf_op jit(solution)/shard_map/all_gather | solution.py:307
  642.3 216.5 %all-gather.36.cloned.1.call-start = ((), (), s32[]{:S(2)}) async-start(), calls=%async_computation.42 | async-start | bytes 5242880 | tf_op jit(solution)/shard_map/all_gather | solution.py:307
  649.2 82.1 %collective-permute-start.11 = (bf16[3,256,1024]{2,1,0:T(8,128)(2,1)}, bf16[3,256,1024]{2,1,0:T(8,128)(2,1)}, u32[]{:S(2)}, u32[]{:S(2)}) collective-permute-start(bf16[3,256,1024]{2,1,0:T(8,128)(2,1)} %get-tuple-element.166), channel_id=1, source_target_pairs={{0,8},{4,12},{8,0},{12,4},{16,24},{20,28},{24,16},{28,20},{1,9},{5... | collective-permute-start | bytes 4718600 | tf_op jit(solution)/shard_map/ppermute | solution.py:31
  650.3 78.4 %collective-permute-start.18 = (bf16[128,2048]{1,0:T(8,128)(2,1)}, bf16[128,2048]{1,0:T(8,128)(2,1)}, u32[]{:S(2)}, u32[]{:S(2)}) collective-permute-start(bf16[128,2048]{1,0:T(8,128)(2,1)} %bitcast.90), channel_id=1, source_target_pairs={{0,8},{4,12},{8,0},{12,4},{16,24},{20,28},{24,16},{28,20},{1,9},{5... | collective-permute-start | bytes 1572872 | tf_op jit(solution)/shard_map/ppermute | solution.py:31
  650.6 81.9 %collective-permute-start.13 = (bf16[3,256,1024]{2,1,0:T(8,128)(2,1)}, bf16[3,256,1024]{2,1,0:T(8,128)(2,1)}, u32[]{:S(2)}, u32[]{:S(2)}) collective-permute-start(bf16[3,256,1024]{2,1,0:T(8,128)(2,1)} %get-tuple-element.165), channel_id=1, source_target_pairs={{0,16},{4,20},{8,24},{12,28},{16,0},{20,4},{24,8},{28,12},{1,17},{... | collective-permute-start | bytes 4718600 | tf_op jit(solution)/shard_map/ppermute | solution.py:31
  661.0 104.5 %collective-permute-start.10 = (bf16[3,256,1024]{2,1,0:T(8,128)(2,1)}, bf16[3,256,1024]{2,1,0:T(8,128)(2,1)}, u32[]{:S(2)}, u32[]{:S(2)}) collective-permute-start(bf16[3,256,1024]{2,1,0:T(8,128)(2,1)} %get-tuple-element.122), channel_id=1, source_target_pairs={{0,4},{4,0},{8,12},{12,8},{16,20},{20,16},{24,28},{28,24},{1,5},{5... | collective-permute-start | bytes 4718600 | tf_op jit(solution)/shard_map/ppermute | solution.py:31
  662.2 102.1 %collective-permute-start.15 = (bf16[3,256,1024]{2,1,0:T(8,128)(2,1)}, bf16[3,256,1024]{2,1,0:T(8,128)(2,1)}, u32[]{:S(2)}, u32[]{:S(2)}) collective-permute-start(bf16[3,256,1024]{2,1,0:T(8,128)(2,1)} %get-tuple-element.164), channel_id=1, source_target_pairs={{0,24},{4,28},{8,16},{12,20},{16,8},{20,12},{24,0},{28,4},{1,25},{... | collective-permute-start | bytes 4718600 | tf_op jit(solution)/shard_map/ppermute | solution.py:31
  731.1 199.4 %reduce-scatter.21.cloned.1.call-start = ((), (), s32[]{:S(2)}) async-start(), calls=%async_computation.31 | async-start | bytes 5242880 | tf_op jit(solution)/shard_map/reduce_scatter | solution.py:313
  732.5 66.0 %collective-permute-start.14 = (bf16[3,256,1024]{2,1,0:T(8,128)(2,1)}, bf16[3,256,1024]{2,1,0:T(8,128)(2,1)S(1)}, u32[]{:S(2)}, u32[]{:S(2)}) collective-permute-start(bf16[3,256,1024]{2,1,0:T(8,128)(2,1)} %collective-permute-done.13), channel_id=1, source_target_pairs={{0,4},{4,0},{8,12},{12,8},{16,20},{20,16},{24,28},{28,24},{1,5},{5... | collective-permute-start | bytes 4718600 | tf_op jit(solution)/shard_map/ppermute | solution.py:31
  764.3 68.0 %collective-permute-start.16 = (bf16[3,256,1024]{2,1,0:T(8,128)(2,1)}, bf16[3,256,1024]{2,1,0:T(8,128)(2,1)S(1)}, u32[]{:S(2)}, u32[]{:S(2)}) collective-permute-start(bf16[3,256,1024]{2,1,0:T(8,128)(2,1)} %collective-permute-done.15), channel_id=1, source_target_pairs={{0,4},{4,0},{8,12},{12,8},{16,20},{20,16},{24,28},{28,24},{1,5},{5... | collective-permute-start | bytes 4718600 | tf_op jit(solution)/shard_map/ppermute | solution.py:31
  882.9 94.5 %reduce-scatter.19.cloned.1.call-start = ((), (), s32[]{:S(2)}) async-start(), calls=%async_computation.30 | async-start | bytes 5242880 | tf_op jit(solution)/shard_map/reduce_scatter | solution.py:313
  892.8 125.9 %all-gather.38.cloned.1.call-start = ((), (), s32[]{:S(2)}) async-start(), calls=%async_computation.43 | async-start | bytes 2621440 | tf_op jit(solution)/shard_map/all_gather | solution.py:293
  994.7 110.6 %reduce-scatter.23.cloned.1.call-start = ((), (), s32[]{:S(2)}) async-start(), calls=%async_computation.32 | async-start | bytes 2621440 | tf_op jit(solution)/shard_map/reduce_scatter | solution.py:298
  1074.6 84.1 %all-gather.40.cloned.1.call-start = ((), (), s32[]{:S(2)}) async-start(), calls=%async_computation.44 | async-start | bytes 5242880 | tf_op jit(solution)/shard_map/all_gather | solution.py:307
  1122.7 102.9 %reduce-scatter.25.cloned.1.call-start = ((), (), s32[]{:S(2)}) async-start(), calls=%async_computation.33 | async-start | bytes 5242880 | tf_op jit(solution)/shard_map/reduce_scatter | solution.py:313
  1181.3 94.1 %all-gather.42.cloned.1.call-start = ((), (), s32[]{:S(2)}) async-start(), calls=%async_computation.45 | async-start | bytes 2621440 | tf_op jit(solution)/shard_map/all_gather | solution.py:293
  1243.3 387.3 %reduce-scatter.35.cloned.1.call-start = ((), (), s32[]{:S(2)}) async-start(), calls=%async_computation.38 | async-start | bytes 2359296 | tf_op jit(solution)/shard_map/reduce_scatter | solution.py:481
  1248.9 383.5 %reduce-scatter.33.cloned.1.call-start = ((), (), s32[]{:S(2)}) async-start(), calls=%async_computation.37 | async-start | bytes 2359296 | tf_op jit(solution)/shard_map/reduce_scatter | solution.py:481
  1251.7 533.5 %reduce-scatter.31.cloned.1.call-start = ((), (), s32[]{:S(2)}) async-start(), calls=%async_computation.36 | async-start | bytes 2359296 | tf_op jit(solution)/shard_map/reduce_scatter | solution.py:481
  1285.9 81.3 %collective-permute-start.32 = (bf16[3,256,1024]{2,1,0:T(8,128)(2,1)S(1)}, bf16[3,256,1024]{2,1,0:T(8,128)(2,1)S(1)}, u32[]{:S(2)}, u32[]{:S(2)}) collective-permute-start(bf16[3,256,1024]{2,1,0:T(8,128)(2,1)S(1)} %get-tuple-element.132), channel_id=1, source_target_pairs={{0,4},{4,0},{8,12},{12,8},{16,20},{20,16},{24,28},{28,24},{1,5},{5... | collective-permute-start | bytes 4718600 | tf_op jit(solution)/shard_map/ppermute | solution.py:31
  1286.1 123.1 %collective-permute-start.34 = (bf16[3,256,1024]{2,1,0:T(8,128)(2,1)S(1)}, bf16[3,256,1024]{2,1,0:T(8,128)(2,1)S(1)}, u32[]{:S(2)}, u32[]{:S(2)}) collective-permute-start(bf16[3,256,1024]{2,1,0:T(8,128)(2,1)S(1)} %get-tuple-element.134), channel_id=1, source_target_pairs={{0,4},{4,0},{8,12},{12,8},{16,20},{20,16},{24,28},{28,24},{1,5},{5... | collective-permute-start | bytes 4718600 | tf_op jit(solution)/shard_map/ppermute | solution.py:31
  1416.7 94.4 %collective-permute-start.35 = (bf16[3,256,1024]{2,1,0:T(8,128)(2,1)}, bf16[3,256,1024]{2,1,0:T(8,128)(2,1)}, u32[]{:S(2)}, u32[]{:S(2)}) collective-permute-start(bf16[3,256,1024]{2,1,0:T(8,128)(2,1)} %get-tuple-element.131), channel_id=1, source_target_pairs={{0,24},{4,28},{8,16},{12,20},{16,8},{20,12},{24,0},{28,4},{1,25},{... | collective-permute-start | bytes 4718600 | tf_op jit(solution)/shard_map/ppermute | solution.py:31
  1419.9 151.6 %all-to-all-start.8 = ((bf16[8,2,128,256]{3,2,1,0:T(8,128)(2,1)}), bf16[8,2,128,256]{3,2,1,0:T(8,128)(2,1)S(1)}, u32[]{:S(2)}, u32[]{:S(2)}) async-start(bf16[8,2,128,256]{3,2,1,0:T(8,128)(2,1)} %maximum_bitcast_fusion.1), calls=%async_computation.16 | async-start | bytes 2097152 | tf_op jit(solution)/shard_map/all_to_all | solution.py:395
  1423.4 363.5 %reduce-scatter.27.cloned.1.call-start = ((), (), s32[]{:S(2)}) async-start(), calls=%async_computation.34 | async-start | bytes 2621440 | tf_op jit(solution)/shard_map/reduce_scatter | solution.py:298
  1459.3 124.1 %collective-permute-start.23 = (bf16[3,256,1024]{2,1,0:T(8,128)(2,1)}, bf16[3,256,1024]{2,1,0:T(8,128)(2,1)}, u32[]{:S(2)}, u32[]{:S(2)}) collective-permute-start(bf16[3,256,1024]{2,1,0:T(8,128)(2,1)} %get-tuple-element.140), channel_id=1, source_target_pairs={{0,4},{4,0},{8,12},{12,8},{16,20},{20,16},{24,28},{28,24},{1,5},{5... | collective-permute-start | bytes 4718600 | tf_op jit(solution)/shard_map/ppermute | solution.py:31
  1460.6 122.8 %collective-permute-start.25 = (bf16[3,256,1024]{2,1,0:T(8,128)(2,1)}, bf16[3,256,1024]{2,1,0:T(8,128)(2,1)}, u32[]{:S(2)}, u32[]{:S(2)}) collective-permute-start(bf16[3,256,1024]{2,1,0:T(8,128)(2,1)} %get-tuple-element.139), channel_id=1, source_target_pairs={{0,4},{4,0},{8,12},{12,8},{16,20},{20,16},{24,28},{28,24},{1,5},{5... | collective-permute-start | bytes 4718600 | tf_op jit(solution)/shard_map/ppermute | solution.py:31
  1460.8 122.6 %collective-permute-start.27 = (bf16[3,256,1024]{2,1,0:T(8,128)(2,1)}, bf16[3,256,1024]{2,1,0:T(8,128)(2,1)}, u32[]{:S(2)}, u32[]{:S(2)}) collective-permute-start(bf16[3,256,1024]{2,1,0:T(8,128)(2,1)} %get-tuple-element.141), channel_id=1, source_target_pairs={{0,4},{4,0},{8,12},{12,8},{16,20},{20,16},{24,28},{28,24},{1,5},{5... | collective-permute-start | bytes 4718600 | tf_op jit(solution)/shard_map/ppermute | solution.py:31
  1473.4 140.2 %collective-permute-start.29 = (bf16[3,256,1024]{2,1,0:T(8,128)(2,1)}, bf16[3,256,1024]{2,1,0:T(8,128)(2,1)}, u32[]{:S(2)}, u32[]{:S(2)}) collective-permute-start(bf16[3,256,1024]{2,1,0:T(8,128)(2,1)} %get-tuple-element.135), channel_id=1, source_target_pairs={{0,4},{4,0},{8,12},{12,8},{16,20},{20,16},{24,28},{28,24},{1,5},{5... | collective-permute-start | bytes 4718600 | tf_op jit(solution)/shard_map/ppermute | solution.py:31
  1511.1 102.5 %collective-permute-start.31 = (bf16[3,256,1024]{2,1,0:T(8,128)(2,1)}, bf16[3,256,1024]{2,1,0:T(8,128)(2,1)}, u32[]{:S(2)}, u32[]{:S(2)}) collective-permute-start(bf16[3,256,1024]{2,1,0:T(8,128)(2,1)} %get-tuple-element.130), channel_id=1, source_target_pairs={{0,16},{4,20},{8,24},{12,28},{16,0},{20,4},{24,8},{28,12},{1,17},{... | collective-permute-start | bytes 4718600 | tf_op jit(solution)/shard_map/ppermute | solution.py:31
  1579.2 247.1 %reduce-scatter.29.cloned.1.call-start = ((), (), s32[]{:S(2)}) async-start(), calls=%async_computation.35 | async-start | bytes 2359296 | tf_op jit(solution)/shard_map/reduce_scatter | solution.py:481
  1591.3 102.9 %collective-permute-start.26 = (bf16[3,256,1024]{2,1,0:T(8,128)(2,1)}, bf16[3,256,1024]{2,1,0:T(8,128)(2,1)}, u32[]{:S(2)}, u32[]{:S(2)}) collective-permute-start(bf16[3,256,1024]{2,1,0:T(8,128)(2,1)} %get-tuple-element.136), channel_id=1, source_target_pairs={{0,8},{4,12},{8,0},{12,4},{16,24},{20,28},{24,16},{28,20},{1,9},{5... | collective-permute-start | bytes 4718600 | tf_op jit(solution)/shard_map/ppermute | solution.py:31
  1591.3 102.9 %collective-permute-start.28 = (bf16[3,256,1024]{2,1,0:T(8,128)(2,1)}, bf16[3,256,1024]{2,1,0:T(8,128)(2,1)}, u32[]{:S(2)}, u32[]{:S(2)}) collective-permute-start(bf16[3,256,1024]{2,1,0:T(8,128)(2,1)} %get-tuple-element.138), channel_id=1, source_target_pairs={{0,24},{4,28},{8,16},{12,20},{16,8},{20,12},{24,0},{28,4},{1,25},{... | collective-permute-start | bytes 4718600 | tf_op jit(solution)/shard_map/ppermute | solution.py:31
  1616.9 81.5 %collective-permute-start.22 = (bf16[3,256,1024]{2,1,0:T(8,128)(2,1)}, bf16[3,256,1024]{2,1,0:T(8,128)(2,1)}, u32[]{:S(2)}, u32[]{:S(2)}) collective-permute-start(bf16[3,256,1024]{2,1,0:T(8,128)(2,1)} %get-tuple-element.142), channel_id=1, source_target_pairs={{0,4},{4,0},{8,12},{12,8},{16,20},{20,16},{24,28},{28,24},{1,5},{5... | collective-permute-start | bytes 4718600 | tf_op jit(solution)/shard_map/ppermute | solution.py:31
  1617.9 147.5 %collective-permute-start.24 = (bf16[3,256,1024]{2,1,0:T(8,128)(2,1)}, bf16[3,256,1024]{2,1,0:T(8,128)(2,1)}, u32[]{:S(2)}, u32[]{:S(2)}) collective-permute-start(bf16[3,256,1024]{2,1,0:T(8,128)(2,1)} %get-tuple-element.137), channel_id=1, source_target_pairs={{0,16},{4,20},{8,24},{12,28},{16,0},{20,4},{24,8},{28,12},{1,17},{... | collective-permute-start | bytes 4718600 | tf_op jit(solution)/shard_map/ppermute | solution.py:31
  (89 other events, 2065.8 us)
Sparse Core Ops, SparseCore 0:
  11.2 25.7 all-gather.19
  39.1 47.7 all-gather.21
  88.9 50.0 all-gather.23
  143.4 30.1 reduce-scatter.12
  190.4 35.7 all-gather.29
  390.2 54.4 reduce-scatter.14
  446.8 49.5 all-gather.25
  498.6 22.5 all-gather.31
  523.2 67.1 all-gather.27
  595.3 31.2 reduce-scatter.16
  642.4 35.7 all-gather.33
  731.2 38.6 all-gather.35
  883.0 47.4 reduce-scatter.20
  932.8 44.4 reduce-scatter.18
  994.9 23.8 all-gather.37
  1074.7 30.6 reduce-scatter.22
  1122.8 35.7 all-gather.39
  1181.4 44.1 reduce-scatter.24
  1243.4 23.8 all-gather.41
  1271.7 73.8 reduce-scatter.34
  1350.1 74.7 reduce-scatter.32
  1428.8 96.3 reduce-scatter.30
  1527.9 34.9 reduce-scatter.26
  1583.5 142.4 reduce-scatter.28

commit v2 on v1

--- a/solution.py
+++ b/solution.py
@@ -1,3 +1,5 @@
+from types import SimpleNamespace
+
 import jax
 import jax.numpy as jnp
 from jax import lax
@@ -63,107 +65,6 @@
 
 def dot_right_t(left, right):
     return lax.dot_general(left, right, (((1,), (1,)), ((), ())), preferred_element_type=F32)
-
-
-def tile_mask(docs_col, docs_row, start, tile):
-    keys = start + tile
-    q_pos = lax.broadcasted_iota(jnp.int32, (tile, keys), 0) + start
-    k_pos = lax.broadcasted_iota(jnp.int32, (tile, keys), 1)
-    return (k_pos <= q_pos) & (docs_col[pl.ds(start, tile), :] == docs_row[:, pl.ds(0, keys)])
-
-
-def attention_forward_kernel(tile, q_ref, k_ref, v_ref, docs_col, docs_row, out_ref, stat_ref):
-    length = q_ref.shape[0]
-    scale = HEAD_DIM ** (-0.5)
-    for start in range(0, length, tile):
-        keys = start + tile
-        allowed = tile_mask(docs_col, docs_row, start, tile)
-        scores = dot_right_t(q_ref[pl.ds(start, tile), :], k_ref[pl.ds(0, keys), :]) * scale
-        scores = jnp.where(allowed, scores, MASKED)
-        top = jnp.max(scores, axis=1, keepdims=True)
-        expo = jnp.exp(scores - top)
-        total = jnp.sum(expo, axis=1, keepdims=True)
-        probs = (expo * (1.0 / total)).astype(BF)
-        out_ref[pl.ds(start, tile), :] = dot_plain(probs, v_ref[pl.ds(0, keys), :]).astype(BF)
-        stat_ref[pl.ds(start, tile), :] = jnp.broadcast_to(top + jnp.log(total), (tile, HEAD_DIM))
-
-
-def attention_forward(q, k, v, docs):
-    length, lanes = q.shape
-    heads = lanes // HEAD_DIM
-    tile = min(256, length)
-    block = pl.BlockSpec((length, HEAD_DIM), lambda h: (0, h))
-    return pl.pallas_call(
-        lambda *refs: attention_forward_kernel(tile, *refs),
-        grid=(heads,),
-        in_specs=[
-            block,
-            block,
-            block,
-            pl.BlockSpec((length, 1), lambda h: (0, 0)),
-            pl.BlockSpec((1, length), lambda h: (0, 0)),
-        ],
-        out_specs=[block, block],
-        out_shape=[
-            jax.ShapeDtypeStruct((length, lanes), BF),
-            jax.ShapeDtypeStruct((length, lanes), F32),
-        ],
-        compiler_params=pltpu.CompilerParams(vmem_limit_bytes=40 * 2**20),
-    )(q, k, v, docs[:, None], docs[None, :])
-
-
-def attention_backward_kernel(
-    tile, q_ref, k_ref, v_ref, dout_ref, stat_ref, docs_col, docs_row, dq_ref, dk_ref, dv_ref, dk_acc, dv_acc
-):
-    length = q_ref.shape[0]
-    scale = HEAD_DIM ** (-0.5)
-    for start in reversed(range(0, length, tile)):
-        keys = start + tile
-        allowed = tile_mask(docs_col, docs_row, start, tile)
-        q = q_ref[pl.ds(start, tile), :]
-        dout = dout_ref[pl.ds(start, tile), :]
-        k = k_ref[pl.ds(0, keys), :]
-        scores = dot_right_t(q, k) * scale
-        probs = jnp.where(allowed, jnp.exp(scores - stat_ref[pl.ds(start, tile), 0:1]), 0.0)
-        dprob = dot_right_t(dout, v_ref[pl.ds(0, keys), :])
-        delta = jnp.sum(probs * dprob, axis=1, keepdims=True)
-        dscores = (probs * (dprob - delta)).astype(BF)
-        dq_ref[pl.ds(start, tile), :] = (dot_plain(dscores, k) * scale).astype(BF)
-        dk = dot_left_t(dscores, q)
-        dv = dot_left_t(probs.astype(BF), dout)
-        if keys == length:
-            dk_acc[...] = dk
-            dv_acc[...] = dv
-        else:
-            dk_acc[pl.ds(0, keys), :] += dk
-            dv_acc[pl.ds(0, keys), :] += dv
-    dk_ref[...] = (dk_acc[...] * scale).astype(BF)
-    dv_ref[...] = dv_acc[...].astype(BF)
-
-
-def attention_backward(q, k, v, dout, stat, docs):
-    length, lanes = q.shape
-    heads = lanes // HEAD_DIM
-    tile = min(256, length)
-    block = pl.BlockSpec((length, HEAD_DIM), lambda h: (0, h))
-    shape = jax.ShapeDtypeStruct((length, lanes), BF)
-    return pl.pallas_call(
-        lambda *refs: attention_backward_kernel(tile, *refs),
-        grid=(heads,),
-        in_specs=[
-            block,
-            block,
-            block,
-            block,
-            block,
-            pl.BlockSpec((length, 1), lambda h: (0, 0)),
-            pl.BlockSpec((1, length), lambda h: (0, 0)),
-        ],
-        out_specs=[block, block, block],
-        out_shape=[shape, shape, shape],
-        scratch_shapes=[pltpu.VMEM((length, HEAD_DIM), F32), pltpu.VMEM((length, HEAD_DIM), F32)],
-        compiler_params=pltpu.CompilerParams(vmem_limit_bytes=40 * 2**20),
-    )(q, k, v, dout, stat, docs[:, None], docs[None, :])
 
 
 def ring_attention(queries, kv_here, doc_lengths, tok_len, head_count):
@@ -255,7 +156,997 @@
     return outputs.astype(BF), backward
 
 
-def body(
+MESH = pl.DeviceIdType.MESH
+VMEM_LIMIT = 62 * 2**20
+
+
+def flipped(value, mask):
+    bit = 1
+    while bit <= mask:
+        if mask & bit:
+            value = value + bit - 2 * bit * lax.rem(lax.div(value, bit), 2)
+        bit *= 2
+    return value
+
+
+def rows_at(index, size):
+    return pl.ds(pl.multiple_of(index * size, size), size)
+
+
+def part_of(index, size):
+    return pl.ds(index * size, size)
+
+
+class Links:
+    def __init__(self, send, recv):
+        self.send, self.recv, self.used, self.sent = send, recv, 0, []
+        self.row, self.seq = lax.axis_index("row"), lax.axis_index("seq")
+        self.z, self.y = lax.div(self.seq, 2), lax.rem(self.seq, 2)
+        self.parity = lax.rem(self.z, 2)
+
+    def device(self, row_mask, seq_mask):
+        return {"row": flipped(self.row, row_mask), "seq": flipped(self.seq, seq_mask)}
+
+    def greet(self, masks):
+        barrier = pltpu.get_barrier_semaphore()
+        for mask in masks:
+            pl.semaphore_signal(barrier, inc=1, device_id=self.device(*mask), device_id_type=MESH)
+        pl.semaphore_wait(barrier, len(masks))
+
+    def slot(self):
+        self.used += 1
+        assert self.used <= self.send.shape[0]
+        return self.used - 1
+
+    def copy(self, src, dst, row_mask, seq_mask):
+        slot = self.slot()
+        move = pltpu.make_async_remote_copy(
+            src_ref=src,
+            dst_ref=dst,
+            send_sem=self.send.at[slot],
+            recv_sem=self.recv.at[slot],
+            device_id=self.device(row_mask, seq_mask),
+            device_id_type=MESH,
+        )
+        move.start()
+        self.sent.append(move)
+        return move
+
+    def local(self, src, dst):
+        move = pltpu.make_async_copy(src, dst, self.send.at[self.slot()])
+        move.start()
+        return move
+
+    def finish(self, moves=None):
+        moves = list(self.sent if moves is None else moves)
+        for move in moves:
+            move.wait_send()
+        done = {id(move) for move in moves}
+        self.sent = [move for move in self.sent if id(move) not in done]
+
+
+def wait(moves):
+    for move in moves:
+        move.wait()
+
+
+def landed(moves):
+    for move in moves[0]:
+        move.wait_recv()
+    moves[1].wait()
+
+
+class Gather:
+    def __init__(self, links, shard, whole, outer, parts):
+        self.links, self.shard, self.whole, self.outer, self.parts = links, shard, whole, outer, parts
+        self.z_moves, self.y_moves = {}, {}
+
+    def piece(self, step):
+        if self.parts == 1:
+            return self.shard
+        part = lax.rem(self.links.parity + step, 2)
+        if self.outer:
+            return self.shard.at[rows_at(part, self.shard.shape[0] // 2), :]
+        return self.shard.at[:, rows_at(part, self.shard.shape[1] // 2)]
+
+    def place(self, source):
+        if self.outer:
+            return self.whole.at[:, rows_at(source, self.shard.shape[1])]
+        return self.whole.at[rows_at(source, self.shard.shape[0]), :]
+
+    def own(self):
+        self.keep = self.links.local(self.piece(0), self.place(self.links.seq))
+        self.y_moves[0] = self.links.copy(self.piece(0), self.place(self.links.seq), 0, 1)
+
+    def over_z(self, *steps):
+        for step in steps:
+            if step == 3 and self.parts == 1:
+                self.z_moves[2].wait_recv()
+                here = self.place(flipped(self.links.seq, 4))
+                self.z_moves[3] = self.links.copy(here, here, 0, 2)
+            else:
+                self.z_moves[step] = self.links.copy(self.piece(step), self.place(self.links.seq), 0, 2 * step)
+
+    def over_y(self, *steps):
+        for step in steps:
+            if not (step == 2 and 3 in self.z_moves and self.parts == 1):
+                self.z_moves[step].wait_recv()
+            here = self.place(flipped(self.links.seq, 2 * step))
+            self.y_moves[step] = self.links.copy(here, here, 0, 1)
+
+    def arrived(self):
+        self.keep.wait()
+        for step in range(4):
+            self.y_moves[step].wait_recv()
+
+
+def each(weights, action, *steps):
+    for step in steps:
+        for weight in weights:
+            action(weight, step)
+
+
+def chip_masks(wide):
+    return [(0, 0), (2, 0)] + ([(0, 2), (2, 2)] if wide else [])
+
+
+def chip_rows(links, mask, wide, tok):
+    chip = lax.div(flipped(links.row, mask[0]), 2)
+    if wide:
+        chip = chip * 2 + lax.rem(links.parity + mask[1] // 2, 2)
+    return rows_at(chip, 2 * tok)
+
+
+def block_rows(links, mask, wide, tok, other=0):
+    chip = lax.div(flipped(links.row, mask[0]), 2)
+    if wide:
+        chip = chip * 2 + lax.rem(links.parity + mask[1] // 2, 2)
+    return rows_at(chip * 2 + lax.rem(links.row + other, 2), tok)
+
+
+class Spread:
+    def __init__(self, links, whole, wide, tok):
+        self.links, self.whole, self.wide, self.tok = links, whole, wide, tok
+        self.masks = chip_masks(wide)
+
+    def place(self, mask):
+        return self.whole.at[block_rows(self.links, mask, self.wide, self.tok), :]
+
+    def own(self):
+        return block_rows(self.links, (0, 0), self.wide, self.tok)
+
+    def start(self):
+        here = self.place((0, 0))
+        self.far = [self.links.copy(here, here, *mask) for mask in self.masks[1:]]
+        self.near = [self.links.copy(here, here, 1, 0)]
+
+    def forward(self):
+        for mask, move in zip(self.masks[1:], self.far):
+            move.wait_recv()
+            there = self.place(mask)
+            self.near.append(self.links.copy(there, there, 1, 0))
+
+    def wait(self):
+        for move in self.near:
+            move.wait_recv()
+
+    def by_chip(self, compute):
+        for k, mask in enumerate(self.masks):
+            if k:
+                self.far[k - 1].wait_recv()
+                there = self.place(mask)
+                self.near.append(self.links.copy(there, there, 1, 0))
+            self.near[k].wait_recv()
+            compute(chip_rows(self.links, mask, self.wide, self.tok))
+
+    def finish(self):
+        self.links.finish(self.far + self.near)
+
+
+class Collect:
+    def __init__(self, links, parts, from_core, from_far, wide, tok):
+        self.links, self.parts, self.wide, self.tok = links, parts, wide, tok
+        self.from_core, self.from_far = from_core, from_far
+        self.masks = chip_masks(wide)
+        self.near, self.far = {}, {}
+
+    def block(self, mask, other=0):
+        return self.parts.at[block_rows(self.links, mask, self.wide, self.tok, other), :]
+
+    def slot(self, ref, k):
+        return ref.at[part_of(k, self.tok), :]
+
+    def forward(self, k):
+        self.near[k].wait_recv()
+        mine = self.block(self.masks[k])
+        mine[...] = (mine[...].astype(F32) + self.slot(self.from_core, k)[...].astype(F32)).astype(BF)
+        self.far[k] = self.links.copy(mine, self.slot(self.from_far, k - 1), *self.masks[k])
+
+    def run(self, compute):
+        last = len(self.masks) - 1
+        for k in range(last, -1, -1):
+            compute(chip_rows(self.links, self.masks[k], self.wide, self.tok))
+            self.near[k] = self.links.copy(self.block(self.masks[k], 1), self.slot(self.from_core, k), 1, 0)
+            if k < last:
+                self.forward(k + 1)
+
+    def result(self):
+        self.near[0].wait_recv()
+        total = self.block((0, 0))[...].astype(F32) + self.slot(self.from_core, 0)[...].astype(F32)
+        for k in range(1, len(self.masks)):
+            self.far[k].wait_recv()
+            total = total + self.slot(self.from_far, k - 1)[...].astype(F32)
+        return total
+
+    def finish(self):
+        self.links.finish(list(self.near.values()) + list(self.far.values()))
+
+
+def normed_block(values, gain):
+    inverse = lax.rsqrt(jnp.mean(values * values, axis=-1, keepdims=True) + EPSILON)
+    return (values * inverse * gain).astype(BF)
+
+
+def norm_back(values, gain, grad_normed):
+    inverse = lax.rsqrt(jnp.mean(values * values, axis=-1, keepdims=True) + EPSILON)
+    scaled = grad_normed * gain
+    gain_grad = jnp.sum(grad_normed * values * inverse, axis=0, keepdims=True)
+    inner_sum = jnp.mean(scaled * values, axis=-1, keepdims=True)
+    return inverse * scaled - values * inverse * inverse * inverse * inner_sum, gain_grad
+
+
+def silu(values):
+    return values * jax.nn.sigmoid(values)
+
+
+def columns_loop(columns, tile, step):
+    @pl.loop(0, columns // tile)
+    def _(index):
+        step(rows_at(index, tile))
+
+
+def to_heads(links, src, dst, tok):
+    wide = dst.shape[1]
+
+    def block(seq):
+        return src.at[rows_at(lax.div(seq, 2), tok), rows_at(lax.rem(seq, 2), wide)]
+
+    here = dst.at[rows_at(links.seq, tok), :]
+    moves = [links.copy(block(flipped(links.seq, mask)), here, 0, mask) for mask in range(1, 8)]
+    return moves, links.local(block(links.seq), here)
+
+
+def from_heads(links, src, dst, tok):
+    wide = src.shape[1]
+    here = dst.at[rows_at(links.z, tok), rows_at(links.y, wide)]
+    moves = [links.copy(src.at[rows_at(flipped(links.seq, mask), tok), :], here, 0, mask) for mask in range(1, 8)]
+    return moves, links.local(src.at[rows_at(links.seq, tok), :], here)
+
+
+def to_columns(links, src, dst, tok, cols):
+    here = dst.at[rows_at(links.row, tok), :]
+    moves = [links.copy(src.at[:, rows_at(flipped(links.row, mask), cols)], here, mask, 0) for mask in (1, 2, 3)]
+    return moves, links.local(src.at[:, rows_at(links.row, cols)], here)
+
+
+def from_columns(links, src, dst, tok, cols):
+    here = dst.at[:, rows_at(links.row, cols)]
+    moves = [links.copy(src.at[rows_at(flipped(links.row, mask), tok), :], here, mask, 0) for mask in (1, 2, 3)]
+    return moves, links.local(src.at[rows_at(links.row, tok), :], here)
+
+
+def tile_mask(docs_col, docs_row, start, tile):
+    keys = start + tile
+    q_pos = lax.broadcasted_iota(jnp.int32, (tile, keys), 0) + start
+    k_pos = lax.broadcasted_iota(jnp.int32, (tile, keys), 1)
+    return (k_pos <= q_pos) & (docs_col[pl.ds(start, tile), :] == docs_row[:, pl.ds(0, keys)])
+
+
+def softmax_tile(q, k, docs_col, docs_row, start, tile):
+    scores = dot_right_t(q, k) * (HEAD_DIM ** (-0.5))
+    scores = jnp.where(tile_mask(docs_col, docs_row, start, tile), scores, MASKED)
+    expo = jnp.exp(scores - jnp.max(scores, axis=1, keepdims=True))
+    return expo * (1.0 / jnp.sum(expo, axis=1, keepdims=True))
+
+
+def attend(q_ref, k_ref, v_ref, docs_col, docs_row, out_ref):
+    length = q_ref.shape[0]
+    tile = min(256, length)
+
+    @pl.loop(0, q_ref.shape[1] // HEAD_DIM)
+    def _(head):
+        lanes = rows_at(head, HEAD_DIM)
+        for start in range(0, length, tile):
+            keys, here = pl.ds(0, start + tile), pl.ds(start, tile)
+            probs = softmax_tile(q_ref[here, lanes], k_ref[keys, lanes], docs_col, docs_row, start, tile)
+            out_ref[here, lanes] = dot_plain(probs.astype(BF), v_ref[keys, lanes]).astype(BF)
+
+
+def attend_back(q_ref, k_ref, v_ref, dout_ref, docs_col, docs_row, dq_ref, dk_ref, dv_ref, dk_acc, dv_acc):
+    length = q_ref.shape[0]
+    tile = min(256, length)
+    scale = HEAD_DIM ** (-0.5)
+
+    @pl.loop(0, q_ref.shape[1] // HEAD_DIM)
+    def _(head):
+        lanes = rows_at(head, HEAD_DIM)
+        for start in reversed(range(0, length, tile)):
+            keys, here = pl.ds(0, start + tile), pl.ds(start, tile)
+            q, k, dout = q_ref[here, lanes], k_ref[keys, lanes], dout_ref[here, lanes]
+            probs = softmax_tile(q, k, docs_col, docs_row, start, tile)
+            dprob = dot_right_t(dout, v_ref[keys, lanes])
+            delta = jnp.sum(probs * dprob, axis=1, keepdims=True)
+            dscores = (probs * (dprob - delta)).astype(BF)
+            dq_ref[here, lanes] = (dot_plain(dscores, k) * scale).astype(BF)
+            dk, dv = dot_left_t(dscores, q), dot_left_t(probs.astype(BF), dout)
+            if start + tile == length:
+                dk_acc[...] = dk
+                dv_acc[...] = dv
+            else:
+                dk_acc[keys, :] += dk
+                dv_acc[keys, :] += dv
+        dk_ref[:, lanes] = (dk_acc[...] * scale).astype(BF)
+        dv_ref[:, lanes] = dv_acc[...].astype(BF)
+
+
+def hidden_rows(r, rows_in, rows):
+    def step(at):
+        gate_val = dot_plain(rows_in[rows, :], r.gate_v[:, at])
+        up_val = dot_plain(rows_in[rows, :], r.up_v[:, at])
+        r.gate[rows, at] = gate_val.astype(BF)
+        r.up[rows, at] = up_val.astype(BF)
+        r.hidden[rows, at] = (silu(gate_val) * up_val).astype(BF)
+
+    columns_loop(r.gate.shape[1], 256, step)
+
+
+def hidden_back(r, rows):
+    def step(at):
+        dhid = dot_right_t(r.cot[rows, :], r.down_v[at, :])
+        gate_val, up_val = r.gate[rows, at].astype(F32), r.up[rows, at].astype(F32)
+        sigmoid = jax.nn.sigmoid(gate_val)
+        r.gate[rows, at] = (dhid * up_val * (sigmoid * (1.0 + gate_val * (1.0 - sigmoid)))).astype(BF)
+        r.up[rows, at] = (dhid * (gate_val * sigmoid)).astype(BF)
+
+    columns_loop(r.gate.shape[1], 512, step)
+
+
+def plain_rows(left, right, out):
+    def compute(rows):
+        def step(at):
+            out[rows, at] = dot_plain(left[rows, :], right[:, at]).astype(BF)
+
+        columns_loop(right.shape[1], 1024, step)
+
+    return compute
+
+
+def turned_rows(pairs, out):
+    def compute(rows):
+        def step(at):
+            value = dot_right_t(pairs[0][0][rows, :], pairs[0][1][at, :])
+            for left, right in pairs[1:]:
+                value = value + dot_right_t(left[rows, :], right[at, :])
+            out[rows, at] = value.astype(BF)
+
+        columns_loop(pairs[0][1].shape[0], 512, step)
+
+    return compute
+
+
+def run_kernel(kernel, ident, moves, large, small, outs, scratch):
+    anywhere = pl.BlockSpec(memory_space=pl.ANY)
+    whole = pl.BlockSpec(memory_space=pltpu.VMEM)
+    names = [*large, *small, *outs, *scratch]
+
+    def body(*refs):
+        kernel(Links(*refs[-2:]), SimpleNamespace(**dict(zip(names, refs[:-2], strict=True))))
+
+    results = pl.pallas_call(
+        body,
+        out_shape=[jax.ShapeDtypeStruct(*item) for item in outs.values()],
+        in_specs=[anywhere] * len(large) + [whole] * len(small),
+        out_specs=[anywhere] * len(outs),
+        scratch_shapes=[pltpu.VMEM(*item) for item in scratch.values()] + [pltpu.SemaphoreType.DMA((moves,))] * 2,
+        compiler_params=pltpu.CompilerParams(
+            collective_id=ident, has_side_effects=True, vmem_limit_bytes=VMEM_LIMIT
+        ),
+    )(*large.values(), *small.values())
+    return SimpleNamespace(**dict(zip(outs, results, strict=True)))
+
+
+def typed(kind, **shapes):
+    return {name: (dims, kind) for name, dims in shapes.items()}
+
+
+ALL_MASKS = [(1, 0), (2, 0), (3, 0), (0, 2), (2, 2)] + [(0, mask) for mask in (1, 3, 4, 5, 6, 7)]
+
+
+def forward_kernel(links, r):
+    links.greet(ALL_MASKS)
+    row = links.row
+    tok, width = r.x.shape
+    cols = r.gmu_gate.shape[1]
+    part = r.part
+    outs = []
+
+    def keep(ref, out):
+        outs.append(links.local(ref, out))
+
+    gmu_in, gmu_to = Gather(links, r.gmu_gate, r.gmu_gate_w, False, 1), Gather(links, r.gmu_out, r.gmu_out_w, True, 1)
+    weights_g = [gmu_in, gmu_to]
+    weights_1 = [
+        Gather(links, r.f1_gate, r.f1_gate_w, False, 2),
+        Gather(links, r.f1_up, r.f1_up_w, False, 2),
+        Gather(links, r.f1_down, r.f1_down_w, True, 2),
+    ]
+    weights_q = [Gather(links, r.query, r.query_w, False, 1), Gather(links, r.attn_out, r.attn_out_w, True, 1)]
+    weights_2 = [
+        Gather(links, r.f2_gate, r.f2_gate_w, False, 2),
+        Gather(links, r.f2_up, r.f2_up_w, False, 2),
+        Gather(links, r.f2_down, r.f2_down_w, True, 2),
+    ]
+    gate_2, up_2, down_2 = weights_2
+
+    each(weights_g, Gather.over_z, 2, 1)
+    for weight in weights_g:
+        weight.own()
+
+    spread_a = Spread(links, r.rows_a, False, tok)
+    r.rows_a[spread_a.own(), :] = normed_block(r.x[...].astype(F32), r.gain_a[...])
+    spread_a.start()
+    k_cols = to_columns(links, r.keys, r.k_cols, tok, cols)
+    v_cols = to_columns(links, r.values, r.v_cols, tok, cols)
+    mem_moves = to_columns(links, r.memory, r.mem, tok, cols)
+    spread_a.forward()
+    landed(k_cols)
+    landed(v_cols)
+    k_moves = to_heads(links, r.k_cols, r.k_heads, tok)
+    v_moves = to_heads(links, r.v_cols, r.v_heads, tok)
+    each(weights_g, Gather.over_z, 3)
+    each(weights_1, Gather.over_z, 2, 1, 3)
+    each(weights_g, Gather.over_y, 2, 1, 3)
+    for weight in weights_1 + weights_q + [gate_2]:
+        weight.own()
+    spread_a.wait()
+    landed(mem_moves)
+    keep(r.rows_a, r.rows_a_out)
+    keep(r.mem, r.mem_out)
+    gmu_in.arrived()
+    load_in = links.local(r.gmu_gate_w, r.in_v)
+    gmu_to.arrived()
+    load_out = links.local(r.gmu_out_w, r.out_v)
+    load_in.wait()
+
+    def gmu_step(at):
+        value = dot_plain(r.rows_a[...], r.in_v[:, at])
+        r.pre[:, at] = value.astype(BF)
+        r.act[:, at] = (r.mem[:, at].astype(F32) * silu(value)).astype(BF)
+
+    columns_loop(cols, 256, gmu_step)
+    load_out.wait()
+    collect_a = Collect(links, part, r.core_a, r.far_a, False, tok)
+    collect_a.run(plain_rows(r.act, r.out_v, part))
+    keep(r.pre, r.pre_out)
+    keep(r.act, r.act_out)
+    r.x_one[...] = r.x[...].astype(F32) + collect_a.result()
+    keep(r.x_one, r.x_one_out)
+
+    spread_b = Spread(links, r.rows_b, True, tok)
+    r.rows_b[spread_b.own(), :] = normed_block(r.x_one[...], r.gain_b[...])
+    spread_b.start()
+    each(weights_q, Gather.over_z, 2, 1)
+    each(weights_1, Gather.over_y, 2, 1, 3)
+    spread_b.forward()
+    spread_b.wait()
+    keep(r.rows_b, r.rows_b_out)
+    each(weights_q, Gather.over_z, 3)
+    gate_2.over_z(2, 1, 3)
+    loads = []
+    for weight, place in zip(weights_1, (r.gate_v, r.up_v, r.down_v)):
+        weight.arrived()
+        loads.append(links.local(weight.whole, place))
+    collect_a.finish()
+    wait(loads)
+    hidden_rows(r, r.rows_b, pl.ds(0, 8 * tok))
+    spread_a.finish()
+    outs[0].wait()
+    del outs[0]
+    collect_b = Collect(links, part, r.core_b, r.far_b, True, tok)
+    collect_b.run(plain_rows(r.hidden, r.down_v, part))
+    up_2.over_z(2, 1, 3)
+    each(weights_q, Gather.over_y, 2, 1, 3)
+    gate_2.over_y(2, 1, 3)
+    landed(k_moves)
+    landed(v_moves)
+    keep(r.k_heads, r.k_heads_out)
+    keep(r.v_heads, r.v_heads_out)
+    keep(r.gate, r.gate_out)
+    keep(r.up, r.up_out)
+    keep(r.hidden, r.hidden_out)
+    r.x_two[...] = r.x_one[...] + collect_b.result()
+    keep(r.x_two, r.x_two_out)
+
+    spread_c = Spread(links, r.rows_a, False, tok)
+    r.rows_a[spread_c.own(), :] = normed_block(r.x_two[...], r.gain_c[...])
+    spread_c.start()
+    loads = []
+    for weight, place in zip(weights_q, (r.in_v, r.out_v)):
+        weight.arrived()
+        loads.append(links.local(weight.whole, place))
+    spread_c.forward()
+    wait(loads)
+    spread_c.wait()
+    keep(r.rows_a, r.rows_c_out)
+
+    def query_step(at):
+        r.q_cols[:, at] = dot_plain(r.rows_a[...], r.in_v[:, at]).astype(BF)
+
+    columns_loop(cols, 512, query_step)
+    q_moves = to_heads(links, r.q_cols, r.q_heads, tok)
+    down_2.over_z(2, 1)
+    up_2.own()
+    up_2.over_y(2, 1)
+    landed(q_moves)
+    keep(r.q_heads, r.q_heads_out)
+    attend(r.q_heads, r.k_heads, r.v_heads, r.docs_col, r.docs_row, r.out_heads)
+    spread_b.finish()
+    wait(outs)
+    outs.clear()
+    out_moves = from_heads(links, r.out_heads, r.attended, tok)
+    down_2.over_z(3)
+    up_2.over_y(3)
+    down_2.own()
+    landed(out_moves)
+    keep(r.attended, r.attended_out)
+    collect_b.finish()
+    collect_c = Collect(links, part, r.core_c, r.far_c, False, tok)
+    collect_c.run(plain_rows(r.attended, r.out_v, part))
+    r.x_three[...] = r.x_two[...] + collect_c.result()
+    keep(r.x_three, r.x_three_out)
+    spread_d = Spread(links, r.rows_b, True, tok)
+    r.rows_b[spread_d.own(), :] = normed_block(r.x_three[...], r.gain_d[...])
+    spread_d.start()
+    spread_d.forward()
+    down_2.over_y(2, 1, 3)
+    spread_d.wait()
+    keep(r.rows_b, r.rows_d_out)
+    for weight in weights_2:
+        weight.arrived()
+    wait(outs)
+    links.finish()
+
+
+def forward_pass(large, small):
+    tok, width = small["x"].shape
+    cols = large["gmu_gate"].shape[1]
+    half = large["f1_gate"].shape[1] // 2
+    tokens = 4 * tok
+    positions = small["docs_col"].shape[0]
+    heads = (positions, cols * tokens // positions)
+    inner, outer = (width, half), (half, width)
+    outs = typed(
+        BF,
+        gmu_gate_w=(width, cols),
+        gmu_out_w=(cols, width),
+        f1_gate_w=inner,
+        f1_up_w=inner,
+        f1_down_w=outer,
+        query_w=(width, cols),
+        attn_out_w=(cols, width),
+        f2_gate_w=inner,
+        f2_up_w=inner,
+        f2_down_w=outer,
+        rows_a_out=(tokens, width),
+        mem_out=(tokens, cols),
+        pre_out=(tokens, cols),
+        act_out=(tokens, cols),
+        rows_b_out=(2 * tokens, width),
+        gate_out=(2 * tokens, half),
+        up_out=(2 * tokens, half),
+        hidden_out=(2 * tokens, half),
+        rows_c_out=(tokens, width),
+        q_heads_out=heads,
+        k_heads_out=heads,
+        v_heads_out=heads,
+        attended_out=(tokens, cols),
+        rows_d_out=(2 * tokens, width),
+    ) | typed(F32, x_one_out=(tok, width), x_two_out=(tok, width), x_three_out=(tok, width))
+    scratch = typed(
+        BF,
+        rows_a=(tokens, width),
+        mem=(tokens, cols),
+        k_cols=(tokens, cols),
+        v_cols=(tokens, cols),
+        in_v=(width, cols),
+        out_v=(cols, width),
+        pre=(tokens, cols),
+        act=(tokens, cols),
+        part=(2 * tokens, width),
+        core_a=(2 * tok, width),
+        far_a=(tok, width),
+        core_b=(4 * tok, width),
+        far_b=(3 * tok, width),
+        core_c=(2 * tok, width),
+        far_c=(tok, width),
+        rows_b=(2 * tokens, width),
+        gate_v=inner,
+        up_v=inner,
+        down_v=outer,
+        gate=(2 * tokens, half),
+        up=(2 * tokens, half),
+        hidden=(2 * tokens, half),
+        q_cols=(tokens, cols),
+        q_heads=heads,
+        k_heads=heads,
+        v_heads=heads,
+        out_heads=heads,
+        attended=(tokens, cols),
+    ) | typed(F32, x_one=(tok, width), x_two=(tok, width), x_three=(tok, width))
+    return run_kernel(forward_kernel, 0, 256, large, small, outs, scratch)
+
+
+def weight_blocks(links, order, pairs, stages, blocks):
+    size = stages[0].shape[0]
+    depth = size // len(pairs)
+    moves = [None, None]
+    for count, block in enumerate(order):
+        stage, kind = stages[count % 2], count % 2
+        if moves[kind] is not None:
+            moves[kind].wait()
+        at = rows_at(block, depth)
+        for k, (left, right) in enumerate(pairs):
+            stage[part_of(k, depth), :] = dot_left_t(left[:, at], right[...]).astype(BF)
+        moves[kind] = links.local(stage, blocks.at[rows_at(block, size), :])
+    for move in moves:
+        if move is not None:
+            move.wait()
+
+
+class Scatter:
+    def __init__(self, links, blocks, land_y, land_z, here, there, total, out, parts):
+        self.links, self.blocks, self.land_y, self.land_z = links, blocks, land_y, land_z
+        self.here, self.there, self.total, self.out, self.parts = here, there, total, out, parts
+        self.size = blocks.shape[0] // 8
+        self.y_moves, self.z_moves = {}, {}
+
+    def slot(self, ref, k):
+        return ref.at[part_of(k, self.size), :]
+
+    def block(self, step, y):
+        return self.blocks.at[rows_at(2 * flipped(self.links.z, step) + y, self.size), :]
+
+    def over_y(self, *steps):
+        for step in steps:
+            self.y_moves[step] = self.links.copy(
+                self.block(step, 1 - self.links.y), self.slot(self.land_y, step), 0, 1
+            )
+
+    def over_z(self, *steps):
+        for step in steps:
+            first = self.links.local(self.block(step, self.links.y), self.here)
+            self.y_moves[step].wait_recv()
+            mine = self.slot(self.land_y, step)
+            second = self.links.local(mine, self.there)
+            first.wait()
+            second.wait()
+            total = self.here[...].astype(F32) + self.there[...].astype(F32)
+            mask = 2 * step
+            if self.parts == 1 and step == 2:
+                self.z_moves[3].wait_recv()
+                self.links.local(self.slot(self.land_z, 2), self.there).wait()
+                total = total + self.there[...].astype(F32)
+            elif self.parts == 1 and step == 3:
+                mask = 2
+            self.here[...] = total.astype(BF)
+            self.links.local(self.here, mine).wait()
+            self.z_moves[step] = self.links.copy(mine, self.slot(self.land_z, step - 1), 0, mask)
+
+    def finish(self):
+        rows, width = self.total.shape
+        self.y_moves[0].wait_recv()
+        steps = (2, 1) if self.parts == 1 else (2, 1, 3)
+        for step in steps:
+            self.z_moves[step].wait_recv()
+        sources = [self.block(0, self.links.y), self.slot(self.land_y, 0)]
+        sources += [self.slot(self.land_z, step - 1) for step in steps]
+        parity = self.links.parity
+        for start in range(0, self.size, rows):
+            here = pl.ds(start, rows)
+            spots = [ref.at[part_of(k, rows), :] for ref in (self.here, self.there) for k in range(2)]
+            wait([self.links.local(source.at[here, :], spot) for source, spot in zip(sources, spots)])
+            self.total[...] = spots[0][...].astype(F32) + spots[1][...].astype(F32) + spots[2][...].astype(F32)
+            if self.parts == 1:
+                self.total[...] = self.total[...] + spots[3][...].astype(F32)
+                self.links.local(self.total, self.out.at[here, :]).wait()
+            else:
+                last = self.links.local(sources[4].at[here, :], spots[0])
+                self.links.local(self.total, self.out.at[here, rows_at(parity, width)]).wait()
+                last.wait()
+                self.total[...] = spots[3][...].astype(F32) + spots[0][...].astype(F32)
+                self.links.local(self.total, self.out.at[here, rows_at(1 - parity, width)]).wait()
+        self.links.finish(list(self.y_moves.values()) + list(self.z_moves.values()))
+
+
+def backward_kernel(links, r):
+    links.greet(ALL_MASKS)
+    row, seq, y = links.row, links.seq, links.y
+    tok, width = r.grad.shape
+    cols = r.left.shape[1]
+    half = r.gate.shape[1]
+    part, grad = r.part, r.grad
+    everything = pl.ds(0, 8 * tok)
+    outs = []
+    stages = [r.stage_0, r.stage_1]
+    small_stages = [ref.at[part_of(0, 2 * r.total_q.shape[0]), part_of(0, cols)] for ref in stages]
+    far_y = [2 * z + 1 - y for z in range(4)]
+    own_y = [2 * z + y for z in range(4)]
+
+    spread = Spread(links, r.cot, True, tok)
+    r.cot[spread.own(), :] = r.cotangent[...]
+    spread.start()
+    loads = [
+        links.local(r.rows_d, r.rows),
+        links.local(r.f2_gate_w, r.gate_v),
+        links.local(r.f2_up_w, r.up_v),
+        links.local(r.f2_down_w, r.down_v),
+        links.local(r.x_three, r.values),
+    ]
+    wait(loads)
+    hidden_rows(r, r.rows, everything)
+    spread.by_chip(lambda rows: hidden_back(r, rows))
+    collect_d = Collect(links, part, r.core_b, r.far_b, True, tok)
+    collect_d.run(turned_rows([(r.gate, r.gate_v), (r.up, r.up_v)], part))
+    pairs = [(r.rows, r.gate), (r.rows, r.up), (r.cot, r.hidden)]
+    weight_blocks(links, far_y, pairs, stages, r.blocks_2)
+    stream_2 = Scatter(links, r.blocks_2, r.land_y_2, r.land_z_2, *stages, r.total_2, r.sum_2, 2)
+    stream_2.over_y(2)
+    dx, gain_grad = norm_back(r.values[...], r.gain_d[...], collect_d.result())
+    r.gains[pl.ds(3, 1), :] = gain_grad
+    grad[...] = r.cotangent[...].astype(F32) + dx
+
+    spread_a = Spread(links, r.cot_a, False, tok)
+    r.cot_a[spread_a.own(), :] = grad[...].astype(BF)
+    spread_a.start()
+    weight_blocks(links, own_y, pairs, stages, r.blocks_2)
+    in_v = r.gate_v.at[:, pl.ds(0, cols)]
+    heads = r.q_heads.shape[1]
+    q_v, k_v, v_v = (r.gate.at[:, part_of(k, heads)] for k in range(3))
+    dout_v = r.dout_v
+    dq_v, dk_v, dv_v = (r.up.at[:, part_of(k, heads)] for k in range(3))
+    loads = [
+        links.local(r.attn_out_w, r.out_w),
+        links.local(r.query_w, in_v),
+        links.local(r.attended, r.left),
+        links.local(r.q_heads, q_v),
+        links.local(r.k_heads, k_v),
+        links.local(r.v_heads, v_v),
+    ]
+    spread_a.forward()
+    for k in range(4):
+        plain_rows(r.hidden, r.down_v, r.rows)(part_of(k, 2 * tok))
+    spread.finish()
+    collect_d.finish()
+    wait(loads)
+    spread_a.wait()
+
+    def back_step(at):
+        r.dcols[:, at] = dot_right_t(r.cot_a[...], r.out_w[at, :]).astype(BF)
+
+    columns_loop(cols, 512, back_step)
+    dout_moves = to_heads(links, r.dcols, dout_v, tok)
+    landed(dout_moves)
+    attend_back(
+        q_v, k_v, v_v, dout_v, r.docs_col, r.docs_row, dq_v, dk_v, dv_v, r.dk_acc, r.dv_acc
+    )
+    dq_moves = from_heads(links, dq_v, r.dq_cols, tok)
+    dk_moves = from_heads(links, dk_v, r.k_cols, tok)
+    dv_moves = from_heads(links, dv_v, r.v_cols, tok)
+    stream_2.over_y(3, 1, 0)
+    rows_c = part.at[pl.ds(4 * tok, 4 * tok), :]
+    load = links.local(r.rows_c, rows_c)
+    collect_m = Collect(links, r.rows, r.core_m, r.far_m, True, tok)
+    collect_m.run(lambda rows: None)
+    stream_2.over_z(2)
+    load.wait()
+    landed(dq_moves)
+    collect_c = Collect(links, part, r.core_c, r.far_c, False, tok)
+    collect_c.run(turned_rows([(r.dq_cols, in_v)], part))
+    weight_blocks(links, range(8), [(rows_c, r.dq_cols), (r.cot_a, r.left)], small_stages, r.blocks_q)
+    stream_q = Scatter(links, r.blocks_q, r.land_y_q, r.land_z_q, *small_stages, r.total_q, r.sum_q, 1)
+    stream_q.over_y(3, 1, 2, 0)
+    r.values[...] = r.values[...] + collect_m.result()
+    links.local(r.values, r.mixed).wait()
+    links.local(r.x_two, r.values).wait()
+    dx, gain_grad = norm_back(r.values[...], r.gain_c[...], collect_c.result())
+    r.gains[pl.ds(2, 1), :] = gain_grad
+    grad[...] = grad[...] + dx
+
+    spread_b = Spread(links, r.cot, True, tok)
+    r.cot[spread_b.own(), :] = grad[...].astype(BF)
+    spread_b.start()
+    landed(dk_moves)
+    landed(dv_moves)
+    links.finish(dout_moves[0] + dq_moves[0] + dk_moves[0] + dv_moves[0])
+    collect_m.finish()
+    loads = [
+        links.local(r.f1_down_w, r.down_v),
+        links.local(r.gate_1, r.gate),
+        links.local(r.up_1, r.up),
+        links.local(r.f1_gate_w, r.gate_v),
+        links.local(r.f1_up_w, r.up_v),
+        links.local(r.hidden_1, r.hidden),
+        links.local(r.rows_b, r.rows),
+        links.local(r.x_one, r.values),
+    ]
+    home = [
+        from_columns(links, r.k_cols, r.key_grad, tok, cols),
+        from_columns(links, r.v_cols, r.value_grad, tok, cols),
+    ]
+    stream_2.over_z(3)
+    wait(loads)
+    spread_b.by_chip(lambda rows: hidden_back(r, rows))
+    collect_c.finish()
+    spread_a.finish()
+    collect_b = Collect(links, part, r.core_b, r.far_b, True, tok)
+    collect_b.run(turned_rows([(r.gate, r.gate_v), (r.up, r.up_v)], part))
+    weight_blocks(links, far_y, pairs, stages, r.blocks_1)
+    stream_1 = Scatter(links, r.blocks_1, r.land_y_1, r.land_z_1, *stages, r.total_2, r.sum_1, 2)
+    stream_1.over_y(2, 3)
+    weight_blocks(links, own_y, pairs, stages, r.blocks_1)
+    stream_2.over_z(1)
+    dx, gain_grad = norm_back(r.values[...], r.gain_b[...], collect_b.result())
+    r.gains[pl.ds(1, 1), :] = gain_grad
+    grad[...] = grad[...] + dx
+
+    spread_g = Spread(links, r.cot_a, False, tok)
+    r.cot_a[spread_g.own(), :] = grad[...].astype(BF)
+    spread_g.start()
+    spread_b.finish()
+    collect_b.finish()
+    rows_a = part.at[pl.ds(4 * tok, 4 * tok), :]
+    loads = [
+        links.local(r.gmu_out_w, r.out_w),
+        links.local(r.gmu_gate_w, in_v),
+        links.local(r.pre, r.dcols),
+        links.local(r.mem, r.dq_cols),
+        links.local(r.act, r.left),
+        links.local(r.rows_a, rows_a),
+    ]
+    spread_g.forward()
+    stream_q.over_z(3, 1)
+    wait(loads)
+    spread_g.wait()
+
+    def gmu_back(at):
+        dact = dot_right_t(r.cot_a[...], r.out_w[at, :])
+        pre, mem = r.dcols[:, at].astype(F32), r.dq_cols[:, at].astype(F32)
+        sigmoid = jax.nn.sigmoid(pre)
+        r.dcols[:, at] = (dact * (pre * sigmoid)).astype(BF)
+        r.dq_cols[:, at] = (dact * mem * (sigmoid * (1.0 + pre * (1.0 - sigmoid)))).astype(BF)
+
+    columns_loop(cols, 256, gmu_back)
+    collect_g = Collect(links, part, r.core_c, r.far_c, False, tok)
+    collect_g.run(turned_rows([(r.dq_cols, in_v)], part))
+    home.append(from_columns(links, r.dcols, r.mem_grad, tok, cols))
+    weight_blocks(links, range(8), [(rows_a, r.dq_cols), (r.cot_a, r.left)], small_stages, r.blocks_g)
+    stream_g = Scatter(links, r.blocks_g, r.land_y_g, r.land_z_g, *small_stages, r.total_q, r.sum_g, 1)
+    stream_g.over_y(3, 1, 2, 0)
+    stream_1.over_y(1, 0)
+    stream_q.over_z(2)
+    stream_1.over_z(2)
+    dx, gain_grad = norm_back(r.x[...].astype(F32), r.gain_a[...], collect_g.result())
+    grad[...] = grad[...] + dx
+    outs.append(links.local(grad, r.input_grad))
+
+    r.gains[pl.ds(0, 1), :] = gain_grad
+    r.row_sums[row] = r.gains[...]
+    for move in [links.copy(r.gains, r.row_sums.at[row], mask, 0) for mask in (1, 2, 3)]:
+        move.wait_recv()
+    r.seq_sums[seq] = r.row_sums[0] + r.row_sums[1] + r.row_sums[2] + r.row_sums[3]
+    gain_moves = [links.copy(r.seq_sums.at[seq], r.seq_sums.at[seq], 0, mask) for mask in range(1, 8)]
+    for moves in home:
+        landed(moves)
+
+    stream_1.over_z(3)
+    stream_2.finish()
+    stream_g.over_z(3, 1, 2)
+    stream_1.over_z(1)
+    stream_q.finish()
+    for move in gain_moves:
+        move.wait_recv()
+    total = r.seq_sums[0]
+    for k in range(1, 8):
+        total = total + r.seq_sums[k]
+    r.gain_total[...] = total
+    outs.append(links.local(r.gain_total, r.gain_grads))
+    stream_g.finish()
+    stream_1.finish()
+    wait(outs)
+    links.finish()
+
+
+def backward_pass(large, small):
+    tok, width = small["x"].shape
+    tokens, cols = large["mem"].shape
+    wide, half = large["gate_1"].shape
+    depth = width // 8
+    ffn, unit = (3 * depth, half), (2 * depth, cols)
+
+    def times(count, shape):
+        return (count * shape[0], shape[1])
+
+    outs = typed(
+        F32,
+        mixed=(tok, width),
+        input_grad=(tok, width),
+        gain_grads=(4, width),
+        sum_2=(3 * depth, 2 * half),
+        sum_1=(3 * depth, 2 * half),
+        sum_q=unit,
+        sum_g=unit,
+    ) | typed(
+        BF,
+        key_grad=(tok, width),
+        value_grad=(tok, width),
+        mem_grad=(tok, width),
+        blocks_2=times(8, ffn),
+        blocks_1=times(8, ffn),
+        blocks_q=times(8, unit),
+        blocks_g=times(8, unit),
+        land_y_2=times(4, ffn),
+        land_y_1=times(4, ffn),
+        land_y_q=times(4, unit),
+        land_y_g=times(4, unit),
+        land_z_2=times(3, ffn),
+        land_z_1=times(3, ffn),
+        land_z_q=times(3, unit),
+        land_z_g=times(3, unit),
+    )
+    scratch = typed(
+        BF,
+        rows=(wide, width),
+        cot=(wide, width),
+        cot_a=(tokens, width),
+        gate_v=(width, half),
+        up_v=(width, half),
+        down_v=(half, width),
+        out_w=(cols, width),
+        gate=(wide, half),
+        up=(wide, half),
+        hidden=(wide, half),
+        part=(wide, width),
+        left=(tokens, cols),
+        dcols=(tokens, cols),
+        dq_cols=(tokens, cols),
+        k_cols=(tokens, cols),
+        v_cols=(tokens, cols),
+        dout_v=(small["docs_col"].shape[0], cols // 2),
+        core_b=(4 * tok, width),
+        far_b=(3 * tok, width),
+        core_m=(4 * tok, width),
+        far_m=(3 * tok, width),
+        core_c=(2 * tok, width),
+        far_c=(tok, width),
+        stage_0=ffn,
+        stage_1=ffn,
+    ) | typed(
+        F32,
+        values=(tok, width),
+        grad=(tok, width),
+        dk_acc=(small["docs_col"].shape[0], HEAD_DIM),
+        dv_acc=(small["docs_col"].shape[0], HEAD_DIM),
+        total_2=(depth, half),
+        total_q=(depth, cols),
+        gains=(4, width),
+        gain_total=(4, width),
+        row_sums=(4, 4, width),
+        seq_sums=(8, 4, width),
+    )
+    return run_kernel(backward_kernel, 1, 384, large, small, outs, scratch)
+
+
+def body_general(
     block_input,
     memory,
     key_cache,
@@ -379,23 +1270,6 @@
         jnp.concatenate([key_cache, value_cache], axis=0)[:, None], "row", split_axis=3, concat_axis=1, tiled=True
     )
 
-    by_heads = seq_count % row_count == 0 and head_count % (seq_count // row_count) == 0
-    share = max(1, seq_count // row_count)
-
-    def to_heads(value):
-        count = value.shape[0]
-        value = value.reshape(count, row_count, tok_len, share, -1).transpose(1, 3, 0, 2, 4)
-        value = value.reshape(seq_count, count, tok_len, -1)
-        value = lax.all_to_all(value, "seq", split_axis=0, concat_axis=0, tiled=True)
-        return value.transpose(1, 0, 2, 3).reshape(count, seq_count * tok_len, -1)
-
-    def from_heads(value):
-        count = value.shape[0]
-        value = value.reshape(count, seq_count, tok_len, -1).transpose(1, 0, 2, 3)
-        value = lax.all_to_all(value, "seq", split_axis=0, concat_axis=0, tiled=True)
-        value = value.reshape(row_count, share, count, tok_len, -1).transpose(2, 0, 3, 1, 4)
-        return value.reshape(count, row_count, tok_len, head_count * HEAD_DIM)
-
     x_zero = block_input[0].astype(F32)
     normed_a, inv_a = rms_forward(x_zero, gain_a)
     rows_a = spread(normed_a.astype(BF))
@@ -409,31 +1283,13 @@
     normed_c, inv_c = rms_forward(x_two, gain_c)
     rows_c = spread(normed_c.astype(BF))
     queries = dot_plain(rows_c, query_full).astype(BF)
-    if by_heads:
-        positions = jnp.arange(seq_count * tok_len, dtype=jnp.int32)
-        docs = lax.dynamic_index_in_dim(
-            doc_numbers(doc_lengths, positions), seq_index // share, 0, keepdims=False
-        )
-        kv_heads = to_heads(kv_here)
-        q_heads = to_heads(queries.reshape(1, row_count, tok_len, -1))[0]
-        out_heads, stats = attention_forward(q_heads, kv_heads[0], kv_heads[1], docs)
-        attended = from_heads(out_heads[None])
-
-        def attention_grad(dout):
-            dout_heads = to_heads(dout.reshape(1, row_count, tok_len, -1))[0]
-            dq, dk, dv = attention_backward(
-                q_heads, kv_heads[0], kv_heads[1], dout_heads, stats, docs
-            )
-            return from_heads(dq[None]), from_heads(jnp.stack([dk, dv]))
-
-    else:
-        head_shape = (row_count, tok_len, head_count, HEAD_DIM)
-        attended, ring_grad = ring_attention(
-            queries.reshape(head_shape), kv_here.reshape((2,) + head_shape), doc_lengths, tok_len, head_count
-        )
-
-        def attention_grad(dout):
-            return ring_grad(dout.reshape(head_shape))
+    head_shape = (row_count, tok_len, head_count, HEAD_DIM)
+    attended, ring_grad = ring_attention(
+        queries.reshape(head_shape), kv_here.reshape((2,) + head_shape), doc_lengths, tok_len, head_count
+    )
+
+    def attention_grad(dout):
+        return ring_grad(dout.reshape(head_shape))
 
     attended = attended.reshape(row_count * tok_len, head_count * HEAD_DIM)
     x_three = x_two + collect(dot_plain(attended, aout_full))
@@ -510,6 +1366,117 @@
     )
 
 
+def body_fast(
+    block_input,
+    memory,
+    key_cache,
+    value_cache,
+    doc_lengths,
+    gmu_gate,
+    gmu_out,
+    ffn1_gate,
+    ffn1_up,
+    ffn1_down,
+    query_weight,
+    attn_out,
+    ffn2_gate,
+    ffn2_up,
+    ffn2_down,
+    gain_a,
+    gain_b,
+    gain_c,
+    gain_d,
+    cotangent,
+):
+    seq_count = lax.axis_size("seq")
+    row_count = lax.axis_size("row")
+    seq_index = lax.axis_index("seq")
+    positions = jnp.arange(seq_count * block_input.shape[1], dtype=jnp.int32)
+    docs = lax.dynamic_index_in_dim(
+        doc_numbers(doc_lengths, positions), seq_index // (seq_count // row_count), 0, keepdims=False
+    )
+    shared = dict(x=block_input[0], docs_col=docs[:, None], docs_row=docs[None, :])
+    shared |= dict(gain_a=gain_a[None], gain_b=gain_b[None], gain_c=gain_c[None], gain_d=gain_d[None])
+    kept = forward_pass(
+        dict(
+            memory=memory[0],
+            keys=key_cache[0],
+            values=value_cache[0],
+            gmu_gate=gmu_gate,
+            gmu_out=gmu_out,
+            f1_gate=ffn1_gate,
+            f1_up=ffn1_up,
+            f1_down=ffn1_down,
+            query=query_weight,
+            attn_out=attn_out,
+            f2_gate=ffn2_gate,
+            f2_up=ffn2_up,
+            f2_down=ffn2_down,
+        ),
+        shared,
+    )
+    back = backward_pass(
+        dict(
+            rows_a=kept.rows_a_out,
+            rows_b=kept.rows_b_out,
+            rows_c=kept.rows_c_out,
+            rows_d=kept.rows_d_out,
+            q_heads=kept.q_heads_out,
+            k_heads=kept.k_heads_out,
+            v_heads=kept.v_heads_out,
+            attended=kept.attended_out,
+            mem=kept.mem_out,
+            pre=kept.pre_out,
+            act=kept.act_out,
+            gate_1=kept.gate_out,
+            up_1=kept.up_out,
+            hidden_1=kept.hidden_out,
+            x_one=kept.x_one_out,
+            x_two=kept.x_two_out,
+            x_three=kept.x_three_out,
+            gmu_gate_w=kept.gmu_gate_w,
+            gmu_out_w=kept.gmu_out_w,
+            query_w=kept.query_w,
+            attn_out_w=kept.attn_out_w,
+            f1_gate_w=kept.f1_gate_w,
+            f1_up_w=kept.f1_up_w,
+            f1_down_w=kept.f1_down_w,
+            f2_gate_w=kept.f2_gate_w,
+            f2_up_w=kept.f2_up_w,
+            f2_down_w=kept.f2_down_w,
+        ),
+        shared | dict(cotangent=cotangent[0]),
+    )
+    depth = gmu_gate.shape[0]
+
+    def shards(sums):
+        parts = [sums[k * depth : (k + 1) * depth] for k in range(sums.shape[0] // depth)]
+        return parts[:-1] + [parts[-1].T]
+
+    gate_a_out, gout_out = shards(back.sum_g)
+    query_out, aout_out = shards(back.sum_q)
+    gate_one_out, up_one_out, down_one_out = shards(back.sum_1)
+    gate_two_out, up_two_out, down_two_out = shards(back.sum_2)
+    return (
+        back.mixed[None],
+        back.input_grad[None],
+        back.mem_grad.astype(F32)[None],
+        back.key_grad.astype(F32)[None],
+        back.value_grad.astype(F32)[None],
+        gate_a_out,
+        gout_out,
+        gate_one_out,
+        up_one_out,
+        down_one_out,
+        query_out,
+        aout_out,
+        gate_two_out,
+        up_two_out,
+        down_two_out,
+        *(back.gain_grads[k] for k in range(4)),
+    )
+
+
 def solution(mesh):
     tokens = P("row", "seq", None)
     inner, outer = P("seq", "row"), P("row", "seq")
@@ -524,4 +1491,6 @@
         + (inner, outer, inner, inner, outer, inner, outer, inner, inner, outer)
         + (P(),) * 4
     )
+    seq_count, row_count = mesh.shape["seq"], mesh.shape["row"]
+    body = body_fast if seq_count == 8 and row_count == 4 else body_general
     return jax.shard_map(body, mesh=mesh, in_specs=in_specs, out_specs=out_specs, check_vma=False)

time: 1850 us -> 1030 us (0.56)
  waiting for transfers between devices: 1190 us -> 0 us
  Pallas kernels: 11.6 us -> 988 us
  matrix products: 179 us -> 0 us
  blocking collectives: 136 us -> 0 us
  other arithmetic: 110 us -> 4.65 us
  local copies, waits for them, and re-layouts: 122 us -> 23.7 us
  starting transfers between devices: 71.2 us -> 0 us
    pallas_call x2, Pallas kernels: 11.6 us -> 988 us  [run_kernel(): pl.pallas_call(body, out_shape=[jax.ShapeDtypeStruct(*item) for item in o...]
    ppermute x36 -> x0, waiting for transfers between devices: 665 us -> none  [swapped(): lax.ppermute(value, axis, [(source, source ^ mask) for source in range(co...]
    reduce_scatter x12 -> x0, waiting for transfers between devices: 271 us -> none  [the longest x4 179 us: collect_wide(): summed = lax.psum_scatter(parts, 'row', scatter_dimension=0, tiled=True)[0]]
    dot_general x30 -> x0, matrix products: 179 us -> none  [the longest x10 72.1 us: dot_plain(): return jnp.dot(left, right, preferred_element_type=F32)]
    all_gather x12 -> x0, waiting for transfers between devices: 176 us -> none  [the longest x4 47.8 us: spread(): lax.all_gather(normed[None], 'row', axis=0, tiled=True)]
    all_to_all x5 -> x0, blocking collectives: 98.1 us -> none  [the longest x2 47.4 us: from_heads(): lax.all_to_all(value, 'seq', split_axis=0, concat_axis=0, tiled=True)]
    all_to_all x5 -> x0, waiting for transfers between devices: 77.7 us -> none  [the longest x1 56.6 us: from_heads(): lax.all_to_all(value, 'seq', split_axis=0, concat_axis=0, tiled=True)]
    ppermute x36 -> x0, starting transfers between devices: 40.3 us -> none  [swapped(): lax.ppermute(value, axis, [(source, source ^ mask) for source in range(co...]
  transfers between devices with their start and end apart: 65 -> 0, of which waited for: 36 -> 0; matrix products, arithmetic and copies ran while one was open for 16% -> 0% of each run, Pallas kernels for 0% -> 0%
where the time goes in v2:
time: 1030 us; the launch traced here: 1020 us
  Pallas kernels  988 us (96%)
  local copies, waits for them, and re-layouts  23.7 us (2%)
    pallas_call x2, Pallas kernels, run_kernel(): pl.pallas_call(body, out_shape=[jax.ShapeDtypeStruct(*item) for item in o...  988 us

profile of v2, /device:TPU:1, one launch (start us, length us, event | category | flops | bytes accessed | tf_op | source)
XLA Modules:
  0.0 1017.6 jit_solution(7004085223415093242)
XLA Ops:
  0.7 0.9 reduce_window_sum.11
  1.5 0.1 convert_reduce_fusion
  1.6 0.6 constant_dynamic-slice_fusion.refs_15_.refs_29_
  2.3 1.0 copy.49.refs_14_.refs_28_
  3.3 448.0 %shard_map.339 = (bf16[2048,512]{1,0:T(8,128)(2,1)}, bf16[512,2048]{1,0:T(8,128)(2,1)}, bf16[2048,1024]{1,0:T(8,128)(2,1)}, bf16[2048,1024]{1,0:T(8,128)(2,1)}, ...) custom-call(bf16[128,2048]{1,0:T(8,128)(2,1)} %bitcast.39, ...), custom_call_target="tpu_custom_call" | custom-call | tf_op jit(solution)/shard_map/pallas_call | solution.py:545
  451.3 540.4 %shard_map.340 = (f32[128,2048]{1,0:T(8,128)}, f32[128,2048]{1,0:T(8,128)}, f32[4,2048]{1,0:T(4,128)}, f32[768,2048]{1,0:T(8,128)}, f32[768,2048]{1,0:T(8,128)},...) custom-call(bf16[512,2048]{1,0:T(8,128)(2,1)} %get-tuple-element.56., ...), custom_call_target="tpu_custom_call" | custom-call | tf_op jit(solution)/shard_map/pallas_call | solution.py:545
  991.7 0.0 copy-start.2
  991.7 1.5 fusion
  993.3 2.1 bitcast_convert_fusion.2
  995.4 0.0 copy-done.2
  995.4 2.4 slice_bitcast_fusion.2
  997.8 0.0 copy-start.3
  997.8 0.0 copy-start.4
  997.8 1.0 copy.53
  998.8 1.0 copy.51
  999.8 0.0 copy-done.3
  999.8 0.0 copy-done.4
  999.8 1.6 bitcast_convert_fusion
  1001.3 8.8 slice_bitcast_fusion
  1010.2 2.9 copy.54
  1013.0 0.0 copy-start.1
  1013.0 1.8 copy.52
  1014.8 0.0 copy-done.1
  1014.8 0.0 copy-start
  1014.9 1.0 copy.57
  1015.8 0.6 copy-done
  1016.5 1.0 copy.58
  (1 shorter events, 0.0 us)
Async XLA Ops:
  991.7 3.7 copy-start.2
  997.8 2.0 copy-start.3
  997.8 2.0 copy-start.4
  1013.0 1.8 copy-start.1
  1014.8 1.6 copy-start

commit v3 on v2

--- a/solution.py
+++ b/solution.py
@@ -642,6 +642,7 @@
     keep(r.rows_b, r.rows_b_out)
     each(weights_q, Gather.over_z, 3)
     gate_2.over_z(2, 1, 3)
+    each(weights_q, Gather.over_y, 2, 1, 3)
     loads = []
     for weight, place in zip(weights_1, (r.gate_v, r.up_v, r.down_v)):
         weight.arrived()
@@ -655,7 +656,6 @@
     collect_b = Collect(links, part, r.core_b, r.far_b, True, tok)
     collect_b.run(plain_rows(r.hidden, r.down_v, part))
     up_2.over_z(2, 1, 3)
-    each(weights_q, Gather.over_y, 2, 1, 3)
     gate_2.over_y(2, 1, 3)
     landed(k_moves)
     landed(v_moves)
@@ -804,9 +804,9 @@
 
 
 class Scatter:
-    def __init__(self, links, blocks, land_y, land_z, here, there, total, out, parts):
+    def __init__(self, links, blocks, land_y, land_z, here, there, total, turned, parts, *outs):
         self.links, self.blocks, self.land_y, self.land_z = links, blocks, land_y, land_z
-        self.here, self.there, self.total, self.out, self.parts = here, there, total, out, parts
+        self.here, self.there, self.total, self.turned, self.parts, self.outs = here, there, total, turned, parts, outs
         self.size = blocks.shape[0] // 8
         self.y_moves, self.z_moves = {}, {}
 
@@ -842,30 +842,42 @@
             self.links.local(self.here, mine).wait()
             self.z_moves[step] = self.links.copy(mine, self.slot(self.land_z, step - 1), 0, mask)
 
+    def store(self, k, half):
+        rows, width = self.total.shape
+        if k < len(self.outs) - 1:
+            self.links.local(self.total, self.outs[k].at[:, rows_at(half, width)]).wait()
+        else:
+            self.turned[...] = self.total[...].T
+            self.links.local(self.turned, self.outs[k].at[rows_at(half, width), :]).wait()
+
+    def spots(self):
+        rows = self.total.shape[0]
+        return [ref.at[part_of(n, rows), :] for ref in (self.here, self.there) for n in range(2)]
+
+    def add(self, sources, half):
+        rows, spots = self.total.shape[0], self.spots()
+        for k in range(len(self.outs)):
+            wait([self.links.local(source.at[part_of(k, rows), :], spot) for source, spot in zip(sources, spots)])
+            total = spots[0][...].astype(F32)
+            for spot in spots[1 : len(sources)]:
+                total = total + spot[...].astype(F32)
+            self.total[...] = total
+            self.store(k, half)
+
+    def finish_other(self):
+        for step in (1, 3):
+            self.z_moves[step].wait_recv()
+        self.add([self.slot(self.land_z, 0), self.slot(self.land_z, 2)], 1 - self.links.parity)
+
     def finish(self):
-        rows, width = self.total.shape
         self.y_moves[0].wait_recv()
-        steps = (2, 1) if self.parts == 1 else (2, 1, 3)
-        for step in steps:
-            self.z_moves[step].wait_recv()
-        sources = [self.block(0, self.links.y), self.slot(self.land_y, 0)]
-        sources += [self.slot(self.land_z, step - 1) for step in steps]
-        parity = self.links.parity
-        for start in range(0, self.size, rows):
-            here = pl.ds(start, rows)
-            spots = [ref.at[part_of(k, rows), :] for ref in (self.here, self.there) for k in range(2)]
-            wait([self.links.local(source.at[here, :], spot) for source, spot in zip(sources, spots)])
-            self.total[...] = spots[0][...].astype(F32) + spots[1][...].astype(F32) + spots[2][...].astype(F32)
-            if self.parts == 1:
-                self.total[...] = self.total[...] + spots[3][...].astype(F32)
-                self.links.local(self.total, self.out.at[here, :]).wait()
-            else:
-                last = self.links.local(sources[4].at[here, :], spots[0])
-                self.links.local(self.total, self.out.at[here, rows_at(parity, width)]).wait()
-                last.wait()
-                self.total[...] = spots[3][...].astype(F32) + spots[0][...].astype(F32)
-                self.links.local(self.total, self.out.at[here, rows_at(1 - parity, width)]).wait()
-        self.links.finish(list(self.y_moves.values()) + list(self.z_moves.values()))
+        self.z_moves[2].wait_recv()
+        sources = [self.block(0, self.links.y), self.slot(self.land_y, 0), self.slot(self.land_z, 1)]
+        if self.parts == 1:
+            self.z_moves[1].wait_recv()
+            self.add([*sources, self.slot(self.land_z, 0)], 0)
+        else:
+            self.add(sources, self.links.parity)
 
 
 def backward_kernel(links, r):
@@ -878,7 +890,10 @@
     everything = pl.ds(0, 8 * tok)
     outs = []
     stages = [r.stage_0, r.stage_1]
-    small_stages = [ref.at[part_of(0, 2 * r.total_q.shape[0]), part_of(0, cols)] for ref in stages]
+    depth = r.total.shape[0]
+    small_stages = [ref.at[part_of(0, 2 * depth), part_of(0, cols)] for ref in stages]
+    totals = [r.total, r.turned]
+    small_totals = [r.total.at[:, part_of(0, cols)], r.turned.at[part_of(0, cols), :]]
     far_y = [2 * z + 1 - y for z in range(4)]
     own_y = [2 * z + y for z in range(4)]
 
@@ -895,11 +910,11 @@
     wait(loads)
     hidden_rows(r, r.rows, everything)
     spread.by_chip(lambda rows: hidden_back(r, rows))
+    pairs = [(r.rows, r.gate), (r.rows, r.up), (r.cot, r.hidden)]
     collect_d = Collect(links, part, r.core_b, r.far_b, True, tok)
     collect_d.run(turned_rows([(r.gate, r.gate_v), (r.up, r.up_v)], part))
-    pairs = [(r.rows, r.gate), (r.rows, r.up), (r.cot, r.hidden)]
     weight_blocks(links, far_y, pairs, stages, r.blocks_2)
-    stream_2 = Scatter(links, r.blocks_2, r.land_y_2, r.land_z_2, *stages, r.total_2, r.sum_2, 2)
+    stream_2 = Scatter(links, r.blocks_2, r.land_y_2, r.land_z_2, *stages, *totals, 2, r.f2_gate_g, r.f2_up_g, r.f2_down_g)
     stream_2.over_y(2)
     dx, gain_grad = norm_back(r.values[...], r.gain_d[...], collect_d.result())
     r.gains[pl.ds(3, 1), :] = gain_grad
@@ -953,7 +968,7 @@
     collect_c = Collect(links, part, r.core_c, r.far_c, False, tok)
     collect_c.run(turned_rows([(r.dq_cols, in_v)], part))
     weight_blocks(links, range(8), [(rows_c, r.dq_cols), (r.cot_a, r.left)], small_stages, r.blocks_q)
-    stream_q = Scatter(links, r.blocks_q, r.land_y_q, r.land_z_q, *small_stages, r.total_q, r.sum_q, 1)
+    stream_q = Scatter(links, r.blocks_q, r.land_y_q, r.land_z_q, *small_stages, *small_totals, 1, r.query_g, r.attn_out_g)
     stream_q.over_y(3, 1, 2, 0)
     r.values[...] = r.values[...] + collect_m.result()
     links.local(r.values, r.mixed).wait()
@@ -991,8 +1006,8 @@
     collect_b = Collect(links, part, r.core_b, r.far_b, True, tok)
     collect_b.run(turned_rows([(r.gate, r.gate_v), (r.up, r.up_v)], part))
     weight_blocks(links, far_y, pairs, stages, r.blocks_1)
-    stream_1 = Scatter(links, r.blocks_1, r.land_y_1, r.land_z_1, *stages, r.total_2, r.sum_1, 2)
-    stream_1.over_y(2, 3)
+    stream_1 = Scatter(links, r.blocks_1, r.land_y_1, r.land_z_1, *stages, *totals, 2, r.f1_gate_g, r.f1_up_g, r.f1_down_g)
+    stream_1.over_y(2, 1, 3)
     weight_blocks(links, own_y, pairs, stages, r.blocks_1)
     stream_2.over_z(1)
     dx, gain_grad = norm_back(r.values[...], r.gain_b[...], collect_b.result())
@@ -1028,13 +1043,14 @@
     columns_loop(cols, 256, gmu_back)
     collect_g = Collect(links, part, r.core_c, r.far_c, False, tok)
     collect_g.run(turned_rows([(r.dq_cols, in_v)], part))
+    stream_1.over_z(2)
     home.append(from_columns(links, r.dcols, r.mem_grad, tok, cols))
     weight_blocks(links, range(8), [(rows_a, r.dq_cols), (r.cot_a, r.left)], small_stages, r.blocks_g)
-    stream_g = Scatter(links, r.blocks_g, r.land_y_g, r.land_z_g, *small_stages, r.total_q, r.sum_g, 1)
+    stream_g = Scatter(links, r.blocks_g, r.land_y_g, r.land_z_g, *small_stages, *small_totals, 1, r.gmu_gate_g, r.gmu_out_g)
     stream_g.over_y(3, 1, 2, 0)
-    stream_1.over_y(1, 0)
+    stream_1.over_y(0)
     stream_q.over_z(2)
-    stream_1.over_z(2)
+    stream_1.over_z(1)
     dx, gain_grad = norm_back(r.x[...].astype(F32), r.gain_a[...], collect_g.result())
     grad[...] = grad[...] + dx
     outs.append(links.local(grad, r.input_grad))
@@ -1050,8 +1066,8 @@
 
     stream_1.over_z(3)
     stream_2.finish()
+    stream_2.finish_other()
     stream_g.over_z(3, 1, 2)
-    stream_1.over_z(1)
     stream_q.finish()
     for move in gain_moves:
         move.wait_recv()
@@ -1060,6 +1076,7 @@
         total = total + r.seq_sums[k]
     r.gain_total[...] = total
     outs.append(links.local(r.gain_total, r.gain_grads))
+    stream_1.finish_other()
     stream_g.finish()
     stream_1.finish()
     wait(outs)
@@ -1081,10 +1098,16 @@
         mixed=(tok, width),
         input_grad=(tok, width),
         gain_grads=(4, width),
-        sum_2=(3 * depth, 2 * half),
-        sum_1=(3 * depth, 2 * half),
-        sum_q=unit,
-        sum_g=unit,
+        f2_gate_g=(depth, 2 * half),
+        f2_up_g=(depth, 2 * half),
+        f2_down_g=(2 * half, depth),
+        f1_gate_g=(depth, 2 * half),
+        f1_up_g=(depth, 2 * half),
+        f1_down_g=(2 * half, depth),
+        query_g=(depth, cols),
+        attn_out_g=(cols, depth),
+        gmu_gate_g=(depth, cols),
+        gmu_out_g=(cols, depth),
     ) | typed(
         BF,
         key_grad=(tok, width),
@@ -1136,8 +1159,8 @@
         grad=(tok, width),
         dk_acc=(small["docs_col"].shape[0], HEAD_DIM),
         dv_acc=(small["docs_col"].shape[0], HEAD_DIM),
-        total_2=(depth, half),
-        total_q=(depth, cols),
+        total=(depth, half),
+        turned=(half, depth),
         gains=(4, width),
         gain_total=(4, width),
         row_sums=(4, 4, width),
@@ -1447,32 +1470,22 @@
         ),
         shared | dict(cotangent=cotangent[0]),
     )
-    depth = gmu_gate.shape[0]
-
-    def shards(sums):
-        parts = [sums[k * depth : (k + 1) * depth] for k in range(sums.shape[0] // depth)]
-        return parts[:-1] + [parts[-1].T]
-
-    gate_a_out, gout_out = shards(back.sum_g)
-    query_out, aout_out = shards(back.sum_q)
-    gate_one_out, up_one_out, down_one_out = shards(back.sum_1)
-    gate_two_out, up_two_out, down_two_out = shards(back.sum_2)
     return (
         back.mixed[None],
         back.input_grad[None],
         back.mem_grad.astype(F32)[None],
         back.key_grad.astype(F32)[None],
         back.value_grad.astype(F32)[None],
-        gate_a_out,
-        gout_out,
-        gate_one_out,
-        up_one_out,
-        down_one_out,
-        query_out,
-        aout_out,
-        gate_two_out,
-        up_two_out,
-        down_two_out,
+        back.gmu_gate_g,
+        back.gmu_out_g,
+        back.f1_gate_g,
+        back.f1_up_g,
+        back.f1_down_g,
+        back.query_g,
+        back.attn_out_g,
+        back.f2_gate_g,
+        back.f2_up_g,
+        back.f2_down_g,
         *(back.gain_grads[k] for k in range(4)),
     )
 

time: 1030 us -> 993 us (0.964)
  Pallas kernels: 988 us -> 956 us
    pallas_call x2, Pallas kernels: 988 us -> 956 us  [run_kernel(): pl.pallas_call(body, out_shape=[jax.ShapeDtypeStruct(*item) for item in o...]
    transpose x2 -> x0, local copies, waits for them, and re-layouts: 11.2 us -> none  [shards(): return parts[:-1] + [parts[-1].T]]
where the time goes in v3:
time: 993 us; the launch traced here: 984 us
  Pallas kernels  956 us (96%)
  local copies, waits for them, and re-layouts  20.4 us (2%)
    pallas_call x2, Pallas kernels, run_kernel(): pl.pallas_call(body, out_shape=[jax.ShapeDtypeStruct(*item) for item in o...  956 us

profile of v3, /device:TPU:1, one launch (start us, length us, event | category | flops | bytes accessed | tf_op | source)
XLA Modules:
  0.0 983.7 jit_solution(17758647585939416783)
XLA Ops:
  0.7 0.9 reduce_window_sum.11
  1.5 0.1 convert_reduce_fusion
  1.6 0.6 constant_dynamic-slice_fusion.refs_15_.refs_29_
  2.3 1.0 copy.41.refs_14_.refs_28_
  3.3 442.6 %shard_map.339 = (bf16[2048,512]{1,0:T(8,128)(2,1)}, bf16[512,2048]{1,0:T(8,128)(2,1)}, bf16[2048,1024]{1,0:T(8,128)(2,1)}, bf16[2048,1024]{1,0:T(8,128)(2,1)}, ...) custom-call(bf16[128,2048]{1,0:T(8,128)(2,1)} %bitcast.31, ...), custom_call_target="tpu_custom_call" | custom-call | tf_op jit(solution)/shard_map/pallas_call | solution.py:545
  445.9 513.8 %shard_map.340 = (f32[128,2048]{1,0:T(8,128)}, f32[128,2048]{1,0:T(8,128)}, f32[4,2048]{1,0:T(4,128)}, f32[256,2048]{1,0:T(8,128)}, f32[256,2048]{1,0:T(8,128)},...) custom-call(bf16[512,2048]{1,0:T(8,128)(2,1)} %get-tuple-element.62., ...), custom_call_target="tpu_custom_call" | custom-call | tf_op jit(solution)/shard_map/pallas_call | solution.py:545
  959.7 1.6 fusion
  961.2 0.0 copy-start.7
  961.2 2.2 bitcast_convert_fusion.2
  963.4 0.0 copy-start.6
  963.4 2.8 bitcast_convert_fusion
  966.3 0.0 copy-done.7
  966.3 0.0 copy-start.11
  966.3 1.0 copy.55
  967.3 0.0 copy-done.6
  967.3 0.0 copy-start.10
  967.3 0.0 copy-start.5
  967.3 1.0 copy.56
  968.2 0.0 copy-done.11
  968.2 0.8 copy.57
  969.0 0.0 copy-done.10
  969.0 0.8 copy.58
  969.8 0.0 copy-done.5
  969.8 0.0 copy-start.4
  969.8 1.3 copy.59
  971.2 1.0 copy-done.4
  972.2 0.0 copy-start.3
  972.2 1.3 copy.60
  973.5 1.0 copy-done.3
  974.5 0.0 copy-start.9
  974.5 0.0 copy-start.8
  974.5 0.0 copy-start.2
  974.5 1.3 copy.61
  975.9 0.0 copy-done.9
  975.9 0.8 copy.62
  976.7 0.0 copy-done.8
  976.7 0.8 copy.63
  977.5 0.0 copy-done.2
  977.5 0.0 copy-start.1
  977.5 1.3 copy.64
  978.8 1.0 copy-done.1
  979.9 0.0 copy-start
  979.9 1.3 copy.65
  981.2 1.0 copy-done
  982.2 1.3 copy.66
  (1 shorter events, 0.0 us)
Async XLA Ops:
  961.2 5.1 copy-start.7
  963.4 3.8 copy-start.6
  966.3 2.0 copy-start.11
  967.3 1.8 copy-start.10
  967.3 2.6 copy-start.5
  969.8 2.3 copy-start.4
  972.2 2.3 copy-start.3
  974.5 1.4 copy-start.9
  974.5 2.2 copy-start.8
  974.5 3.0 copy-start.2
  977.5 2.3 copy-start.1
  979.9 2.3 copy-start

commit v4 on v3

--- a/solution.py
+++ b/solution.py
@@ -595,6 +595,8 @@
     spread_a = Spread(links, r.rows_a, False, tok)
     r.rows_a[spread_a.own(), :] = normed_block(r.x[...].astype(F32), r.gain_a[...])
     spread_a.start()
+    spread_y = Spread(links, r.cot_rows, True, tok)
+    own_y = links.local(r.cotangent, r.cot_rows.at[spread_y.own(), :])
     k_cols = to_columns(links, r.keys, r.k_cols, tok, cols)
     v_cols = to_columns(links, r.values, r.v_cols, tok, cols)
     mem_moves = to_columns(links, r.memory, r.mem, tok, cols)
@@ -604,6 +606,8 @@
     k_moves = to_heads(links, r.k_cols, r.k_heads, tok)
     v_moves = to_heads(links, r.v_cols, r.v_heads, tok)
     each(weights_g, Gather.over_z, 3)
+    own_y.wait()
+    spread_y.start()
     each(weights_1, Gather.over_z, 2, 1, 3)
     each(weights_g, Gather.over_y, 2, 1, 3)
     for weight in weights_1 + weights_q + [gate_2]:
@@ -612,6 +616,7 @@
     landed(mem_moves)
     keep(r.rows_a, r.rows_a_out)
     keep(r.mem, r.mem_out)
+    spread_y.forward()
     gmu_in.arrived()
     load_in = links.local(r.gmu_gate_w, r.in_v)
     gmu_to.arrived()
@@ -642,7 +647,7 @@
     keep(r.rows_b, r.rows_b_out)
     each(weights_q, Gather.over_z, 3)
     gate_2.over_z(2, 1, 3)
-    each(weights_q, Gather.over_y, 2, 1, 3)
+    each(weights_q, Gather.over_y, 2, 1)
     loads = []
     for weight, place in zip(weights_1, (r.gate_v, r.up_v, r.down_v)):
         weight.arrived()
@@ -656,6 +661,7 @@
     collect_b = Collect(links, part, r.core_b, r.far_b, True, tok)
     collect_b.run(plain_rows(r.hidden, r.down_v, part))
     up_2.over_z(2, 1, 3)
+    each(weights_q, Gather.over_y, 3)
     gate_2.over_y(2, 1, 3)
     landed(k_moves)
     landed(v_moves)
@@ -684,7 +690,6 @@
 
     columns_loop(cols, 512, query_step)
     q_moves = to_heads(links, r.q_cols, r.q_heads, tok)
-    down_2.over_z(2, 1)
     up_2.own()
     up_2.over_y(2, 1)
     landed(q_moves)
@@ -694,7 +699,7 @@
     wait(outs)
     outs.clear()
     out_moves = from_heads(links, r.out_heads, r.attended, tok)
-    down_2.over_z(3)
+    down_2.over_z(2, 1, 3)
     up_2.over_y(3)
     down_2.own()
     landed(out_moves)
@@ -702,17 +707,19 @@
     collect_b.finish()
     collect_c = Collect(links, part, r.core_c, r.far_c, False, tok)
     collect_c.run(plain_rows(r.attended, r.out_v, part))
+    down_2.over_y(2, 1)
     r.x_three[...] = r.x_two[...] + collect_c.result()
     keep(r.x_three, r.x_three_out)
     spread_d = Spread(links, r.rows_b, True, tok)
     r.rows_b[spread_d.own(), :] = normed_block(r.x_three[...], r.gain_d[...])
     spread_d.start()
     spread_d.forward()
-    down_2.over_y(2, 1, 3)
+    down_2.over_y(3)
     spread_d.wait()
     keep(r.rows_b, r.rows_d_out)
     for weight in weights_2:
         weight.arrived()
+    spread_y.wait()
     wait(outs)
     links.finish()
 
@@ -751,6 +758,7 @@
         v_heads_out=heads,
         attended_out=(tokens, cols),
         rows_d_out=(2 * tokens, width),
+        cot_rows=(2 * tokens, width),
     ) | typed(F32, x_one_out=(tok, width), x_two_out=(tok, width), x_three_out=(tok, width))
     scratch = typed(
         BF,
@@ -897,10 +905,8 @@
     far_y = [2 * z + 1 - y for z in range(4)]
     own_y = [2 * z + y for z in range(4)]
 
-    spread = Spread(links, r.cot, True, tok)
-    r.cot[spread.own(), :] = r.cotangent[...]
-    spread.start()
     loads = [
+        links.local(r.cot_rows, r.cot),
         links.local(r.rows_d, r.rows),
         links.local(r.f2_gate_w, r.gate_v),
         links.local(r.f2_up_w, r.up_v),
@@ -909,7 +915,8 @@
     ]
     wait(loads)
     hidden_rows(r, r.rows, everything)
-    spread.by_chip(lambda rows: hidden_back(r, rows))
+    for k in range(2):
+        hidden_back(r, part_of(k, 4 * tok))
     pairs = [(r.rows, r.gate), (r.rows, r.up), (r.cot, r.hidden)]
     collect_d = Collect(links, part, r.core_b, r.far_b, True, tok)
     collect_d.run(turned_rows([(r.gate, r.gate_v), (r.up, r.up_v)], part))
@@ -940,7 +947,6 @@
     spread_a.forward()
     for k in range(4):
         plain_rows(r.hidden, r.down_v, r.rows)(part_of(k, 2 * tok))
-    spread.finish()
     collect_d.finish()
     wait(loads)
     spread_a.wait()
@@ -1030,6 +1036,7 @@
     ]
     spread_g.forward()
     stream_q.over_z(3, 1)
+    stream_1.over_z(2)
     wait(loads)
     spread_g.wait()
 
@@ -1043,7 +1050,6 @@
     columns_loop(cols, 256, gmu_back)
     collect_g = Collect(links, part, r.core_c, r.far_c, False, tok)
     collect_g.run(turned_rows([(r.dq_cols, in_v)], part))
-    stream_1.over_z(2)
     home.append(from_columns(links, r.dcols, r.mem_grad, tok, cols))
     weight_blocks(links, range(8), [(rows_a, r.dq_cols), (r.cot_a, r.left)], small_stages, r.blocks_g)
     stream_g = Scatter(links, r.blocks_g, r.land_y_g, r.land_z_g, *small_stages, *small_totals, 1, r.gmu_gate_g, r.gmu_out_g)
@@ -1076,9 +1082,9 @@
         total = total + r.seq_sums[k]
     r.gain_total[...] = total
     outs.append(links.local(r.gain_total, r.gain_grads))
+    stream_1.finish()
     stream_1.finish_other()
     stream_g.finish()
-    stream_1.finish()
     wait(outs)
     links.finish()
 
@@ -1422,6 +1428,7 @@
     shared |= dict(gain_a=gain_a[None], gain_b=gain_b[None], gain_c=gain_c[None], gain_d=gain_d[None])
     kept = forward_pass(
         dict(
+            cotangent=cotangent[0],
             memory=memory[0],
             keys=key_cache[0],
             values=value_cache[0],
@@ -1440,6 +1447,7 @@
     )
     back = backward_pass(
         dict(
+            cot_rows=kept.cot_rows,
             rows_a=kept.rows_a_out,
             rows_b=kept.rows_b_out,
             rows_c=kept.rows_c_out,

time: 993 us -> 965 us (0.972)
  Pallas kernels: 956 us -> 929 us
    pallas_call x2, Pallas kernels: 956 us -> 929 us  [run_kernel(): pl.pallas_call(body, out_shape=[jax.ShapeDtypeStruct(*item) for item in o...]
where the time goes in v4:
time: 965 us; the launch traced here: 956 us
  Pallas kernels  929 us (96%)
  local copies, waits for them, and re-layouts  20.4 us (2%)
    pallas_call x2, Pallas kernels, run_kernel(): pl.pallas_call(body, out_shape=[jax.ShapeDtypeStruct(*item) for item in o...  929 us

profile of v4, /device:TPU:1, one launch (start us, length us, event | category | flops | bytes accessed | tf_op | source)
XLA Modules:
  0.0 956.1 jit_solution(3123546775484501658)
XLA Ops:
  0.7 0.9 reduce_window_sum.11
  1.5 0.1 convert_reduce_fusion
  1.6 0.6 constant_dynamic-slice_fusion.refs_16_.refs_30_
  2.3 1.0 copy.41.refs_15_.refs_29_
  3.3 430.1 %shard_map.339 = (bf16[2048,512]{1,0:T(8,128)(2,1)}, bf16[512,2048]{1,0:T(8,128)(2,1)}, bf16[2048,1024]{1,0:T(8,128)(2,1)}, bf16[2048,1024]{1,0:T(8,128)(2,1)}, ...) custom-call(bf16[128,2048]{1,0:T(8,128)(2,1)} %bitcast.26, ...), custom_call_target="tpu_custom_call" | custom-call | tf_op jit(solution)/shard_map/pallas_call | solution.py:545
  433.4 498.6 %shard_map.340 = (f32[128,2048]{1,0:T(8,128)}, f32[128,2048]{1,0:T(8,128)}, f32[4,2048]{1,0:T(4,128)}, f32[256,2048]{1,0:T(8,128)}, f32[256,2048]{1,0:T(8,128)},...) custom-call(bf16[1024,2048]{1,0:T(8,128)(2,1)} %get-tuple-element.63, ...), custom_call_target="tpu_custom_call" | custom-call | tf_op jit(solution)/shard_map/pallas_call | solution.py:545
  932.1 1.6 fusion
  933.7 0.0 copy-start.7
  933.7 2.2 bitcast_convert_fusion.2
  935.9 0.0 copy-start.6
  935.9 2.8 bitcast_convert_fusion
  938.7 0.0 copy-done.7
  938.7 0.0 copy-start.11
  938.7 1.0 copy.55
  939.7 0.0 copy-done.6
  939.7 0.0 copy-start.10
  939.7 0.0 copy-start.5
  939.7 1.0 copy.56
  940.7 0.0 copy-done.11
  940.7 0.8 copy.57
  941.5 0.0 copy-done.10
  941.5 0.8 copy.58
  942.3 0.0 copy-done.5
  942.3 0.0 copy-start.4
  942.3 1.3 copy.59
  943.6 1.0 copy-done.4
  944.6 0.0 copy-start.3
  944.6 1.3 copy.60
  945.9 1.0 copy-done.3
  947.0 0.0 copy-start.9
  947.0 0.0 copy-start.8
  947.0 0.0 copy-start.2
  947.0 1.3 copy.61
  948.3 0.0 copy-done.9
  948.3 0.8 copy.62
  949.1 0.0 copy-done.8
  949.1 0.8 copy.63
  949.9 0.0 copy-done.2
  949.9 0.0 copy-start.1
  949.9 1.3 copy.64
  951.2 1.0 copy-done.1
  952.3 0.0 copy-start
  952.3 1.3 copy.65
  953.6 1.0 copy-done
  954.6 1.3 copy.66
  (1 shorter events, 0.0 us)
Async XLA Ops:
  933.7 5.1 copy-start.7
  935.9 3.8 copy-start.6
  938.7 2.0 copy-start.11
  939.7 1.8 copy-start.10
  939.7 2.6 copy-start.5
  942.3 2.3 copy-start.4
  944.6 2.3 copy-start.3
  947.0 1.4 copy-start.9
  947.0 2.2 copy-start.8
  947.0 3.0 copy-start.2
  949.9 2.3 copy-start.1
  952.3 2.3 copy-start

commit v5 on v4

--- a/solution.py
+++ b/solution.py
@@ -906,15 +906,16 @@
     own_y = [2 * z + y for z in range(4)]
 
     loads = [
-        links.local(r.cot_rows, r.cot),
         links.local(r.rows_d, r.rows),
         links.local(r.f2_gate_w, r.gate_v),
         links.local(r.f2_up_w, r.up_v),
         links.local(r.f2_down_w, r.down_v),
+        links.local(r.cot_rows, r.cot),
         links.local(r.x_three, r.values),
     ]
-    wait(loads)
+    wait(loads[:3])
     hidden_rows(r, r.rows, everything)
+    wait(loads[3:])
     for k in range(2):
         hidden_back(r, part_of(k, 4 * tok))
     pairs = [(r.rows, r.gate), (r.rows, r.up), (r.cot, r.hidden)]
@@ -1001,8 +1002,8 @@
         links.local(r.x_one, r.values),
     ]
     home = [
-        from_columns(links, r.k_cols, r.key_grad, tok, cols),
-        from_columns(links, r.v_cols, r.value_grad, tok, cols),
+        from_columns(links, r.k_cols, r.key_land, tok, cols),
+        from_columns(links, r.v_cols, r.value_land, tok, cols),
     ]
     stream_2.over_z(3)
     wait(loads)
@@ -1050,7 +1051,7 @@
     columns_loop(cols, 256, gmu_back)
     collect_g = Collect(links, part, r.core_c, r.far_c, False, tok)
     collect_g.run(turned_rows([(r.dq_cols, in_v)], part))
-    home.append(from_columns(links, r.dcols, r.mem_grad, tok, cols))
+    home.append(from_columns(links, r.dcols, r.mem_land, tok, cols))
     weight_blocks(links, range(8), [(rows_a, r.dq_cols), (r.cot_a, r.left)], small_stages, r.blocks_g)
     stream_g = Scatter(links, r.blocks_g, r.land_y_g, r.land_z_g, *small_stages, *small_totals, 1, r.gmu_gate_g, r.gmu_out_g)
     stream_g.over_y(3, 1, 2, 0)
@@ -1067,13 +1068,17 @@
         move.wait_recv()
     r.seq_sums[seq] = r.row_sums[0] + r.row_sums[1] + r.row_sums[2] + r.row_sums[3]
     gain_moves = [links.copy(r.seq_sums.at[seq], r.seq_sums.at[seq], 0, mask) for mask in range(1, 8)]
-    for moves in home:
+    wide_grads = ((r.key_land, r.key_grad), (r.value_land, r.value_grad), (r.mem_land, r.mem_grad))
+    for moves, (land, out) in zip(home, wide_grads):
         landed(moves)
+        links.local(land, r.rows.at[pl.ds(0, tok), :]).wait()
+        r.values[...] = r.rows[pl.ds(0, tok), :].astype(F32)
+        links.local(r.values, out).wait()
 
     stream_1.over_z(3)
     stream_2.finish()
     stream_2.finish_other()
-    stream_g.over_z(3, 1, 2)
+    stream_g.over_z(3, 1)
     stream_q.finish()
     for move in gain_moves:
         move.wait_recv()
@@ -1082,8 +1087,9 @@
         total = total + r.seq_sums[k]
     r.gain_total[...] = total
     outs.append(links.local(r.gain_total, r.gain_grads))
+    stream_g.over_z(2)
+    stream_1.finish_other()
     stream_1.finish()
-    stream_1.finish_other()
     stream_g.finish()
     wait(outs)
     links.finish()
@@ -1103,6 +1109,9 @@
         F32,
         mixed=(tok, width),
         input_grad=(tok, width),
+        key_grad=(tok, width),
+        value_grad=(tok, width),
+        mem_grad=(tok, width),
         gain_grads=(4, width),
         f2_gate_g=(depth, 2 * half),
         f2_up_g=(depth, 2 * half),
@@ -1116,9 +1125,9 @@
         gmu_out_g=(cols, depth),
     ) | typed(
         BF,
-        key_grad=(tok, width),
-        value_grad=(tok, width),
-        mem_grad=(tok, width),
+        key_land=(tok, width),
+        value_land=(tok, width),
+        mem_land=(tok, width),
         blocks_2=times(8, ffn),
         blocks_1=times(8, ffn),
         blocks_q=times(8, unit),
@@ -1481,9 +1490,9 @@
     return (
         back.mixed[None],
         back.input_grad[None],
-        back.mem_grad.astype(F32)[None],
-        back.key_grad.astype(F32)[None],
-        back.value_grad.astype(F32)[None],
+        back.mem_grad[None],
+        back.key_grad[None],
+        back.value_grad[None],
         back.gmu_gate_g,
         back.gmu_out_g,
         back.f1_gate_g,

time: 965 us -> 962 us (level)
    unnamed x36 -> x43, local copies, waits for them, and re-layouts: 17.2 us -> 21.5 us
where the time goes in v5:
time: 962 us; the launch traced here: 953 us
  Pallas kernels  926 us (96%)
  local copies, waits for them, and re-layouts  24.7 us (3%)
    pallas_call x2, Pallas kernels, run_kernel(): pl.pallas_call(body, out_shape=[jax.ShapeDtypeStruct(*item) for item in o...  926 us
    unnamed x43, local copies, waits for them, and re-layouts  21.5 us

profile of v5, /device:TPU:1, one launch (start us, length us, event | category | flops | bytes accessed | tf_op | source)
XLA Modules:
  0.0 952.7 jit_solution(403772964633392044)
XLA Ops:
  0.7 0.9 reduce_window_sum.11
  1.5 0.1 convert_reduce_fusion
  1.6 0.6 constant_dynamic-slice_fusion.refs_16_.refs_30_
  2.3 1.0 copy.41.refs_15_.refs_29_
  3.3 430.1 %shard_map.339 = (bf16[2048,512]{1,0:T(8,128)(2,1)}, bf16[512,2048]{1,0:T(8,128)(2,1)}, bf16[2048,1024]{1,0:T(8,128)(2,1)}, bf16[2048,1024]{1,0:T(8,128)(2,1)}, ...) custom-call(bf16[128,2048]{1,0:T(8,128)(2,1)} %bitcast.20, ...), custom_call_target="tpu_custom_call" | custom-call | tf_op jit(solution)/shard_map/pallas_call | solution.py:545
  433.4 495.9 %shard_map.340 = (f32[128,2048]{1,0:T(8,128)}, f32[128,2048]{1,0:T(8,128)}, f32[128,2048]{1,0:T(8,128)}, f32[128,2048]{1,0:T(8,128)}, f32[128,2048]{1,0:T(8,128)...) custom-call(bf16[1024,2048]{1,0:T(8,128)(2,1)} %get-tuple-element.63, ...), custom_call_target="tpu_custom_call" | custom-call | tf_op jit(solution)/shard_map/pallas_call | solution.py:545
  929.4 0.0 copy-start.9
  929.4 1.5 fusion
  930.9 0.0 copy-start.8
  930.9 2.4 copy.58
  933.3 0.0 copy-done.9
  933.3 0.0 copy-start.7
  933.3 1.0 copy.59
  934.3 0.0 copy-done.8
  934.3 0.0 copy-start.6
  934.3 1.0 copy.60
  935.2 0.0 copy-done.7
  935.2 0.0 copy-start.13
  935.2 1.0 copy.61
  936.2 0.0 copy-done.6
  936.2 0.0 copy-start.5
  936.2 1.0 copy.62
  937.2 0.0 copy-done.13
  937.2 0.8 copy.63
  938.0 0.0 copy-done.12
  938.0 0.8 copy.64
  938.8 0.0 copy-done.5
  938.8 1.3 copy.65
  940.1 1.0 copy-done.4
  941.1 0.0 copy-start.3
  941.1 1.3 copy.66
  942.5 1.0 copy-done.3
  943.5 0.0 copy-start.11
  943.5 0.0 copy-start.10
  943.5 0.0 copy-start.2
  943.5 1.3 copy.67
  944.8 0.0 copy-done.11
  944.9 0.8 copy.68
  945.7 0.0 copy-done.10
  945.7 0.8 copy.69
  946.5 0.0 copy-done.2
  946.5 0.0 copy-start.1
  946.5 1.3 copy.70
  947.8 1.0 copy-done.1
  948.8 0.0 copy-start
  948.8 1.3 copy.71
  950.1 1.0 copy-done
  951.2 1.3 copy.72
  (3 shorter events, 0.0 us)
Async XLA Ops:
  929.4 3.9 copy-start.9
  930.9 3.4 copy-start.8
  933.3 1.9 copy-start.7
  934.3 1.9 copy-start.6
  935.2 2.0 copy-start.13
  936.2 1.8 copy-start.12
  936.2 2.6 copy-start.5
  938.8 2.3 copy-start.4
  941.1 2.3 copy-start.3
  943.5 1.4 copy-start.11
  943.5 2.2 copy-start.10
  943.5 3.0 copy-start.2
  946.5 2.3 copy-start.1
  948.8 2.3 copy-start
